TPU v7x, 512 devices: a whole 4x8x8 slice. The times are simulated.
512 devices in a mesh: dp: 256 (over z, x_hi, y, core), rep: 2 (over x_lo).
Axes of the slice: x: 4 (x_hi: 2, x_lo: 2; x = x_hi * 2 + x_lo), y: 8, z: 8, core: 2. Of those that a mesh axis runs over, the one named last changes fastest.
Arguments:
- features: bfloat16 [65536, 1152], P('dp'), may hold values from -0.046875 to 0.046875
- img_weight: bfloat16 [1152, 1152], P(None, 'rep'), may hold values from -4 to 4
- text_embed: bfloat16 [65536, 1152], P('dp', 'rep'), may hold values from -0.4375 to 0.4375
- log_scale: float32 [1], replicated, may hold values from 1.6 to 2.6
- logit_bias: float32 [1], replicated, may hold values from -4 to -1
Outputs:
- image_grad: bfloat16 [65536, 1152], P('dp', 'rep')
- text_grad: bfloat16 [65536, 1152], P('dp', 'rep')
- weight_grad: bfloat16 [1152, 1152], P(None, 'rep')
All inputs are finite; a program needn't handle non-finite values.
Results may differ from a plain program's by a relative error of at most 0.017.
Values may be sent and summed in bfloat16 or wider, within the bound.
No kernel may reach another device: no remote copies, remote signals or barrier semaphores. Data moves between devices by JAX's collectives and lax.ppermute only.
A program may use at most 64 MiB of HBM per device.

v0:
```python
import jax
import jax.numpy as jnp
from jax import lax
from jax.sharding import PartitionSpec as P

STEPS = 4


epsilon = 1e-06


def passed_along(array, axis, by):
    peers = lax.axis_size(axis)
    return lax.ppermute(array, axis, [(i, (i + by) % peers) for i in range(peers)])


def shards(features, img_weight, text_embed, log_scale, logit_bias):
    logit_scale = jnp.exp(log_scale[0])
    offset_value = logit_bias[0]
    row_count = features.shape[0]
    half_width = img_weight.shape[1]
    img_raw = jnp.dot(features, img_weight, preferred_element_type=jnp.float32)
    txt_raw = text_embed.astype(jnp.float32)
    img_sq, txt_sq = lax.psum(
        (
            jnp.sum(img_raw * img_raw, axis=1, keepdims=True),
            jnp.sum(txt_raw * txt_raw, axis=1, keepdims=True),
        ),
        "rep",
    )
    img_inv = lax.rsqrt(img_sq + epsilon)
    txt_inv = lax.rsqrt(txt_sq + epsilon)
    img_hat = img_raw * img_inv
    txt_hat = txt_raw * txt_inv
    img_bf = img_hat.astype(jnp.bfloat16)
    txt_bf = txt_hat.astype(jnp.bfloat16)
    img_use, text_span = (
        lax.all_gather(img_bf, "rep", axis=1, tiled=True),
        lax.all_gather(txt_bf, "rep", axis=1, tiled=True),
    )
    positives = jnp.eye(row_count, dtype=jnp.float32)
    grad_img = jnp.zeros(img_use.shape, jnp.float32)
    carried = jnp.zeros(text_span.shape, jnp.float32)
    for stride in range(STEPS + 1):
        if stride > 0:
            text_span = passed_along(text_span, "dp", 1)
            carried = passed_along(carried.astype(jnp.bfloat16), "dp", 1).astype(carried.dtype)
        scores = lax.dot_general(
            img_use, text_span, (((1,), (1,)), ((), ())), preferred_element_type=jnp.float32
        )
        logits = logit_scale * scores + offset_value
        sig_grad = jax.nn.sigmoid(logits)
        if stride == 0:
            sig_grad = sig_grad - positives
        grad_bf = sig_grad.astype(jnp.bfloat16)
        grad_img = grad_img + logit_scale * jnp.dot(
            grad_bf, text_span, preferred_element_type=jnp.float32
        )
        contrib = logit_scale * lax.dot_general(
            grad_bf, img_use, (((0,), (0,)), ((), ())), preferred_element_type=jnp.float32
        )
        carried = carried + contrib
    grad_txt = passed_along(carried.astype(jnp.bfloat16), "dp", -STEPS).astype(carried.dtype)
    column_start = lax.axis_index("rep") * half_width
    grad_img = lax.dynamic_slice_in_dim(grad_img, column_start, half_width, 1)
    grad_txt = lax.dynamic_slice_in_dim(grad_txt, column_start, half_width, 1)
    img_dot, txt_dot = lax.psum(
        (
            jnp.sum(img_hat * grad_img, axis=1, keepdims=True),
            jnp.sum(txt_hat * grad_txt, axis=1, keepdims=True),
        ),
        "rep",
    )
    image_grad = ((grad_img - img_hat * img_dot) * img_inv).astype(jnp.bfloat16)
    text_grad = ((grad_txt - txt_hat * txt_dot) * txt_inv).astype(jnp.bfloat16)
    weight_part = lax.dot_general(
        features, image_grad, (((0,), (0,)), ((), ())), preferred_element_type=jnp.float32
    )
    weight_grad = lax.psum(weight_part, "dp").astype(jnp.bfloat16)
    return (image_grad, text_grad, weight_grad)


def solution(mesh):
    in_specs = (P("dp", None), P(None, "rep"), P("dp", "rep"), P(), P())
    out_specs = (P("dp", "rep"), P("dp", "rep"), P(None, "rep"))
    return jax.shard_map(shards, mesh=mesh, in_specs=in_specs, out_specs=out_specs, check_vma=False)
```

profile of v0, /device:TPU:1, one launch (start us, length us, event | category | flops | bytes accessed | tf_op | source)
XLA Modules:
  0.0 1450.8 jit_solution(12612385890170473160)
XLA Ops:
  2.0 1.7 multiply_reduce_fusion.1
  3.8 4.4 all-reduce.1
  8.2 6.3 all_gather.7
  14.5 7.2 collective-permute-start
  21.7 14.2 all_gather.6
  38.0 1.9 collective-permute-start.4
  39.9 1.9 collective-permute-start.1
  42.3 4.5 collective-permute-done.4
  47.9 4.4 collective-permute-start.5
  53.6 3.9 collective-permute-start.2
  57.5 1.5 fusion.29
  59.3 2.6 collective-permute-done.5
  63.2 1.9 collective-permute-start.6
  65.4 1.7 collective-permute-done.2
  67.1 2.9 collective-permute-start.3
  70.8 9.3 collective-permute-done.6
  80.2 1.9 collective-permute-start.7
  83.5 1.5 collective-permute-done.3
  85.8 11.3 collective-permute-done.7
  97.3 3.9 collective-permute-start.8
  103.1 9.5 collective-permute-done.8
  113.5 4.1 all-reduce
  118.4 2.1 convolution_bitcast_fusion
  120.5 1329.5 %all-reduce.3 = bf16[1152,576]{0,1:T(8,128)(2,1)} all-reduce(f32[1152,576]{0,1:T(8,128)} %convolution_bitcast_fusion), channel_id=1, replica_groups=mesh['dp'=256,'rep'=2] {'dp'}, use_global_device_ids=true, to_apply=%region_8.0 | all-reduce | flops 663552 | bytes 3981312 | tf_op jit(solution)/shard_map/psum | solution.py:79
  (42 shorter events, 14.6 us)
Async XLA Ops:
  0.6 1.4 copy-start
  2.0 6.1 copy-start.1
  14.5 25.5 %collective-permute-start = (bf16[256,1152]{0,1:T(8,128)(2,1)S(1)}, bf16[256,1152]{0,1:T(8,128)(2,1)S(1)}, u32[]{:S(2)}, u32[]{:S(2)}) collective-permute-start(bf16[256,1152]{0,1:T(8,128)(2,1)S(1)} %all_gather.7), channel_id=1, source_target_pairs={{0,2},{2,4},{4,6},{6,8},{8,10},{10,12},{12,14},{14,16},{16,18},{18... | collective-permute-start | bytes 1769480 | tf_op jit(solution)/shard_map/ppermute | solution.py:14
  38.0 8.7 collective-permute-start.4
  39.9 13.7 collective-permute-start.1
  47.9 14.1 collective-permute-start.5
  53.6 13.5 collective-permute-start.2
  63.2 16.9 %collective-permute-start.6 = (bf16[256,1152]{0,1:T(8,128)(2,1)S(1)}, bf16[256,1152]{0,1:T(8,128)(2,1)S(1)}, u32[]{:S(2)}, u32[]{:S(2)}) collective-permute-start(bf16[256,1152]{0,1:T(8,128)(2,1)S(1)} %add_convert_fusion.2), channel_id=1, source_target_pairs={{0,2},{2,4},{4,6},{6,8},{8,10},{10,12},{12,14},{14,16},{16,18},{18... | collective-permute-start | bytes 1769480 | tf_op jit(solution)/shard_map/ppermute | solution.py:14
  67.1 17.9 %collective-permute-start.3 = (bf16[256,1152]{0,1:T(8,128)(2,1)S(1)}, bf16[256,1152]{0,1:T(8,128)(2,1)S(1)}, u32[]{:S(2)}, u32[]{:S(2)}) collective-permute-start(bf16[256,1152]{0,1:T(8,128)(2,1)S(1)} %collective-permute-done.2), channel_id=1, source_target_pairs={{0,2},{2,4},{4,6},{6,8},{8,10},{10,12},{12,14},{14,16},{16,18},{18... | collective-permute-start | bytes 1769480 | tf_op jit(solution)/shard_map/ppermute | solution.py:14
  80.2 16.9 %collective-permute-start.7 = (bf16[256,1152]{0,1:T(8,128)(2,1)S(1)}, bf16[256,1152]{0,1:T(8,128)(2,1)S(1)}, u32[]{:S(2)}, u32[]{:S(2)}) collective-permute-start(bf16[256,1152]{0,1:T(8,128)(2,1)S(1)} %add_convert_fusion.1), channel_id=1, source_target_pairs={{0,2},{2,4},{4,6},{6,8},{8,10},{10,12},{12,14},{14,16},{16,18},{18... | collective-permute-start | bytes 1769480 | tf_op jit(solution)/shard_map/ppermute | solution.py:14
  97.3 15.3 %collective-permute-start.8 = (bf16[256,1152]{0,1:T(8,128)(2,1)S(1)}, bf16[256,1152]{0,1:T(8,128)(2,1)S(1)}, u32[]{:S(2)}, u32[]{:S(2)}) collective-permute-start(bf16[256,1152]{0,1:T(8,128)(2,1)S(1)} %add_convert_fusion), channel_id=1, source_target_pairs={{0,504},{2,506},{4,508},{6,510},{8,0},{10,2},{12,4},{14,6},{16,8},... | collective-permute-start | bytes 1769480 | tf_op jit(solution)/shard_map/ppermute | solution.py:14
  101.5 1.3 copy-start.2
  103.1 15.3 %copy-start.3 = (bf16[256,1152]{1,0:T(8,128)(2,1)S(1)}, bf16[256,1152]{1,0:T(8,128)(2,1)}, u32[]{:S(2)}) copy-start(bf16[256,1152]{1,0:T(8,128)(2,1)} %param.5) | copy-start | bytes 1769476
  112.5 0.8 copy-start.5
  117.7 0.7 copy-start.4
  120.5 1329.5 %copy-start.6 = (bf16[256,1152]{0,1:T(8,128)(2,1)S(1)}, bf16[256,1152]{0,1:T(8,128)(2,1)}, u32[]{:S(2)}) copy-start(bf16[256,1152]{0,1:T(8,128)(2,1)} %copy-done.5) | copy-start | bytes 1769476
where the time goes:
time: 1460 us; the launch traced here: 1450 us
  blocking collectives  1360 us (93%)
  waiting for transfers between devices  40.4 us (3%)
  starting transfers between devices  29.9 us (2%)
    psum x1, blocking collectives, shards(): weight_grad = lax.psum(weight_part, 'dp').astype(jnp.bfloat16)  1330 us
    ppermute x9, waiting for transfers between devices, passed_along(): lax.ppermute(array, axis, [(i, (i + by) % peers) for i in range(peers)])  40.4 us
    ppermute x9, starting transfers between devices, passed_along(): lax.ppermute(array, axis, [(i, (i + by) % peers) for i in range(peers)])  29.9 us
  transfers between devices with their start and end apart: 9, of which 7 were waited for; matrix products, arithmetic and copies ran while one was open for 1% of the time, Pallas kernels for 0%

commit v1 on v0

--- a/solution.py
+++ b/solution.py
@@ -1,17 +1,52 @@
 import jax
 import jax.numpy as jnp
 from jax import lax
-from jax.sharding import PartitionSpec as P
+from jax.sharding import Mesh, PartitionSpec as P
 
 STEPS = 4
-
+AXES = ("z", "xh", "y", "core", "rep")
+DP = ("z", "xh", "y", "core")
+PLANE = ("z", "y")
 
 epsilon = 1e-06
 
 
-def passed_along(array, axis, by):
-    peers = lax.axis_size(axis)
-    return lax.ppermute(array, axis, [(i, (i + by) % peers) for i in range(peers)])
+def passed_along(array, by):
+    peers = 256
+    return lax.ppermute(array, DP, [(i, (i + by) % peers) for i in range(peers)])
+
+
+def swapped(array, axis):
+    return lax.ppermute(array, axis, [(0, 1), (1, 0)])
+
+
+def weight_sum(features, image_grad):
+    peers = lax.axis_size(PLANE)
+    core = lax.axis_index("core")
+    grad_t = image_grad.T
+    part = grad_t.shape[0] // 2
+    width = features.shape[1]
+    mine = lax.dynamic_slice_in_dim(grad_t, core * part, part, 0)
+    theirs = lax.dynamic_slice_in_dim(grad_t, (1 - core) * part, part, 0)
+    received = swapped(theirs, "core")
+    other_features = swapped(features, "core")
+    total = jnp.dot(mine, features, preferred_element_type=jnp.float32) + jnp.dot(
+        received, other_features, preferred_element_type=jnp.float32
+    )
+    groups = width // 128
+    rows = groups * part
+    tiles = total.astype(jnp.bfloat16).reshape(part, groups, 128).transpose(1, 0, 2).reshape(rows, 128)
+    deep = -(-rows // (peers * 16)) * 16
+    tiles = jnp.pad(tiles, ((0, peers * deep - rows), (0, 0))).reshape(peers, deep, 128)
+    pieces = lax.all_to_all(tiles, PLANE, 0, 0, tiled=True)
+    piece = jnp.sum(pieces.astype(jnp.float32), axis=0)
+    piece = (piece + swapped(piece, "xh")).astype(jnp.bfloat16)
+    sent = jnp.broadcast_to(piece[None], (peers, deep, 128))
+    whole = lax.all_to_all(sent, PLANE, 0, 0, tiled=True).reshape(peers * deep, 128)[:rows]
+    half = whole.reshape(groups, part, 128).transpose(1, 0, 2).reshape(part, width)
+    other = swapped(half, "core")
+    out = jnp.where(core == 0, jnp.concatenate([half, other], 0), jnp.concatenate([other, half], 0))
+    return out.T
 
 
 def shards(features, img_weight, text_embed, log_scale, logit_bias):
@@ -43,8 +78,8 @@
     carried = jnp.zeros(text_span.shape, jnp.float32)
     for stride in range(STEPS + 1):
         if stride > 0:
-            text_span = passed_along(text_span, "dp", 1)
-            carried = passed_along(carried.astype(jnp.bfloat16), "dp", 1).astype(carried.dtype)
+            text_span = passed_along(text_span, 1)
+            carried = passed_along(carried.astype(jnp.bfloat16), 1).astype(carried.dtype)
         scores = lax.dot_general(
             img_use, text_span, (((1,), (1,)), ((), ())), preferred_element_type=jnp.float32
         )
@@ -60,7 +95,7 @@
             grad_bf, img_use, (((0,), (0,)), ((), ())), preferred_element_type=jnp.float32
         )
         carried = carried + contrib
-    grad_txt = passed_along(carried.astype(jnp.bfloat16), "dp", -STEPS).astype(carried.dtype)
+    grad_txt = passed_along(carried.astype(jnp.bfloat16), -STEPS).astype(carried.dtype)
     column_start = lax.axis_index("rep") * half_width
     grad_img = lax.dynamic_slice_in_dim(grad_img, column_start, half_width, 1)
     grad_txt = lax.dynamic_slice_in_dim(grad_txt, column_start, half_width, 1)
@@ -73,14 +108,11 @@
     )
     image_grad = ((grad_img - img_hat * img_dot) * img_inv).astype(jnp.bfloat16)
     text_grad = ((grad_txt - txt_hat * txt_dot) * txt_inv).astype(jnp.bfloat16)
-    weight_part = lax.dot_general(
-        features, image_grad, (((0,), (0,)), ((), ())), preferred_element_type=jnp.float32
-    )
-    weight_grad = lax.psum(weight_part, "dp").astype(jnp.bfloat16)
-    return (image_grad, text_grad, weight_grad)
+    return (image_grad, text_grad, weight_sum(features, image_grad))
 
 
 def solution(mesh):
-    in_specs = (P("dp", None), P(None, "rep"), P("dp", "rep"), P(), P())
-    out_specs = (P("dp", "rep"), P("dp", "rep"), P(None, "rep"))
-    return jax.shard_map(shards, mesh=mesh, in_specs=in_specs, out_specs=out_specs, check_vma=False)
+    fine = Mesh(mesh.devices.reshape(8, 2, 8, 2, 2), AXES)
+    in_specs = (P(DP, None), P(None, "rep"), P(DP, "rep"), P(), P())
+    out_specs = (P(DP, "rep"), P(DP, "rep"), P(None, "rep"))
+    return jax.shard_map(shards, mesh=fine, in_specs=in_specs, out_specs=out_specs, check_vma=False)

time: 1460 us -> 234 us (0.16)
  blocking collectives: 1360 us -> 94.6 us
  starting transfers between devices: 29.9 us -> 63.1 us
    psum x1 -> x0, blocking collectives: 1330 us -> none  [shards(): weight_grad = lax.psum(weight_part, 'dp').astype(jnp.bfloat16)]
    all_to_all x0 -> x2, blocking collectives: none -> 65.6 us  [the longest x1 38.3 us: weight_sum(): pieces = lax.all_to_all(tiles, PLANE, 0, 0, tiled=True)]
    ppermute x9 -> x13, starting transfers between devices: 29.9 us -> 63.1 us  [the longest x4 32.6 us: swapped(): return lax.ppermute(array, axis, [(0, 1), (1, 0)])]
    ppermute x9 -> x13, waiting for transfers between devices: 40.4 us -> 36.9 us  [the longest x9 33.9 us: passed_along(): lax.ppermute(array, DP, [(i, (i + by) % peers) for i in range(peers)])]
  transfers between devices with their start and end apart: 9 -> 13, of which waited for: 7 -> 9; matrix products, arithmetic and copies ran while one was open for 1% -> 6% of each run, Pallas kernels for 0% -> 0%
where the time goes in v1:
time: 234 us; the launch traced here: 233 us
  blocking collectives  94.6 us (40%)
  starting transfers between devices  63.1 us (27%)
  waiting for transfers between devices  36.9 us (16%)
  matrix products  15.8 us (7%)
  local copies, waits for them, and re-layouts  13.5 us (6%)
  other arithmetic  6.5 us (3%)
    all_to_all x1, blocking collectives, weight_sum(): pieces = lax.all_to_all(tiles, PLANE, 0, 0, tiled=True)  38.3 us
    ppermute x9, waiting for transfers between devices, passed_along(): lax.ppermute(array, DP, [(i, (i + by) % peers) for i in range(peers)])  33.9 us
    ppermute x4, starting transfers between devices, swapped(): return lax.ppermute(array, axis, [(0, 1), (1, 0)])  32.6 us
    ppermute x9, starting transfers between devices, passed_along(): lax.ppermute(array, DP, [(i, (i + by) % peers) for i in range(peers)])  30.4 us
    all_to_all x1, blocking collectives, weight_sum(): lax.all_to_all(sent, PLANE, 0, 0, tiled=True).reshape(peers * deep, 128)  27.3 us
    all_gather x1, blocking collectives, shards(): lax.all_gather(img_bf, 'rep', axis=1, tiled=True)  14.3 us
    all_gather x1, blocking collectives, shards(): lax.all_gather(txt_bf, 'rep', axis=1, tiled=True)  6.27 us
    dot_general x5, matrix products, shards(): jnp.dot(grad_bf, text_span, preferred_element_type=jnp.float32)  4.86 us
  transfers between devices with their start and end apart: 13, of which 9 were waited for; matrix products, arithmetic and copies ran while one was open for 6% of the time, Pallas kernels for 0%

profile of v1, /device:TPU:1, one launch (start us, length us, event | category | flops | bytes accessed | tf_op | source)
XLA Modules:
  0.0 232.7 jit_solution(16796097330420884506)
XLA Ops:
  3.8 4.4 %all-reduce.2 = (f32[256,1]{0,1:T(1,128)S(1)}, f32[256,1]{0,1:T(1,128)S(1)}) all-reduce(f32[256,1]{0,1:T(1,128)S(1)} %bitcast.72, f32[256,1]{0,1:T(1,128)S(1)} %bitcast.71), channel_id=1, replica_groups=mesh['z'=8,'xh'=2,'y'=8,'core'=2,'rep'=2] {'rep'}, use_global_device_ids=true, to_apply=%region_1.0 | all-reduce | flops 512 | bytes 4096 | tf_op jit(solution)/shard_map/psum | solution.py:59
  8.2 6.3 %all_gather.7 = bf16[256,1152]{0,1:T(8,128)(2,1)S(1)} all-gather(bf16[256,576]{0,1:T(8,128)(2,1)S(1)} %fusion.35), channel_id=1, replica_groups=mesh['z'=8,'xh'=2,'y'=8,'core'=2,'rep'=2] {'rep'}, dimensions={1}, use_global_device_ids=true | all-gather | bytes 884736 | tf_op jit(solution)/shard_map/all_gather | solution.py:74
  14.5 7.2 %collective-permute-start = (bf16[256,1152]{0,1:T(8,128)(2,1)S(1)}, bf16[256,1152]{0,1:T(8,128)(2,1)}, u32[]{:S(2)}, u32[]{:S(2)}) collective-permute-start(bf16[256,1152]{0,1:T(8,128)(2,1)S(1)} %all_gather.7), channel_id=1, source_target_pairs={{0,2},{2,4},{4,6},{6,8},{8,10},{10,12},{12,14},{14,16},{16,18},{18... | collective-permute-start | bytes 1769480 | tf_op jit(solution)/shard_map/ppermute | solution.py:16
  21.7 14.3 %all_gather.6 = bf16[256,1152]{0,1:T(8,128)(2,1)S(1)} all-gather(bf16[256,576]{0,1:T(8,128)(2,1)S(1)} %multiply_convert_fusion.1), channel_id=1, replica_groups=mesh['z'=8,'xh'=2,'y'=8,'core'=2,'rep'=2] {'rep'}, dimensions={1}, use_global_device_ids=true | all-gather | bytes 884736 | tf_op jit(solution)/shard_map/all_gather | solution.py:73
  40.0 4.0 %collective-permute-start.10 = (bf16[256,1152]{1,0:T(8,128)(2,1)S(1)}, bf16[256,1152]{1,0:T(8,128)(2,1)}, u32[]{:S(2)}, u32[]{:S(2)}) collective-permute-start(bf16[256,1152]{1,0:T(8,128)(2,1)S(1)} %copy-done.3), channel_id=1, source_target_pairs={{0,2},{2,0},{1,3},{3,1},{4,6},{6,4},{5,7},{7,5},{8,10},{10,8},{9,1... | collective-permute-start | bytes 1769480 | tf_op jit(solution)/shard_map/ppermute | solution.py:20
  44.1 1.9 collective-permute-start.1
  48.7 3.7 %collective-permute-start.5 = (bf16[256,1152]{0,1:T(8,128)(2,1)}, bf16[256,1152]{0,1:T(8,128)(2,1)}, u32[]{:S(2)}, u32[]{:S(2)}) collective-permute-start(bf16[256,1152]{0,1:T(8,128)(2,1)} %add_convert_fusion.3), channel_id=1, source_target_pairs={{0,2},{2,4},{4,6},{6,8},{8,10},{10,12},{12,14},{14,16},{16,18},{18... | collective-permute-start | bytes 1769480 | tf_op jit(solution)/shard_map/ppermute | solution.py:16
  53.8 3.9 %collective-permute-start.2 = (bf16[256,1152]{0,1:T(8,128)(2,1)}, bf16[256,1152]{0,1:T(8,128)(2,1)S(1)}, u32[]{:S(2)}, u32[]{:S(2)}) collective-permute-start(bf16[256,1152]{0,1:T(8,128)(2,1)} %collective-permute-done.1), channel_id=1, source_target_pairs={{0,2},{2,4},{4,6},{6,8},{8,10},{10,12},{12,14},{14,16},{16,18},{18... | collective-permute-start | bytes 1769480 | tf_op jit(solution)/shard_map/ppermute | solution.py:16
  59.5 2.6 %collective-permute-done.5 = bf16[256,1152]{0,1:T(8,128)(2,1)} collective-permute-done((bf16[256,1152]{0,1:T(8,128)(2,1)}, bf16[256,1152]{0,1:T(8,128)(2,1)}, u32[]{:S(2)}, u32[]{:S(2)}) %collective-permute-start.5) | collective-permute-done | bytes 589856 | tf_op jit(solution)/shard_map/ppermute | solution.py:16
  63.2 1.9 collective-permute-start.6
  67.2 3.0 %collective-permute-start.3 = (bf16[256,1152]{0,1:T(8,128)(2,1)S(1)}, bf16[256,1152]{0,1:T(8,128)(2,1)S(1)}, u32[]{:S(2)}, u32[]{:S(2)}) collective-permute-start(bf16[256,1152]{0,1:T(8,128)(2,1)S(1)} %collective-permute-done.2), channel_id=1, source_target_pairs={{0,2},{2,4},{4,6},{6,8},{8,10},{10,12},{12,14},{14,16},{16,18},{18... | collective-permute-start | bytes 1769480 | tf_op jit(solution)/shard_map/ppermute | solution.py:16
  70.9 9.2 %collective-permute-done.6 = bf16[256,1152]{0,1:T(8,128)(2,1)S(1)} collective-permute-done((bf16[256,1152]{0,1:T(8,128)(2,1)S(1)}, bf16[256,1152]{0,1:T(8,128)(2,1)S(1)}, u32[]{:S(2)}, u32[]{:S(2)}) %collective-permute-start.6) | collective-permute-done | bytes 589856 | tf_op jit(solution)/shard_map/ppermute | solution.py:16
  85.9 11.3 %collective-permute-done.7 = bf16[256,1152]{0,1:T(8,128)(2,1)S(1)} collective-permute-done((bf16[256,1152]{0,1:T(8,128)(2,1)S(1)}, bf16[256,1152]{0,1:T(8,128)(2,1)S(1)}, u32[]{:S(2)}, u32[]{:S(2)}) %collective-permute-start.7) | collective-permute-done | bytes 589856 | tf_op jit(solution)/shard_map/ppermute | solution.py:16
  97.4 4.9 %collective-permute-start.8 = (bf16[256,1152]{0,1:T(8,128)(2,1)S(1)}, bf16[256,1152]{0,1:T(8,128)(2,1)S(1)}, u32[]{:S(2)}, u32[]{:S(2)}) collective-permute-start(bf16[256,1152]{0,1:T(8,128)(2,1)S(1)} %add_convert_fusion), channel_id=1, source_target_pairs={{0,504},{2,506},{4,508},{6,510},{8,0},{10,2},{12,4},{14,6},{16,8},... | collective-permute-start | bytes 1769480 | tf_op jit(solution)/shard_map/ppermute | solution.py:16
  104.2 8.7 %collective-permute-done.8 = bf16[256,1152]{0,1:T(8,128)(2,1)S(1)} collective-permute-done((bf16[256,1152]{0,1:T(8,128)(2,1)S(1)}, bf16[256,1152]{0,1:T(8,128)(2,1)S(1)}, u32[]{:S(2)}, u32[]{:S(2)}) %collective-permute-start.8) | collective-permute-done | bytes 589856 | tf_op jit(solution)/shard_map/ppermute | solution.py:16
  113.8 4.1 %all-reduce.1 = (f32[256]{0:T(256)S(1)}, f32[256]{0:T(256)S(1)}) all-reduce(f32[256]{0:T(256)S(1)} %get-tuple-element.13, f32[256]{0:T(256)S(1)} %fusion.39), channel_id=1, replica_groups=mesh['z'=8,'xh'=2,'y'=8,'core'=2,'rep'=2] {'rep'}, use_global_device_ids=true, to_apply=%region_5.0 | all-reduce | flops 512 | bytes 4096 | tf_op jit(solution)/shard_map/psum | solution.py:102
  118.0 13.6 %collective-permute-start.9 = (bf16[288,256]{1,0:T(8,128)(2,1)S(1)}, bf16[288,256]{1,0:T(8,128)(2,1)S(1)}, u32[]{:S(2)}, u32[]{:S(2)}) collective-permute-start(bf16[288,256]{1,0:T(8,128)(2,1)S(1)} %dynamic-slice_bitcast_fusion), channel_id=1, source_target_pairs={{0,2},{2,0},{1,3},{3,1},{4,6},{6,4},{5,7},{7,5},{8,10},{10,8},{9,1... | collective-permute-start | bytes 442376 | tf_op jit(solution)/shard_map/ppermute | solution.py:20
  132.6 2.3 fusion
  138.7 38.3 %all_to_all.10 = bf16[64,48,128]{2,1,0:T(8,128)(2,1)S(1)} all-to-all(bf16[64,48,128]{2,1,0:T(8,128)(2,1)S(1)} %bitcast.62), channel_id=1, replica_groups=mesh['z'=8,'xh'=2,'y'=8,'core'=2,'rep'=2] {'z','y'}, dimensions={0} | all-to-all | bytes 1572864 | tf_op jit(solution)/shard_map/all_to_all | solution.py:41
  177.2 7.8 %collective-permute-start.11 = (f32[48,128]{1,0:T(8,128)S(1)}, f32[48,128]{1,0:T(8,128)S(1)}, u32[]{:S(2)}, u32[]{:S(2)}) collective-permute-start(f32[48,128]{1,0:T(8,128)S(1)} %convert_reduce_fusion), channel_id=1, source_target_pairs={{0,32},{32,0},{1,33},{33,1},{2,34},{34,2},{3,35},{35,3},{4,36},{36... | collective-permute-start | bytes 73736 | tf_op jit(solution)/shard_map/ppermute | solution.py:20
  186.3 27.3 %all_to_all.11 = bf16[64,48,128]{2,1,0:T(8,128)(2,1)S(1)} all-to-all(bf16[64,48,128]{2,1,0:T(8,128)(2,1)S(1)} %broadcast_in_dim.22), channel_id=1, replica_groups=mesh['z'=8,'xh'=2,'y'=8,'core'=2,'rep'=2] {'z','y'}, dimensions={0} | all-to-all | bytes 1572864 | tf_op jit(solution)/shard_map/all_to_all | solution.py:45
  217.1 7.2 %collective-permute-start.12 = (bf16[288,1152]{1,0:T(8,128)(2,1)}, bf16[288,1152]{1,0:T(8,128)(2,1)}, u32[]{:S(2)}, u32[]{:S(2)}) collective-permute-start(bf16[288,1152]{1,0:T(8,128)(2,1)} %copy.30), channel_id=1, source_target_pairs={{0,2},{2,0},{1,3},{3,1},{4,6},{6,4},{5,7},{7,5},{8,10},{10,8},{9,1... | collective-permute-start | bytes 1990664 | tf_op jit(solution)/shard_map/ppermute | solution.py:20
  227.9 2.2 fusion.2
  230.1 2.6 %copy.33 = bf16[1152,576]{0,1:T(8,128)(2,1)} copy(bf16[1152,576]{1,0:T(8,128)(2,1)} %fusion.2) | data formatting | bytes 2654208
  (65 shorter events, 37.7 us)
Async XLA Ops:
  0.6 1.4 copy-start
  2.0 6.1 %copy-start.1 = (bf16[256,576]{0,1:T(8,128)(2,1)S(1)}, bf16[256,576]{0,1:T(8,128)(2,1)}, u32[]{:S(2)}) copy-start(bf16[256,576]{0,1:T(8,128)(2,1)} %param.7) | copy-start | bytes 884740
  14.5 29.6 %collective-permute-start = (bf16[256,1152]{0,1:T(8,128)(2,1)S(1)}, bf16[256,1152]{0,1:T(8,128)(2,1)}, u32[]{:S(2)}, u32[]{:S(2)}) collective-permute-start(bf16[256,1152]{0,1:T(8,128)(2,1)S(1)} %all_gather.7), channel_id=1, source_target_pairs={{0,2},{2,4},{4,6},{6,8},{8,10},{10,12},{12,14},{14,16},{16,18},{18... | collective-permute-start | bytes 1769480 | tf_op jit(solution)/shard_map/ppermute | solution.py:16
  37.8 2.3 copy-start.3
  38.1 9.4 %collective-permute-start.4 = (bf16[256,1152]{0,1:T(8,128)(2,1)S(1)}, bf16[256,1152]{0,1:T(8,128)(2,1)S(1)}, u32[]{:S(2)}, u32[]{:S(2)}) collective-permute-start(bf16[256,1152]{0,1:T(8,128)(2,1)S(1)} %fusion.1), channel_id=1, source_target_pairs={{0,2},{2,4},{4,6},{6,8},{8,10},{10,12},{12,14},{14,16},{16,18},{18... | collective-permute-start | bytes 1769480 | tf_op jit(solution)/shard_map/ppermute | solution.py:16
  40.0 92.0 %collective-permute-start.10 = (bf16[256,1152]{1,0:T(8,128)(2,1)S(1)}, bf16[256,1152]{1,0:T(8,128)(2,1)}, u32[]{:S(2)}, u32[]{:S(2)}) collective-permute-start(bf16[256,1152]{1,0:T(8,128)(2,1)S(1)} %copy-done.3), channel_id=1, source_target_pairs={{0,2},{2,0},{1,3},{3,1},{4,6},{6,4},{5,7},{7,5},{8,10},{10,8},{9,1... | collective-permute-start | bytes 1769480 | tf_op jit(solution)/shard_map/ppermute | solution.py:20
  44.1 9.7 %collective-permute-start.1 = (bf16[256,1152]{0,1:T(8,128)(2,1)}, bf16[256,1152]{0,1:T(8,128)(2,1)}, u32[]{:S(2)}, u32[]{:S(2)}) collective-permute-start(bf16[256,1152]{0,1:T(8,128)(2,1)} %collective-permute-done), channel_id=1, source_target_pairs={{0,2},{2,4},{4,6},{6,8},{8,10},{10,12},{12,14},{14,16},{16,18},{18... | collective-permute-start | bytes 1769480 | tf_op jit(solution)/shard_map/ppermute | solution.py:16
  48.7 13.4 %collective-permute-start.5 = (bf16[256,1152]{0,1:T(8,128)(2,1)}, bf16[256,1152]{0,1:T(8,128)(2,1)}, u32[]{:S(2)}, u32[]{:S(2)}) collective-permute-start(bf16[256,1152]{0,1:T(8,128)(2,1)} %add_convert_fusion.3), channel_id=1, source_target_pairs={{0,2},{2,4},{4,6},{6,8},{8,10},{10,12},{12,14},{14,16},{16,18},{18... | collective-permute-start | bytes 1769480 | tf_op jit(solution)/shard_map/ppermute | solution.py:16
  53.8 13.4 %collective-permute-start.2 = (bf16[256,1152]{0,1:T(8,128)(2,1)}, bf16[256,1152]{0,1:T(8,128)(2,1)S(1)}, u32[]{:S(2)}, u32[]{:S(2)}) collective-permute-start(bf16[256,1152]{0,1:T(8,128)(2,1)} %collective-permute-done.1), channel_id=1, source_target_pairs={{0,2},{2,4},{4,6},{6,8},{8,10},{10,12},{12,14},{14,16},{16,18},{18... | collective-permute-start | bytes 1769480 | tf_op jit(solution)/shard_map/ppermute | solution.py:16
  63.2 16.9 %collective-permute-start.6 = (bf16[256,1152]{0,1:T(8,128)(2,1)S(1)}, bf16[256,1152]{0,1:T(8,128)(2,1)S(1)}, u32[]{:S(2)}, u32[]{:S(2)}) collective-permute-start(bf16[256,1152]{0,1:T(8,128)(2,1)S(1)} %add_convert_fusion.2), channel_id=1, source_target_pairs={{0,2},{2,4},{4,6},{6,8},{8,10},{10,12},{12,14},{14,16},{16,18},{18... | collective-permute-start | bytes 1769480 | tf_op jit(solution)/shard_map/ppermute | solution.py:16
  67.2 18.0 %collective-permute-start.3 = (bf16[256,1152]{0,1:T(8,128)(2,1)S(1)}, bf16[256,1152]{0,1:T(8,128)(2,1)S(1)}, u32[]{:S(2)}, u32[]{:S(2)}) collective-permute-start(bf16[256,1152]{0,1:T(8,128)(2,1)S(1)} %collective-permute-done.2), channel_id=1, source_target_pairs={{0,2},{2,4},{4,6},{6,8},{8,10},{10,12},{12,14},{14,16},{16,18},{18... | collective-permute-start | bytes 1769480 | tf_op jit(solution)/shard_map/ppermute | solution.py:16
  80.3 16.9 %collective-permute-start.7 = (bf16[256,1152]{0,1:T(8,128)(2,1)S(1)}, bf16[256,1152]{0,1:T(8,128)(2,1)S(1)}, u32[]{:S(2)}, u32[]{:S(2)}) collective-permute-start(bf16[256,1152]{0,1:T(8,128)(2,1)S(1)} %add_convert_fusion.1), channel_id=1, source_target_pairs={{0,2},{2,4},{4,6},{6,8},{8,10},{10,12},{12,14},{14,16},{16,18},{18... | collective-permute-start | bytes 1769480 | tf_op jit(solution)/shard_map/ppermute | solution.py:16
  97.4 15.5 %collective-permute-start.8 = (bf16[256,1152]{0,1:T(8,128)(2,1)S(1)}, bf16[256,1152]{0,1:T(8,128)(2,1)S(1)}, u32[]{:S(2)}, u32[]{:S(2)}) collective-permute-start(bf16[256,1152]{0,1:T(8,128)(2,1)S(1)} %add_convert_fusion), channel_id=1, source_target_pairs={{0,504},{2,506},{4,508},{6,510},{8,0},{10,2},{12,4},{14,6},{16,8},... | collective-permute-start | bytes 1769480 | tf_op jit(solution)/shard_map/ppermute | solution.py:16
  102.7 1.3 copy-start.2
  112.8 0.8 copy-start.5
  118.0 14.1 %copy-start.4 = (bf16[256,576]{0,1:T(8,128)(2,1)}, bf16[256,576]{0,1:T(8,128)(2,1)S(1)}, u32[]{:S(2)}) copy-start(bf16[256,576]{0,1:T(8,128)(2,1)S(1)} %multiply_convert_fusion) | copy-start | bytes 884740
  118.0 14.6 %collective-permute-start.9 = (bf16[288,256]{1,0:T(8,128)(2,1)S(1)}, bf16[288,256]{1,0:T(8,128)(2,1)S(1)}, u32[]{:S(2)}, u32[]{:S(2)}) collective-permute-start(bf16[288,256]{1,0:T(8,128)(2,1)S(1)} %dynamic-slice_bitcast_fusion), channel_id=1, source_target_pairs={{0,2},{2,0},{1,3},{3,1},{4,6},{6,4},{5,7},{7,5},{8,10},{10,8},{9,1... | collective-permute-start | bytes 442376 | tf_op jit(solution)/shard_map/ppermute | solution.py:20
  177.2 9.0 %collective-permute-start.11 = (f32[48,128]{1,0:T(8,128)S(1)}, f32[48,128]{1,0:T(8,128)S(1)}, u32[]{:S(2)}, u32[]{:S(2)}) collective-permute-start(f32[48,128]{1,0:T(8,128)S(1)} %convert_reduce_fusion), channel_id=1, source_target_pairs={{0,32},{32,0},{1,33},{33,1},{2,34},{34,2},{3,35},{35,3},{4,36},{36... | collective-permute-start | bytes 73736 | tf_op jit(solution)/shard_map/ppermute | solution.py:20
  214.4 9.9 %copy-start.6 = (bf16[256,1152]{0,1:T(8,128)(2,1)S(1)}, bf16[256,1152]{0,1:T(8,128)(2,1)}, u32[]{:S(2)}) copy-start(bf16[256,1152]{0,1:T(8,128)(2,1)} %copy-done.5) | copy-start | bytes 1769476
  217.1 9.3 %collective-permute-start.12 = (bf16[288,1152]{1,0:T(8,128)(2,1)}, bf16[288,1152]{1,0:T(8,128)(2,1)}, u32[]{:S(2)}, u32[]{:S(2)}) collective-permute-start(bf16[288,1152]{1,0:T(8,128)(2,1)} %copy.30), channel_id=1, source_target_pairs={{0,2},{2,0},{1,3},{3,1},{4,6},{6,4},{5,7},{7,5},{8,10},{10,8},{9,1... | collective-permute-start | bytes 1990664 | tf_op jit(solution)/shard_map/ppermute | solution.py:20

commit v2 on v1

v2 whole, which is shorter than its diff:
```python
import functools

import jax
import jax.numpy as jnp
from jax import lax
from jax.experimental import pallas as pl
from jax.experimental.pallas import tpu as pltpu
from jax.sharding import Mesh, PartitionSpec as P

AXES = ("z", "xh", "y", "core", "rep")
DP = ("z", "xh", "y", "core")
PLANE = ("z", "y")
SIZES = (8, 2, 8, 2, 2)
N_DP, RUN = 256, 16

epsilon = 1e-06
f32, bf16 = jnp.float32, jnp.bfloat16


def shifted(array, by):
    pairs = []
    for block in range(N_DP):
        to = (block + by) % N_DP
        cross = block // RUN != to // RUN
        pairs += [(2 * block + rep, 2 * to + (1 - rep if cross else rep)) for rep in range(2)]
    return lax.ppermute(array, AXES, pairs)


def swapped(array, axis):
    return lax.ppermute(array, axis, [(0, 1), (1, 0)])


def dot(a, b, contract):
    return lax.dot_general(a, b, ((contract[:1], contract[1:]), ((), ())), preferred_element_type=f32)


def pairs_kernel(
    flags, log_scale, bias, t0, tm, p0, p1, i0, ie, if_,
    gi_own, gt_own, gt_back, gi_back, d_p1, d_p0, w_own, w_next,
    ip, i0_n, ip_n,
):
    half = ie.shape[0]
    core, ft, fi = flags[0], flags[1], flags[2]
    scale = jnp.exp(jnp.full((1, 1), log_scale[0], f32))
    offset = bias[0]
    second = core == 1

    def part(which):
        return pl.ds(pl.multiple_of(which * half, half), half)

    ip[part(fi)] = ie[...]
    ip[part(1 - fi)] = if_[...]
    i0_n[...] = i0[...].T
    ip_n[...] = ip[...].T

    def inverse(ref):
        values = ref[...].astype(f32)
        return lax.rsqrt(jnp.sum(values * values, axis=0, keepdims=True) + epsilon)

    def column(row):
        return jnp.broadcast_to(row, (128, row.shape[1])).T[:, :1]

    def row(col):
        return jnp.broadcast_to(col, (col.shape[0], 128)).T[:1]

    i0_inv, ip_inv = inverse(i0), inverse(ip)
    t0_inv, tm_inv, p0_inv, p1_inv = inverse(t0), inverse(tm), inverse(p0), inverse(p1)
    i0_col, ip_col = column(i0_inv), column(ip_inv)

    def pair(image, text, flip, image_col, text_inv, diagonal=False):
        raw = dot(image[:, :half], text[part(flip)], (1, 0)) + dot(image[:, half:], text[part(1 - flip)], (1, 0))
        s = raw * image_col * text_inv
        g = 1.0 / (1.0 + jnp.exp(-(scale * s + offset)))
        if diagonal:
            at = lax.broadcasted_iota(jnp.int32, g.shape, 0) == lax.broadcasted_iota(jnp.int32, g.shape, 1)
            g = g - jnp.where(at, 1.0, 0.0)
        gs = g * s
        return (
            (g * text_inv).astype(bf16),
            (g * image_col).astype(bf16),
            jnp.sum(gs, axis=1, keepdims=True),
            jnp.sum(gs, axis=0, keepdims=True),
        )

    a0, b0, r0, c0 = pair(i0_n, t0, 0, i0_col, t0_inv, True)
    a1, b1, r1, c1 = pair(i0_n, tm, ft, i0_col, tm_inv)
    a2, b2, r2, c2 = pair(ip_n, tm, ft, ip_col, tm_inv)
    a3, b3, r3, c3 = pair(i0_n, p1, ft, i0_col, p1_inv)

    def out_text(grad, text, inv, dots):
        return (grad - text.astype(f32) * (inv * dots)) * (scale * inv)

    def out_image(grad, image, inv, dots):
        return (grad - image.astype(f32) * (inv * dots)) * (scale * inv)

    gt_own[...] = out_text(dot(i0[:half], b0, (1, 0)), t0[:half], t0_inv, c0)
    back = dot(i0[part(ft)], b1, (1, 0)) + dot(ip[part(ft)], b2, (1, 0))
    gt_back[...] = out_text(back, tm[:half], tm_inv, c1 + c2)
    own = (
        dot(t0[:half], a0, (1, 1))
        + dot(tm[part(ft)], a1, (1, 1))
        + dot(p1[part(ft)], a3, (1, 1))
    )
    d3 = dot(i0[part(ft)], b3, (1, 0))

    @pl.when(core == 0)
    def _():
        a4, b4, r4, c4 = pair(ip_n, p1, ft, ip_col, p1_inv)
        whole = out_image(own, i0[:half], i0_inv, row(r0 + r1 + r3))
        gi_own[...] = whole
        w_own[...] = whole.astype(bf16)
        dots = row(r2 + r4)
        first = tm[part(ft)], p1[part(ft)]
        other = tm[part(1 - ft)], p1[part(1 - ft)]
        g_first = out_image(dot(first[0], a2, (1, 1)) + dot(first[1], a4, (1, 1)), ip[:half], ip_inv, dots).astype(bf16)
        w_next[...] = g_first
        gi_back[...] = g_first

        @pl.when(fi == 1)
        def _():
            g_other = dot(other[0], a2, (1, 1)) + dot(other[1], a4, (1, 1))
            gi_back[...] = out_image(g_other, ip[half:], ip_inv, dots).astype(bf16)

        both = d3 + dot(ip[part(ft)], b4, (1, 0))
        d_p1[...] = out_text(both, p1[:half], p1_inv, c3 + c4).astype(bf16)
        d_p0[...] = jnp.zeros(d_p0.shape, bf16)

    @pl.when(second)
    def _():
        a4, b4, r4, c4 = pair(i0_n, p0, 0, i0_col, p0_inv)
        whole = out_image(own + dot(p0[:half], a4, (1, 1)), i0[:half], i0_inv, row(r0 + r1 + r3 + r4))
        gi_own[...] = whole
        w_own[...] = whole.astype(bf16)
        dots = row(r2)
        g_first = out_image(dot(tm[part(ft)], a2, (1, 1)), ip[:half], ip_inv, dots).astype(bf16)
        w_next[...] = g_first
        gi_back[...] = g_first

        @pl.when(fi == 1)
        def _():
            gi_back[...] = out_image(dot(tm[part(1 - ft)], a2, (1, 1)), ip[half:], ip_inv, dots).astype(bf16)

        d_p1[...] = out_text(d3, p1[:half], p1_inv, c3).astype(bf16)
        d_p0[...] = out_text(dot(i0[:half], b4, (1, 0)), p0[:half], p0_inv, c4).astype(bf16)


def block_pairs(flags, log_scale, bias, t0, tm, p0, p1, i0, ie, if_):
    half, rows = ie.shape
    smem, vmem = pl.BlockSpec(memory_space=pltpu.SMEM), pl.BlockSpec(memory_space=pltpu.VMEM)
    out = lambda dtype: jax.ShapeDtypeStruct((half, rows), dtype)
    return pl.pallas_call(
        pairs_kernel,
        out_shape=[out(f32)] * 3 + [out(bf16)] * 5,
        in_specs=[smem] * 3 + [vmem] * 7,
        out_specs=[vmem] * 8,
        scratch_shapes=[
            pltpu.VMEM((2 * half, rows), bf16),
            pltpu.VMEM((rows, 2 * half), bf16),
            pltpu.VMEM((rows, 2 * half), bf16),
        ],
        compiler_params=pltpu.CompilerParams(vmem_limit_bytes=48 * 2**20),
        cost_estimate=pl.CostEstimate(flops=1_700_000_000, bytes_accessed=8_000_000, transcendentals=330_000),
        name="block_pairs",
    )(flags, log_scale, bias, t0, tm, p0, p1, i0, ie, if_)


def weight_kernel(which, w_own, w_next, features, next_features, out):
    part = w_own.shape[0] // 2
    at = pl.ds(pl.multiple_of(which[0] * part, part), part)
    a, b = w_own[at], w_next[at]
    for group in range(features.shape[1] // 128):
        columns = slice(group * 128, group * 128 + 128)
        total = dot(a, features[:, columns], (1, 0)) + dot(b, next_features[:, columns], (1, 0))
        out[group * part : (group + 1) * part] = total.astype(out.dtype)


def weight_part(which, w_own, w_next, features, next_features, dtype):
    part, width = w_own.shape[0] // 2, features.shape[1]
    smem, vmem = pl.BlockSpec(memory_space=pltpu.SMEM), pl.BlockSpec(memory_space=pltpu.VMEM)
    return pl.pallas_call(
        weight_kernel,
        out_shape=jax.ShapeDtypeStruct((part * width // 128, 128), dtype),
        in_specs=[smem] + [vmem] * 4,
        out_specs=vmem,
        compiler_params=pltpu.CompilerParams(vmem_limit_bytes=32 * 2**20),
        cost_estimate=pl.CostEstimate(flops=340_000_000, bytes_accessed=3_000_000, transcendentals=0),
        name="weight_part",
    )(which, w_own, w_next, features, next_features)


def weight_sum(w_own, w_next, features, next_features):
    peers = lax.axis_size(PLANE)
    core = lax.axis_index("core")
    part, width = w_own.shape[0] // 2, features.shape[1]
    groups = width // 128
    rows = groups * part
    index = core.astype(jnp.int32).reshape(1)
    theirs = weight_part(1 - index, w_own, w_next, features, next_features, bf16)
    mine = weight_part(index, w_own, w_next, features, next_features, f32)
    tiles = (mine + swapped(theirs, "core").astype(f32)).astype(bf16)
    deep = -(-rows // (peers * 16)) * 16
    tiles = jnp.pad(tiles, ((0, peers * deep - rows), (0, 0))).reshape(peers, deep, 128)
    pieces = lax.all_to_all(tiles, PLANE, 0, 0, tiled=True)
    piece = jnp.sum(pieces.astype(f32), axis=0)
    piece = (piece + swapped(piece, "xh")).astype(bf16)
    sent = jnp.broadcast_to(piece[None], (peers, deep, 128))
    whole = lax.all_to_all(sent, PLANE, 0, 0, tiled=True).reshape(peers * deep, 128)
    other = swapped(whole, "core")
    first, last = jnp.where(core == 0, whole, other), jnp.where(core == 0, other, whole)
    spread = lambda x: x[:rows].reshape(groups, part, 128).transpose(1, 0, 2).reshape(part, width)
    return jnp.concatenate([spread(first), spread(last)], 0)


def shards(features, img_weight, text_embed, log_scale, logit_bias):
    core, y = lax.axis_index("core"), lax.axis_index("y")
    last = lax.axis_size("y") - 1
    flags = jnp.stack([core, y == 0, y == last]).astype(jnp.int32)
    t_own = text_embed.T
    t_far = swapped(t_own, "rep")
    t_a = shifted(t_own, 2)
    next_features = shifted(features, -2)
    i_own = dot(img_weight, features, (0, 1)).astype(bf16)
    i_far = swapped(i_own, "rep")
    i_e = shifted(i_own, -2)
    t_c = shifted(t_far, 2)
    i_f = shifted(i_far, -2)
    t0 = jnp.concatenate([t_own, t_far], 0)
    tm = jnp.concatenate([t_a, t_c], 0)
    p0 = lax.ppermute(t0, "core", [(0, 1)])
    p1 = swapped(tm, "core")
    i0 = jnp.concatenate([i_own, i_far], 0)
    gi_own, gt_own, gt_back, gi_back, d_p1, d_p0, w_own, w_next = block_pairs(
        flags, log_scale, logit_bias, t0, tm, p0, p1, i0, i_e, i_f
    )
    gi_came = shifted(gi_back, 2)
    d_p1_came = swapped(d_p1, "core")
    d_p0_came = lax.ppermute(d_p0, "core", [(1, 0)])
    gt_came = shifted((gt_back + d_p1_came.astype(f32)).astype(bf16), -2)
    image_grad = (gi_own + gi_came.astype(f32)).astype(bf16)
    text_grad = (gt_own + gt_came.astype(f32) + d_p0_came.astype(f32)).astype(bf16)
    weight_grad = weight_sum(w_own, w_next, features, next_features)
    return image_grad.T, text_grad.T, weight_grad.T


def solution(mesh):
    fine = Mesh(mesh.devices.reshape(SIZES), AXES)
    in_specs = (P(DP, None), P(None, "rep"), P(DP, "rep"), P(), P())
    out_specs = (P(DP, "rep"), P(DP, "rep"), P(None, "rep"))
    return jax.shard_map(shards, mesh=fine, in_specs=in_specs, out_specs=out_specs, check_vma=False)
```

time: 234 us -> 179 us (0.76)
  blocking collectives: 94.6 us -> 28.8 us
  matrix products: 15.8 us -> 2.36 us
  waiting for transfers between devices: 36.9 us -> 47.8 us
  Pallas kernels: 0 us -> 6.93 us
  starting transfers between devices: 63.1 us -> 69 us
  other arithmetic: 6.5 us -> 10.8 us
  local copies, waits for them, and re-layouts: 13.5 us -> 9.55 us
    all_to_all x1 -> x0, blocking collectives: 27.3 us -> none  [weight_sum(): lax.all_to_all(sent, PLANE, 0, 0, tiled=True).reshape(peers * deep, 128)]
    all_gather x2 -> x0, blocking collectives: 20.6 us -> none  [the longest x1 14.3 us: shards(): lax.all_gather(img_bf, 'rep', axis=1, tiled=True)]
    dot_general x18 -> x1, matrix products: 15.8 us -> 2.36 us  [dot(): lax.dot_general(a, b, ((contract[:1], contract[1:]), ((), ())), preferred...]
    all_to_all x1, blocking collectives: 38.3 us -> 28.8 us  [weight_sum(): pieces = lax.all_to_all(tiles, PLANE, 0, 0, tiled=True)]
    all_to_all x0 -> x1, waiting for transfers between devices: none -> 9.06 us  [weight_sum(): lax.all_to_all(sent, PLANE, 0, 0, tiled=True).reshape(peers * deep, 128)]
    psum x2 -> x0, blocking collectives: 8.43 us -> none  [the longest x1 4.35 us: shards(): lax.psum((jnp.sum(img_raw * img_raw, axis=1, keepdims=True), jnp.sum(txt_...]
    all_to_all x0 -> x1, starting transfers between devices: none -> 7.37 us  [weight_sum(): lax.all_to_all(sent, PLANE, 0, 0, tiled=True).reshape(peers * deep, 128)]
    pallas_call x0 -> x3, Pallas kernels: none -> 6.93 us  [the longest x1 5.19 us: block_pairs(): pl.pallas_call(pairs_kernel, out_shape=[out(f32)] * 3 + [out(bf16)] * 5,...]
  transfers between devices with their start and end apart: 13 -> 17, of which waited for: 9 -> 8; matrix products, arithmetic and copies ran while one was open for 6% -> 6% of each run, Pallas kernels for 0% -> 3%
where the time goes in v2:
time: 179 us; the launch traced here: 178 us
  starting transfers between devices  69 us (39%)
  waiting for transfers between devices  47.8 us (27%)
  blocking collectives  28.8 us (16%)
  other arithmetic  10.8 us (6%)
  local copies, waits for them, and re-layouts  9.55 us (5%)
  Pallas kernels  6.93 us (4%)
  matrix products  2.36 us (1%)
  between operations  2.31 us (1%)
    ppermute x7, waiting for transfers between devices, shifted(): return lax.ppermute(array, AXES, pairs)  36.1 us
    ppermute x7, starting transfers between devices, swapped(): return lax.ppermute(array, axis, [(0, 1), (1, 0)])  31.7 us
    all_to_all x1, blocking collectives, weight_sum(): pieces = lax.all_to_all(tiles, PLANE, 0, 0, tiled=True)  28.8 us
    ppermute x7, starting transfers between devices, shifted(): return lax.ppermute(array, AXES, pairs)  26 us
    all_to_all x1, waiting for transfers between devices, weight_sum(): lax.all_to_all(sent, PLANE, 0, 0, tiled=True).reshape(peers * deep, 128)  9.06 us
    all_to_all x1, starting transfers between devices, weight_sum(): lax.all_to_all(sent, PLANE, 0, 0, tiled=True).reshape(peers * deep, 128)  7.37 us
    transpose x3, other arithmetic, shards(): return (image_grad.T, text_grad.T, weight_grad.T)  5.41 us
    unnamed x28, local copies, waits for them, and re-layouts  5.28 us
  transfers between devices with their start and end apart: 17, of which 8 were waited for; matrix products, arithmetic and copies ran while one was open for 6% of the time, Pallas kernels for 3%

profile of v2, /device:TPU:1, one launch (start us, length us, event | category | flops | bytes accessed | tf_op | source)
XLA Modules:
  0.0 177.6 jit_solution(13253105315375090236)
XLA Ops:
  0.7 4.1 %collective-permute-start = (bf16[576,256]{1,0:T(8,128)(2,1)}, bf16[576,256]{1,0:T(8,128)(2,1)S(1)}, u32[]{:S(2)}, u32[]{:S(2)}) collective-permute-start(bf16[576,256]{1,0:T(8,128)(2,1)} %bitcast.27), channel_id=1, source_target_pairs={{0,1},{1,0},{2,3},{3,2},{4,5},{5,4},{6,7},{7,6},{8,9},{9,8},{10,11... | collective-permute-start | bytes 884744 | tf_op jit(solution)/shard_map/ppermute | solution.py:30
  4.7 3.2 %collective-permute-start.1 = (bf16[576,256]{1,0:T(8,128)(2,1)}, bf16[576,256]{1,0:T(8,128)(2,1)S(1)}, u32[]{:S(2)}, u32[]{:S(2)}) collective-permute-start(bf16[576,256]{1,0:T(8,128)(2,1)} %bitcast.28), channel_id=1, source_target_pairs={{0,4},{1,5},{2,6},{3,7},{4,8},{5,9},{6,10},{7,11},{8,12},{9,13},{1... | collective-permute-start | bytes 884744 | tf_op jit(solution)/shard_map/ppermute | solution.py:26
  8.0 2.4 %convolution_convert_fusion = bf16[576,256]{1,0:T(8,128)(2,1)} fusion(bf16[1152,576]{0,1:T(8,128)(2,1)S(1)} %copy-done, bf16[256,1152]{1,0:T(8,128)(2,1)} %features.3), kind=kOutput, calls=%fused_computation.3 | convolution fusion | flops 339886080 | bytes 2211840 | tf_op jit(solution)/shard_map/dot_general | solution.py:34
  12.6 3.2 %collective-permute-start.2 = (bf16[576,256]{1,0:T(8,128)(2,1)S(1)}, bf16[576,256]{1,0:T(8,128)(2,1)S(1)}, u32[]{:S(2)}, u32[]{:S(2)}) collective-permute-start(bf16[576,256]{1,0:T(8,128)(2,1)S(1)} %collective-permute-done), channel_id=1, source_target_pairs={{0,4},{1,5},{2,6},{3,7},{4,8},{5,9},{6,10},{7,11},{8,12},{9,13},{1... | collective-permute-start | bytes 884744 | tf_op jit(solution)/shard_map/ppermute | solution.py:26
  17.2 9.2 %collective-permute-done.1 = bf16[576,256]{1,0:T(8,128)(2,1)S(1)} collective-permute-done((bf16[576,256]{1,0:T(8,128)(2,1)}, bf16[576,256]{1,0:T(8,128)(2,1)S(1)}, u32[]{:S(2)}, u32[]{:S(2)}) %collective-permute-start.1) | collective-permute-done | bytes 294944 | tf_op jit(solution)/shard_map/ppermute | solution.py:26
  27.2 5.9 %collective-permute-done.2 = bf16[576,256]{1,0:T(8,128)(2,1)S(1)} collective-permute-done((bf16[576,256]{1,0:T(8,128)(2,1)S(1)}, bf16[576,256]{1,0:T(8,128)(2,1)S(1)}, u32[]{:S(2)}, u32[]{:S(2)}) %collective-permute-start.2) | collective-permute-done | bytes 294944 | tf_op jit(solution)/shard_map/ppermute | solution.py:26
  33.9 4.1 %collective-permute-start.4 = (bf16[1152,256]{1,0:T(8,128)(2,1)}, bf16[1152,256]{1,0:T(8,128)(2,1)}, u32[]{:S(2)}, u32[]{:S(2)}) collective-permute-start(bf16[1152,256]{1,0:T(8,128)(2,1)} %constant_dynamic-update-slice_fusion.tm), channel_id=1, source_target_pairs={{0,2},{2,0},{1,3},{3,1},{4,6},{6,4},{5,7},{7,5},{8,10},{10,8},{9,1... | collective-permute-start | bytes 1769480 | tf_op jit(solution)/shard_map/ppermute | solution.py:30
  38.0 3.4 %collective-permute-start.12 = (bf16[256,1152]{1,0:T(8,128)(2,1)S(1)}, bf16[256,1152]{1,0:T(8,128)(2,1)S(1)}, u32[]{:S(2)}, u32[]{:S(2)}) collective-permute-start(bf16[256,1152]{1,0:T(8,128)(2,1)S(1)} %copy-done.1), channel_id=1, source_target_pairs={{0,509},{1,508},{2,511},{3,510},{4,0},{5,1},{6,2},{7,3},{8,4},{9,5... | collective-permute-start | bytes 1769480 | tf_op jit(solution)/shard_map/ppermute | solution.py:26
  41.3 3.1 %collective-permute-start.6 = (bf16[576,256]{1,0:T(8,128)(2,1)}, bf16[576,256]{1,0:T(8,128)(2,1)S(1)}, u32[]{:S(2)}, u32[]{:S(2)}) collective-permute-start(bf16[576,256]{1,0:T(8,128)(2,1)} %convolution_convert_fusion), channel_id=1, source_target_pairs={{0,509},{1,508},{2,511},{3,510},{4,0},{5,1},{6,2},{7,3},{8,4},{9,5... | collective-permute-start | bytes 884744 | tf_op jit(solution)/shard_map/ppermute | solution.py:26
  44.5 3.0 %collective-permute-start.7 = (bf16[576,256]{1,0:T(8,128)(2,1)}, bf16[576,256]{1,0:T(8,128)(2,1)S(1)}, u32[]{:S(2)}, u32[]{:S(2)}) collective-permute-start(bf16[576,256]{1,0:T(8,128)(2,1)} %collective-permute-done.5), channel_id=1, source_target_pairs={{0,509},{1,508},{2,511},{3,510},{4,0},{5,1},{6,2},{7,3},{8,4},{9,5... | collective-permute-start | bytes 884744 | tf_op jit(solution)/shard_map/ppermute | solution.py:26
  50.8 10.4 %collective-permute-done.6.ie = bf16[576,256]{1,0:T(8,128)(2,1)S(1)} collective-permute-done((bf16[576,256]{1,0:T(8,128)(2,1)}, bf16[576,256]{1,0:T(8,128)(2,1)S(1)}, u32[]{:S(2)}, u32[]{:S(2)}) %collective-permute-start.6) | collective-permute-done | bytes 294944 | tf_op jit(solution)/shard_map/ppermute | solution.py:26
  61.8 5.6 %collective-permute-done.7.if_ = bf16[576,256]{1,0:T(8,128)(2,1)S(1)} collective-permute-done((bf16[576,256]{1,0:T(8,128)(2,1)}, bf16[576,256]{1,0:T(8,128)(2,1)S(1)}, u32[]{:S(2)}, u32[]{:S(2)}) %collective-permute-start.7) | collective-permute-done | bytes 294944 | tf_op jit(solution)/shard_map/ppermute | solution.py:26
  69.5 5.2 %block_pairs.1 = (f32[576,256]{1,0:T(8,128)S(1)}, f32[576,256]{1,0:T(8,128)S(1)}, f32[576,256]{1,0:T(8,128)S(1)}, bf16[576,256]{1,0:T(8,128)(2,1)S(1)}, bf16[576...) custom-call(s32[3]{0:T(128)S(1)} %pad_add_fusion.flags, ...), custom_call_target="tpu_custom_call" | custom-call | flops 1700000000 | bytes 8000000 | tf_op jit(solution)/shard_map/block_pairs/pallas_call | solution.py:151
  75.6 2.7 %collective-permute-start.13 = (bf16[2592,128]{1,0:T(8,128)(2,1)S(1)}, bf16[2592,128]{1,0:T(8,128)(2,1)S(1)}, u32[]{:S(2)}, u32[]{:S(2)}) collective-permute-start(bf16[2592,128]{1,0:T(8,128)(2,1)S(1)} %weight_part.3), channel_id=1, source_target_pairs={{0,2},{2,0},{1,3},{3,1},{4,6},{6,4},{5,7},{7,5},{8,10},{10,8},{9,1... | collective-permute-start | bytes 1990664 | tf_op jit(solution)/shard_map/ppermute | solution.py:30
  80.3 28.8 %all_to_all.10 = bf16[64,48,128]{2,1,0:T(8,128)(2,1)S(1)} all-to-all(bf16[64,48,128]{2,1,0:T(8,128)(2,1)S(1)} %bitcast.24), channel_id=1, replica_groups=mesh['z'=8,'xh'=2,'y'=8,'core'=2,'rep'=2] {'z','y'}, dimensions={0} | all-to-all | bytes 1572864 | tf_op jit(solution)/shard_map/all_to_all | solution.py:203
  109.2 4.4 %collective-permute-start.14 = (f32[48,128]{1,0:T(8,128)S(1)}, f32[48,128]{1,0:T(8,128)S(1)}, u32[]{:S(2)}, u32[]{:S(2)}) collective-permute-start(f32[48,128]{1,0:T(8,128)S(1)} %convert_reduce_fusion), channel_id=1, source_target_pairs={{0,32},{32,0},{1,33},{33,1},{2,34},{34,2},{3,35},{35,3},{4,36},{36... | collective-permute-start | bytes 73736 | tf_op jit(solution)/shard_map/ppermute | solution.py:30
  116.4 7.4 %all-to-all-start.1 = ((bf16[64,48,128]{2,1,0:T(8,128)(2,1)}), bf16[64,48,128]{2,1,0:T(8,128)(2,1)}, u32[]{:S(2)}, u32[]{:S(2)}) async-start(bf16[64,48,128]{2,1,0:T(8,128)(2,1)} %broadcast_in_dim.2), calls=%async_computation.1 | async-start | bytes 1572864 | tf_op jit(solution)/shard_map/all_to_all | solution.py:207
  123.8 5.0 %collective-permute-start.9 = (bf16[576,256]{1,0:T(8,128)(2,1)}, bf16[576,256]{1,0:T(8,128)(2,1)}, u32[]{:S(2)}, u32[]{:S(2)}) collective-permute-start(bf16[576,256]{1,0:T(8,128)(2,1)} %copy-done.9), channel_id=1, source_target_pairs={{0,2},{2,0},{1,3},{3,1},{4,6},{6,4},{5,7},{7,5},{8,10},{10,8},{9,1... | collective-permute-start | bytes 884744 | tf_op jit(solution)/shard_map/ppermute | solution.py:30
  128.8 2.6 %collective-permute-start.11 = (bf16[576,256]{1,0:T(8,128)(2,1)S(1)}, bf16[576,256]{1,0:T(8,128)(2,1)}, u32[]{:S(2)}, u32[]{:S(2)}) collective-permute-start(bf16[576,256]{1,0:T(8,128)(2,1)S(1)} %get-tuple-element.16), channel_id=1, source_target_pairs={{2,0},{3,1},{6,4},{7,5},{10,8},{11,9},{14,12},{15,13},{18,16},{19,... | collective-permute-start | bytes 884744 | tf_op jit(solution)/shard_map/ppermute | solution.py:237
  131.5 3.1 %collective-permute-start.8 = (bf16[576,256]{1,0:T(8,128)(2,1)}, bf16[576,256]{1,0:T(8,128)(2,1)}, u32[]{:S(2)}, u32[]{:S(2)}) collective-permute-start(bf16[576,256]{1,0:T(8,128)(2,1)} %copy-done.8), channel_id=1, source_target_pairs={{0,4},{1,5},{2,6},{3,7},{4,8},{5,9},{6,10},{7,11},{8,12},{9,13},{1... | collective-permute-start | bytes 884744 | tf_op jit(solution)/shard_map/ppermute | solution.py:26
  134.6 9.1 %all-to-all-done.1 = bf16[64,48,128]{2,1,0:T(8,128)(2,1)} async-done(((bf16[64,48,128]{2,1,0:T(8,128)(2,1)}), bf16[64,48,128]{2,1,0:T(8,128)(2,1)}, u32[]{:S(2)}, u32[]{:S(2)}) %all-to-all-start.1) | async-done | bytes 786464 | tf_op jit(solution)/shard_map/all_to_all | solution.py:207
  143.6 9.1 %collective-permute-start.15 = (bf16[3072,128]{1,0:T(8,128)(2,1)}, bf16[3072,128]{1,0:T(8,128)(2,1)}, u32[]{:S(2)}, u32[]{:S(2)}) collective-permute-start(bf16[3072,128]{1,0:T(8,128)(2,1)} %bitcast.7), channel_id=1, source_target_pairs={{0,2},{2,0},{1,3},{3,1},{4,6},{6,4},{5,7},{7,5},{8,10},{10,8},{9,1... | collective-permute-start | bytes 2359304 | tf_op jit(solution)/shard_map/ppermute | solution.py:30
  154.6 7.0 %collective-permute-start.10 = (bf16[576,256]{1,0:T(8,128)(2,1)}, bf16[576,256]{1,0:T(8,128)(2,1)S(1)}, u32[]{:S(2)}, u32[]{:S(2)}) collective-permute-start(bf16[576,256]{1,0:T(8,128)(2,1)} %add_convert_fusion.2), channel_id=1, source_target_pairs={{0,509},{1,508},{2,511},{3,510},{4,0},{5,1},{6,2},{7,3},{8,4},{9,5... | collective-permute-start | bytes 884744 | tf_op jit(solution)/shard_map/ppermute | solution.py:26
  163.3 5.0 %collective-permute-done.10 = bf16[576,256]{1,0:T(8,128)(2,1)S(1)} collective-permute-done((bf16[576,256]{1,0:T(8,128)(2,1)}, bf16[576,256]{1,0:T(8,128)(2,1)S(1)}, u32[]{:S(2)}, u32[]{:S(2)}) %collective-permute-start.10) | collective-permute-done | bytes 294944 | tf_op jit(solution)/shard_map/ppermute | solution.py:26
  (59 shorter events, 28.3 us)
Async XLA Ops:
  0.6 7.3 %copy-start = (bf16[1152,576]{0,1:T(8,128)(2,1)S(1)}, bf16[1152,576]{0,1:T(8,128)(2,1)}, u32[]{:S(2)}) copy-start(bf16[1152,576]{0,1:T(8,128)(2,1)} %param.6) | copy-start | bytes 3981316
  0.6 15.2 %copy-start.12 = (bf16[256,576]{0,1:T(8,128)(2,1)S(1)}, bf16[256,576]{0,1:T(8,128)(2,1)}, u32[]{:S(2)}) copy-start(bf16[256,576]{0,1:T(8,128)(2,1)} %param.7) | copy-start | bytes 884740
  0.7 12.0 %collective-permute-start = (bf16[576,256]{1,0:T(8,128)(2,1)}, bf16[576,256]{1,0:T(8,128)(2,1)S(1)}, u32[]{:S(2)}, u32[]{:S(2)}) collective-permute-start(bf16[576,256]{1,0:T(8,128)(2,1)} %bitcast.27), channel_id=1, source_target_pairs={{0,1},{1,0},{2,3},{3,2},{4,5},{5,4},{6,7},{7,6},{8,9},{9,8},{10,11... | collective-permute-start | bytes 884744 | tf_op jit(solution)/shard_map/ppermute | solution.py:30
  4.7 21.7 %collective-permute-start.1 = (bf16[576,256]{1,0:T(8,128)(2,1)}, bf16[576,256]{1,0:T(8,128)(2,1)S(1)}, u32[]{:S(2)}, u32[]{:S(2)}) collective-permute-start(bf16[576,256]{1,0:T(8,128)(2,1)} %bitcast.28), channel_id=1, source_target_pairs={{0,4},{1,5},{2,6},{3,7},{4,8},{5,9},{6,10},{7,11},{8,12},{9,13},{1... | collective-permute-start | bytes 884744 | tf_op jit(solution)/shard_map/ppermute | solution.py:26
  10.3 27.6 %copy-start.1 = (bf16[256,1152]{1,0:T(8,128)(2,1)S(1)}, bf16[256,1152]{1,0:T(8,128)(2,1)}, u32[]{:S(2)}) copy-start(bf16[256,1152]{1,0:T(8,128)(2,1)} %features.3) | copy-start | bytes 1769476
  10.3 34.1 %collective-permute-start.5 = (bf16[576,256]{1,0:T(8,128)(2,1)}, bf16[576,256]{1,0:T(8,128)(2,1)}, u32[]{:S(2)}, u32[]{:S(2)}) collective-permute-start(bf16[576,256]{1,0:T(8,128)(2,1)} %convolution_convert_fusion), channel_id=1, source_target_pairs={{0,1},{1,0},{2,3},{3,2},{4,5},{5,4},{6,7},{7,6},{8,9},{9,8},{10,11... | collective-permute-start | bytes 884744 | tf_op jit(solution)/shard_map/ppermute | solution.py:30
  12.6 20.5 %collective-permute-start.2 = (bf16[576,256]{1,0:T(8,128)(2,1)S(1)}, bf16[576,256]{1,0:T(8,128)(2,1)S(1)}, u32[]{:S(2)}, u32[]{:S(2)}) collective-permute-start(bf16[576,256]{1,0:T(8,128)(2,1)S(1)} %collective-permute-done), channel_id=1, source_target_pairs={{0,4},{1,5},{2,6},{3,7},{4,8},{5,9},{6,10},{7,11},{8,12},{9,13},{1... | collective-permute-start | bytes 884744 | tf_op jit(solution)/shard_map/ppermute | solution.py:26
  15.9 51.5 %copy-start.2 = (bf16[1152,256]{1,0:T(8,128)(2,1)}, bf16[1152,256]{1,0:T(8,128)(2,1)S(1)}, u32[]{:S(2)}) copy-start(bf16[1152,256]{1,0:T(8,128)(2,1)S(1)} %pad_maximum_fusion.t0) | copy-start | bytes 1769476
  15.9 51.5 %collective-permute-start.3 = (bf16[1152,256]{1,0:T(8,128)(2,1)S(1)}, bf16[1152,256]{1,0:T(8,128)(2,1)}, u32[]{:S(2)}, u32[]{:S(2)}) collective-permute-start(bf16[1152,256]{1,0:T(8,128)(2,1)S(1)} %pad_maximum_fusion.t0), channel_id=1, source_target_pairs={{0,2},{1,3},{4,6},{5,7},{8,10},{9,11},{12,14},{13,15},{16,18},{17,... | collective-permute-start | bytes 1769480 | tf_op jit(solution)/shard_map/ppermute | solution.py:229
  33.9 33.6 %collective-permute-start.4 = (bf16[1152,256]{1,0:T(8,128)(2,1)}, bf16[1152,256]{1,0:T(8,128)(2,1)}, u32[]{:S(2)}, u32[]{:S(2)}) collective-permute-start(bf16[1152,256]{1,0:T(8,128)(2,1)} %constant_dynamic-update-slice_fusion.tm), channel_id=1, source_target_pairs={{0,2},{2,0},{1,3},{3,1},{4,6},{6,4},{5,7},{7,5},{8,10},{10,8},{9,1... | collective-permute-start | bytes 1769480 | tf_op jit(solution)/shard_map/ppermute | solution.py:30
  38.0 36.8 %collective-permute-start.12 = (bf16[256,1152]{1,0:T(8,128)(2,1)S(1)}, bf16[256,1152]{1,0:T(8,128)(2,1)S(1)}, u32[]{:S(2)}, u32[]{:S(2)}) collective-permute-start(bf16[256,1152]{1,0:T(8,128)(2,1)S(1)} %copy-done.1), channel_id=1, source_target_pairs={{0,509},{1,508},{2,511},{3,510},{4,0},{5,1},{6,2},{7,3},{8,4},{9,5... | collective-permute-start | bytes 1769480 | tf_op jit(solution)/shard_map/ppermute | solution.py:26
  41.3 19.8 %collective-permute-start.6 = (bf16[576,256]{1,0:T(8,128)(2,1)}, bf16[576,256]{1,0:T(8,128)(2,1)S(1)}, u32[]{:S(2)}, u32[]{:S(2)}) collective-permute-start(bf16[576,256]{1,0:T(8,128)(2,1)} %convolution_convert_fusion), channel_id=1, source_target_pairs={{0,509},{1,508},{2,511},{3,510},{4,0},{5,1},{6,2},{7,3},{8,4},{9,5... | collective-permute-start | bytes 884744 | tf_op jit(solution)/shard_map/ppermute | solution.py:26
  44.5 23.0 %collective-permute-start.7 = (bf16[576,256]{1,0:T(8,128)(2,1)}, bf16[576,256]{1,0:T(8,128)(2,1)S(1)}, u32[]{:S(2)}, u32[]{:S(2)}) collective-permute-start(bf16[576,256]{1,0:T(8,128)(2,1)} %collective-permute-done.5), channel_id=1, source_target_pairs={{0,509},{1,508},{2,511},{3,510},{4,0},{5,1},{6,2},{7,3},{8,4},{9,5... | collective-permute-start | bytes 884744 | tf_op jit(solution)/shard_map/ppermute | solution.py:26
  74.7 4.5 %copy-start.4 = (f32[576,256]{1,0:T(8,128)}, f32[576,256]{1,0:T(8,128)S(1)}, u32[]{:S(2)}) copy-start(f32[576,256]{1,0:T(8,128)S(1)} %get-tuple-element.14) | copy-start | bytes 1769476
  75.6 4.4 %collective-permute-start.13 = (bf16[2592,128]{1,0:T(8,128)(2,1)S(1)}, bf16[2592,128]{1,0:T(8,128)(2,1)S(1)}, u32[]{:S(2)}, u32[]{:S(2)}) collective-permute-start(bf16[2592,128]{1,0:T(8,128)(2,1)S(1)} %weight_part.3), channel_id=1, source_target_pairs={{0,2},{2,0},{1,3},{3,1},{4,6},{6,4},{5,7},{7,5},{8,10},{10,8},{9,1... | collective-permute-start | bytes 1990664 | tf_op jit(solution)/shard_map/ppermute | solution.py:30
  109.2 43.6 %copy-start.5 = (f32[576,256]{1,0:T(8,128)S(1)}, f32[576,256]{1,0:T(8,128)}, u32[]{:S(2)}) copy-start(f32[576,256]{1,0:T(8,128)} %copy-done.4) | copy-start | bytes 1769476
  109.2 6.2 %collective-permute-start.14 = (f32[48,128]{1,0:T(8,128)S(1)}, f32[48,128]{1,0:T(8,128)S(1)}, u32[]{:S(2)}, u32[]{:S(2)}) collective-permute-start(f32[48,128]{1,0:T(8,128)S(1)} %convert_reduce_fusion), channel_id=1, source_target_pairs={{0,32},{32,0},{1,33},{33,1},{2,34},{34,2},{3,35},{35,3},{4,36},{36... | collective-permute-start | bytes 73736 | tf_op jit(solution)/shard_map/ppermute | solution.py:30
  116.4 27.2 %all-to-all-start.1 = ((bf16[64,48,128]{2,1,0:T(8,128)(2,1)}), bf16[64,48,128]{2,1,0:T(8,128)(2,1)}, u32[]{:S(2)}, u32[]{:S(2)}) async-start(bf16[64,48,128]{2,1,0:T(8,128)(2,1)} %broadcast_in_dim.2), calls=%async_computation.1 | async-start | bytes 1572864 | tf_op jit(solution)/shard_map/all_to_all | solution.py:207
  123.8 44.4 %copy-start.7 = (f32[576,256]{1,0:T(8,128)S(1)}, f32[576,256]{1,0:T(8,128)}, u32[]{:S(2)}) copy-start(f32[576,256]{1,0:T(8,128)} %copy-done.6) | copy-start | bytes 1769476
  123.8 29.0 %collective-permute-start.9 = (bf16[576,256]{1,0:T(8,128)(2,1)}, bf16[576,256]{1,0:T(8,128)(2,1)}, u32[]{:S(2)}, u32[]{:S(2)}) collective-permute-start(bf16[576,256]{1,0:T(8,128)(2,1)} %copy-done.9), channel_id=1, source_target_pairs={{0,2},{2,0},{1,3},{3,1},{4,6},{6,4},{5,7},{7,5},{8,10},{10,8},{9,1... | collective-permute-start | bytes 884744 | tf_op jit(solution)/shard_map/ppermute | solution.py:30
  128.8 34.5 %collective-permute-start.11 = (bf16[576,256]{1,0:T(8,128)(2,1)S(1)}, bf16[576,256]{1,0:T(8,128)(2,1)}, u32[]{:S(2)}, u32[]{:S(2)}) collective-permute-start(bf16[576,256]{1,0:T(8,128)(2,1)S(1)} %get-tuple-element.16), channel_id=1, source_target_pairs={{2,0},{3,1},{6,4},{7,5},{10,8},{11,9},{14,12},{15,13},{18,16},{19,... | collective-permute-start | bytes 884744 | tf_op jit(solution)/shard_map/ppermute | solution.py:237
  131.5 30.1 %collective-permute-start.8 = (bf16[576,256]{1,0:T(8,128)(2,1)}, bf16[576,256]{1,0:T(8,128)(2,1)}, u32[]{:S(2)}, u32[]{:S(2)}) collective-permute-start(bf16[576,256]{1,0:T(8,128)(2,1)} %copy-done.8), channel_id=1, source_target_pairs={{0,4},{1,5},{2,6},{3,7},{4,8},{5,9},{6,10},{7,11},{8,12},{9,13},{1... | collective-permute-start | bytes 884744 | tf_op jit(solution)/shard_map/ppermute | solution.py:26
  143.6 26.4 %collective-permute-start.15 = (bf16[3072,128]{1,0:T(8,128)(2,1)}, bf16[3072,128]{1,0:T(8,128)(2,1)}, u32[]{:S(2)}, u32[]{:S(2)}) collective-permute-start(bf16[3072,128]{1,0:T(8,128)(2,1)} %bitcast.7), channel_id=1, source_target_pairs={{0,2},{2,0},{1,3},{3,1},{4,6},{6,4},{5,7},{7,5},{8,10},{10,8},{9,1... | collective-permute-start | bytes 2359304 | tf_op jit(solution)/shard_map/ppermute | solution.py:30
  154.6 13.7 %collective-permute-start.10 = (bf16[576,256]{1,0:T(8,128)(2,1)}, bf16[576,256]{1,0:T(8,128)(2,1)S(1)}, u32[]{:S(2)}, u32[]{:S(2)}) collective-permute-start(bf16[576,256]{1,0:T(8,128)(2,1)} %add_convert_fusion.2), channel_id=1, source_target_pairs={{0,509},{1,508},{2,511},{3,510},{4,0},{5,1},{6,2},{7,3},{8,4},{9,5... | collective-permute-start | bytes 884744 | tf_op jit(solution)/shard_map/ppermute | solution.py:26
  (6 other events, 16.3 us)

commit v3 on v2

--- a/solution.py
+++ b/solution.py
@@ -1,5 +1,3 @@
-import functools
-
 import jax
 import jax.numpy as jnp
 from jax import lax
@@ -35,11 +33,11 @@
 
 
 def pairs_kernel(
-    flags, log_scale, bias, t0, tm, p0, p1, i0, ie, if_,
+    flags, log_scale, bias, t0, tm, p0, p1, i0, came,
     gi_own, gt_own, gt_back, gi_back, d_p1, d_p0, w_own, w_next,
     ip, i0_n, ip_n,
 ):
-    half = ie.shape[0]
+    half = came.shape[0] // 2
     core, ft, fi = flags[0], flags[1], flags[2]
     scale = jnp.exp(jnp.full((1, 1), log_scale[0], f32))
     offset = bias[0]
@@ -48,8 +46,8 @@
     def part(which):
         return pl.ds(pl.multiple_of(which * half, half), half)
 
-    ip[part(fi)] = ie[...]
-    ip[part(1 - fi)] = if_[...]
+    ip[:half] = came[part(fi)]
+    ip[half:] = came[part(1 - fi)]
     i0_n[...] = i0[...].T
     ip_n[...] = ip[...].T
 
@@ -144,14 +142,14 @@
         d_p0[...] = out_text(dot(i0[:half], b4, (1, 0)), p0[:half], p0_inv, c4).astype(bf16)
 
 
-def block_pairs(flags, log_scale, bias, t0, tm, p0, p1, i0, ie, if_):
-    half, rows = ie.shape
+def block_pairs(flags, log_scale, bias, t0, tm, p0, p1, i0, came):
+    half, rows = came.shape[0] // 2, came.shape[1]
     smem, vmem = pl.BlockSpec(memory_space=pltpu.SMEM), pl.BlockSpec(memory_space=pltpu.VMEM)
     out = lambda dtype: jax.ShapeDtypeStruct((half, rows), dtype)
     return pl.pallas_call(
         pairs_kernel,
         out_shape=[out(f32)] * 3 + [out(bf16)] * 5,
-        in_specs=[smem] * 3 + [vmem] * 7,
+        in_specs=[smem] * 3 + [vmem] * 6,
         out_specs=[vmem] * 8,
         scratch_shapes=[
             pltpu.VMEM((2 * half, rows), bf16),
@@ -161,7 +159,7 @@
         compiler_params=pltpu.CompilerParams(vmem_limit_bytes=48 * 2**20),
         cost_estimate=pl.CostEstimate(flops=1_700_000_000, bytes_accessed=8_000_000, transcendentals=330_000),
         name="block_pairs",
-    )(flags, log_scale, bias, t0, tm, p0, p1, i0, ie, if_)
+    )(flags, log_scale, bias, t0, tm, p0, p1, i0, came)
 
 
 def weight_kernel(which, w_own, w_next, features, next_features, out):
@@ -188,57 +186,72 @@
     )(which, w_own, w_next, features, next_features)
 
 
-def weight_sum(w_own, w_next, features, next_features):
-    peers = lax.axis_size(PLANE)
-    core = lax.axis_index("core")
-    part, width = w_own.shape[0] // 2, features.shape[1]
-    groups = width // 128
-    rows = groups * part
-    index = core.astype(jnp.int32).reshape(1)
+def join_kernel(core, mine, other, out):
+    part = out.shape[0] // 2
+    here = pl.ds(pl.multiple_of(core[0] * part, part), part)
+    there = pl.ds(pl.multiple_of((1 - core[0]) * part, part), part)
+    for group in range(out.shape[1] // 128):
+        rows, columns = slice(group * part, (group + 1) * part), slice(group * 128, group * 128 + 128)
+        out[here, columns] = mine[rows]
+        out[there, columns] = other[rows]
+
+
+def joined(core, mine, other, shape):
+    smem, vmem = pl.BlockSpec(memory_space=pltpu.SMEM), pl.BlockSpec(memory_space=pltpu.VMEM)
+    return pl.pallas_call(
+        join_kernel,
+        out_shape=jax.ShapeDtypeStruct(shape, bf16),
+        in_specs=[smem] + [vmem] * 2,
+        out_specs=vmem,
+        compiler_params=pltpu.CompilerParams(vmem_limit_bytes=16 * 2**20),
+        cost_estimate=pl.CostEstimate(flops=0, bytes_accessed=3_000_000, transcendentals=0),
+        name="joined",
+    )(core, mine, other)
+
+
+def shards(features, img_weight, text_embed, log_scale, logit_bias):
+    core, y = lax.axis_index("core").astype(jnp.int32), lax.axis_index("y")
+    last = lax.axis_size("y") - 1
+    flags = jnp.stack([core, y == 0, y == last]).astype(jnp.int32)
+    half, width = img_weight.shape[1], features.shape[1]
+
+    t_own = text_embed.T
+    t_far = swapped(t_own, "rep")
+    next_features = shifted(features, -2)
+    i_own = lax.optimization_barrier(dot(img_weight, features, (0, 1)).astype(bf16))
+    i_far = swapped(i_own, "rep")
+    t0 = jnp.concatenate([t_own, t_far], 0)
+    tm = shifted(t0, 2)
+    i0 = jnp.concatenate([i_own, i_far], 0)
+    i0, next_features = lax.optimization_barrier((i0, next_features))
+    ip = shifted(i0, -2)
+    p0 = lax.ppermute(t0, "core", [(0, 1)])
+    p1 = swapped(tm, "core")
+    gi_own, gt_own, gt_back, gi_back, d_p1, d_p0, w_own, w_next = block_pairs(
+        flags, log_scale, logit_bias, t0, tm, p0, p1, i0, ip
+    )
+
+    index = core.reshape(1)
     theirs = weight_part(1 - index, w_own, w_next, features, next_features, bf16)
     mine = weight_part(index, w_own, w_next, features, next_features, f32)
+    peers = lax.axis_size(PLANE)
+    rows = mine.shape[0]
+    deep = -(-rows // (peers * 16)) * 16
     tiles = (mine + swapped(theirs, "core").astype(f32)).astype(bf16)
-    deep = -(-rows // (peers * 16)) * 16
     tiles = jnp.pad(tiles, ((0, peers * deep - rows), (0, 0))).reshape(peers, deep, 128)
     pieces = lax.all_to_all(tiles, PLANE, 0, 0, tiled=True)
+    gi_came = shifted(gi_back, 2)
+    image_grad = (gi_own + gi_came.astype(f32)).astype(bf16)
+    gt_sum = (gt_back + swapped(d_p1, "core").astype(f32)).astype(bf16)
+    gt_own = gt_own + lax.ppermute(d_p0, "core", [(1, 0)]).astype(f32)
     piece = jnp.sum(pieces.astype(f32), axis=0)
     piece = (piece + swapped(piece, "xh")).astype(bf16)
+    piece, image_grad, gt_sum, gt_own = lax.optimization_barrier((piece, image_grad, gt_sum, gt_own))
     sent = jnp.broadcast_to(piece[None], (peers, deep, 128))
     whole = lax.all_to_all(sent, PLANE, 0, 0, tiled=True).reshape(peers * deep, 128)
-    other = swapped(whole, "core")
-    first, last = jnp.where(core == 0, whole, other), jnp.where(core == 0, other, whole)
-    spread = lambda x: x[:rows].reshape(groups, part, 128).transpose(1, 0, 2).reshape(part, width)
-    return jnp.concatenate([spread(first), spread(last)], 0)
-
-
-def shards(features, img_weight, text_embed, log_scale, logit_bias):
-    core, y = lax.axis_index("core"), lax.axis_index("y")
-    last = lax.axis_size("y") - 1
-    flags = jnp.stack([core, y == 0, y == last]).astype(jnp.int32)
-    t_own = text_embed.T
-    t_far = swapped(t_own, "rep")
-    t_a = shifted(t_own, 2)
-    next_features = shifted(features, -2)
-    i_own = dot(img_weight, features, (0, 1)).astype(bf16)
-    i_far = swapped(i_own, "rep")
-    i_e = shifted(i_own, -2)
-    t_c = shifted(t_far, 2)
-    i_f = shifted(i_far, -2)
-    t0 = jnp.concatenate([t_own, t_far], 0)
-    tm = jnp.concatenate([t_a, t_c], 0)
-    p0 = lax.ppermute(t0, "core", [(0, 1)])
-    p1 = swapped(tm, "core")
-    i0 = jnp.concatenate([i_own, i_far], 0)
-    gi_own, gt_own, gt_back, gi_back, d_p1, d_p0, w_own, w_next = block_pairs(
-        flags, log_scale, logit_bias, t0, tm, p0, p1, i0, i_e, i_f
-    )
-    gi_came = shifted(gi_back, 2)
-    d_p1_came = swapped(d_p1, "core")
-    d_p0_came = lax.ppermute(d_p0, "core", [(1, 0)])
-    gt_came = shifted((gt_back + d_p1_came.astype(f32)).astype(bf16), -2)
-    image_grad = (gi_own + gi_came.astype(f32)).astype(bf16)
-    text_grad = (gt_own + gt_came.astype(f32) + d_p0_came.astype(f32)).astype(bf16)
-    weight_grad = weight_sum(w_own, w_next, features, next_features)
+    text_grad = (gt_own + shifted(gt_sum, -2).astype(f32)).astype(bf16)
+    whole, text_grad = lax.optimization_barrier((whole, text_grad))
+    weight_grad = joined(index, whole, swapped(whole, "core"), (half, width))
     return image_grad.T, text_grad.T, weight_grad.T
 
 

time: 179 us -> 148 us (0.83)
  blocking collectives: 28.8 us -> 0 us
  starting transfers between devices: 69 us -> 80 us
  local copies, waits for them, and re-layouts: 9.55 us -> 3.85 us
  waiting for transfers between devices: 47.8 us -> 43 us
  other arithmetic: 10.8 us -> 6.79 us
    all_to_all x1 -> x0, blocking collectives: 28.8 us -> none  [weight_sum(): pieces = lax.all_to_all(tiles, PLANE, 0, 0, tiled=True)]
    ppermute x7 -> x5, waiting for transfers between devices: 36.1 us -> 21.5 us  [shifted(): return lax.ppermute(array, AXES, pairs)]
    ppermute x7 -> x5, starting transfers between devices: 26 us -> 38.1 us  [shifted(): return lax.ppermute(array, AXES, pairs)]
    ppermute x7, waiting for transfers between devices: 2.6 us -> 8.44 us  [swapped(): return lax.ppermute(array, axis, [(0, 1), (1, 0)])]
    transpose x3 -> x0, other arithmetic: 5.41 us -> none  [shards(): return (image_grad.T, text_grad.T, weight_grad.T)]
    ppermute x7, starting transfers between devices: 31.7 us -> 26.9 us  [swapped(): return lax.ppermute(array, axis, [(0, 1), (1, 0)])]
    all_to_all x1 -> x2, waiting for transfers between devices: 9.06 us -> 13 us  [the longest x1 13 us: shards(): pieces = lax.all_to_all(tiles, PLANE, 0, 0, tiled=True)]
    all_to_all x1 -> x2, starting transfers between devices: 7.37 us -> 11.1 us  [the longest x1 6.47 us: shards(): pieces = lax.all_to_all(tiles, PLANE, 0, 0, tiled=True)]
  transfers between devices with their start and end apart: 17 -> 16, of which waited for: 8 -> 7; matrix products, arithmetic and copies ran while one was open for 6% -> 6% of each run, Pallas kernels for 3% -> 1%
where the time goes in v3:
time: 148 us; the launch traced here: 146 us
  starting transfers between devices  80 us (54%)
  waiting for transfers between devices  43 us (29%)
  Pallas kernels  8.18 us (6%)
  other arithmetic  6.79 us (5%)
  local copies, waits for them, and re-layouts  3.85 us (3%)
  between operations  2.26 us (2%)
  matrix products  1.64 us (1%)
    ppermute x5, starting transfers between devices, shifted(): return lax.ppermute(array, AXES, pairs)  38.1 us
    ppermute x7, starting transfers between devices, swapped(): return lax.ppermute(array, axis, [(0, 1), (1, 0)])  26.9 us
    ppermute x5, waiting for transfers between devices, shifted(): return lax.ppermute(array, AXES, pairs)  21.5 us
    all_to_all x1, waiting for transfers between devices, shards(): pieces = lax.all_to_all(tiles, PLANE, 0, 0, tiled=True)  13 us
    ppermute x7, waiting for transfers between devices, swapped(): return lax.ppermute(array, axis, [(0, 1), (1, 0)])  8.44 us
    all_to_all x1, starting transfers between devices, shards(): pieces = lax.all_to_all(tiles, PLANE, 0, 0, tiled=True)  6.47 us
    pallas_call x1, Pallas kernels, block_pairs(): pl.pallas_call(pairs_kernel, out_shape=[out(f32)] * 3 + [out(bf16)] * 5,...  5.18 us
    all_to_all x1, starting transfers between devices, shards(): lax.all_to_all(sent, PLANE, 0, 0, tiled=True).reshape(peers * deep, 128)  4.64 us
  transfers between devices with their start and end apart: 16, of which 7 were waited for; matrix products, arithmetic and copies ran while one was open for 6% of the time, Pallas kernels for 1%

profile of v3, /device:TPU:1, one launch (start us, length us, event | category | flops | bytes accessed | tf_op | source)
XLA Modules:
  0.0 145.7 jit_solution(8471428119371744932)
XLA Ops:
  0.6 4.1 %collective-permute-start = (bf16[576,256]{1,0:T(8,128)(2,1)}, bf16[576,256]{1,0:T(8,128)(2,1)S(1)}, u32[]{:S(2)}, u32[]{:S(2)}) collective-permute-start(bf16[576,256]{1,0:T(8,128)(2,1)} %bitcast.15), channel_id=1, source_target_pairs={{0,1},{1,0},{2,3},{3,2},{4,5},{5,4},{6,7},{7,6},{8,9},{9,8},{10,11... | collective-permute-start | bytes 884744 | tf_op jit(solution)/shard_map/ppermute | solution.py:28
  4.7 15.1 %collective-permute-start.5 = (bf16[256,1152]{1,0:T(8,128)(2,1)}, bf16[256,1152]{1,0:T(8,128)(2,1)S(1)}, u32[]{:S(2)}, u32[]{:S(2)}) collective-permute-start(bf16[256,1152]{1,0:T(8,128)(2,1)} %features.3), channel_id=1, source_target_pairs={{0,509},{1,508},{2,511},{3,510},{4,0},{5,1},{6,2},{7,3},{8,4},{9,5... | collective-permute-start | bytes 1769480 | tf_op jit(solution)/shard_map/ppermute | solution.py:24
  20.9 1.9 %collective-permute-start.1 = (bf16[1152,256]{1,0:T(8,128)(2,1)S(1)}, bf16[1152,256]{1,0:T(8,128)(2,1)}, u32[]{:S(2)}, u32[]{:S(2)}) collective-permute-start(bf16[1152,256]{1,0:T(8,128)(2,1)S(1)} %pad_maximum_fusion.t0), channel_id=1, source_target_pairs={{0,4},{1,5},{2,6},{3,7},{4,8},{5,9},{6,10},{7,11},{8,12},{9,13},{1... | collective-permute-start | bytes 1769480 | tf_op jit(solution)/shard_map/ppermute | solution.py:24
  22.8 1.6 %convolution_convert_fusion = bf16[576,256]{1,0:T(8,128)(2,1)S(1)} fusion(bf16[1152,576]{0,1:T(8,128)(2,1)S(1)} %copy-done, bf16[256,1152]{1,0:T(8,128)(2,1)} %features.3), kind=kOutput, calls=%fused_computation.2 | convolution fusion | flops 339886080 | bytes 2211840 | tf_op jit(solution)/shard_map/dot_general | solution.py:32
  24.4 2.2 %collective-permute-start.4 = (bf16[576,256]{1,0:T(8,128)(2,1)S(1)}, bf16[576,256]{1,0:T(8,128)(2,1)S(1)}, u32[]{:S(2)}, u32[]{:S(2)}) collective-permute-start(bf16[576,256]{1,0:T(8,128)(2,1)S(1)} %convolution_convert_fusion), channel_id=1, source_target_pairs={{0,1},{1,0},{2,3},{3,2},{4,5},{5,4},{6,7},{7,6},{8,9},{9,8},{10,11... | collective-permute-start | bytes 884744 | tf_op jit(solution)/shard_map/ppermute | solution.py:28
  28.0 5.7 %collective-permute-done.4 = bf16[576,256]{1,0:T(8,128)(2,1)S(1)} collective-permute-done((bf16[576,256]{1,0:T(8,128)(2,1)S(1)}, bf16[576,256]{1,0:T(8,128)(2,1)S(1)}, u32[]{:S(2)}, u32[]{:S(2)}) %collective-permute-start.4) | collective-permute-done | bytes 294944 | tf_op jit(solution)/shard_map/ppermute | solution.py:28
  33.8 8.5 %collective-permute-start.6 = (bf16[1152,256]{1,0:T(8,128)(2,1)S(1)}, bf16[1152,256]{1,0:T(8,128)(2,1)}, u32[]{:S(2)}, u32[]{:S(2)}) collective-permute-start(bf16[1152,256]{1,0:T(8,128)(2,1)S(1)} %pad_maximum_fusion.1.i0), channel_id=1, source_target_pairs={{0,509},{1,508},{2,511},{3,510},{4,0},{5,1},{6,2},{7,3},{8,4},{9,5... | collective-permute-start | bytes 1769480 | tf_op jit(solution)/shard_map/ppermute | solution.py:24
  43.1 4.5 %collective-permute-start.3 = (bf16[1152,256]{1,0:T(8,128)(2,1)}, bf16[1152,256]{1,0:T(8,128)(2,1)}, u32[]{:S(2)}, u32[]{:S(2)}) collective-permute-start(bf16[1152,256]{1,0:T(8,128)(2,1)} %collective-permute-done.1.tm), channel_id=1, source_target_pairs={{0,2},{2,0},{1,3},{3,1},{4,6},{6,4},{5,7},{7,5},{8,10},{10,8},{9,1... | collective-permute-start | bytes 1769480 | tf_op jit(solution)/shard_map/ppermute | solution.py:28
  49.0 3.5 %collective-permute-done.6.came = bf16[1152,256]{1,0:T(8,128)(2,1)} collective-permute-done((bf16[1152,256]{1,0:T(8,128)(2,1)S(1)}, bf16[1152,256]{1,0:T(8,128)(2,1)}, u32[]{:S(2)}, u32[]{:S(2)}) %collective-permute-start.6) | collective-permute-done | bytes 589856 | tf_op jit(solution)/shard_map/ppermute | solution.py:24
  53.6 5.2 %block_pairs.1 = (f32[576,256]{1,0:T(8,128)S(1)}, f32[576,256]{1,0:T(8,128)S(1)}, f32[576,256]{1,0:T(8,128)S(1)}, bf16[576,256]{1,0:T(8,128)(2,1)S(1)}, bf16[576...) custom-call(s32[3]{0:T(128)S(1)} %pad_add_fusion.flags, ...), custom_call_target="tpu_custom_call" | custom-call | flops 1700000000 | bytes 8000000 | tf_op jit(solution)/shard_map/block_pairs/pallas_call | solution.py:149
  59.7 5.2 %collective-permute-start.7 = (bf16[2592,128]{1,0:T(8,128)(2,1)S(1)}, bf16[2592,128]{1,0:T(8,128)(2,1)S(1)}, u32[]{:S(2)}, u32[]{:S(2)}) collective-permute-start(bf16[2592,128]{1,0:T(8,128)(2,1)S(1)} %weight_part.3), channel_id=1, source_target_pairs={{0,2},{2,0},{1,3},{3,1},{4,6},{6,4},{5,7},{7,5},{8,10},{10,8},{9,1... | collective-permute-start | bytes 1990664 | tf_op jit(solution)/shard_map/ppermute | solution.py:28
  67.7 6.5 %all-to-all-start = ((bf16[64,48,128]{2,1,0:T(8,128)(2,1)}), bf16[64,48,128]{2,1,0:T(8,128)(2,1)}, u32[]{:S(2)}, u32[]{:S(2)}) async-start(bf16[64,48,128]{2,1,0:T(8,128)(2,1)} %bitcast.13), calls=%async_computation | async-start | bytes 1572864 | tf_op jit(solution)/shard_map/all_to_all | solution.py:242
  74.2 2.6 %collective-permute-start.11 = (bf16[576,256]{1,0:T(8,128)(2,1)}, bf16[576,256]{1,0:T(8,128)(2,1)S(1)}, u32[]{:S(2)}, u32[]{:S(2)}) collective-permute-start(bf16[576,256]{1,0:T(8,128)(2,1)} %copy-done.9), channel_id=1, source_target_pairs={{2,0},{3,1},{6,4},{7,5},{10,8},{11,9},{14,12},{15,13},{18,16},{19,... | collective-permute-start | bytes 884744 | tf_op jit(solution)/shard_map/ppermute | solution.py:246
  76.8 1.9 %collective-permute-start.10 = (bf16[576,256]{1,0:T(8,128)(2,1)}, bf16[576,256]{1,0:T(8,128)(2,1)S(1)}, u32[]{:S(2)}, u32[]{:S(2)}) collective-permute-start(bf16[576,256]{1,0:T(8,128)(2,1)} %copy-done.8), channel_id=1, source_target_pairs={{0,2},{2,0},{1,3},{3,1},{4,6},{6,4},{5,7},{7,5},{8,10},{10,8},{9,1... | collective-permute-start | bytes 884744 | tf_op jit(solution)/shard_map/ppermute | solution.py:28
  78.7 3.1 %collective-permute-start.9 = (bf16[576,256]{1,0:T(8,128)(2,1)S(1)}, bf16[576,256]{1,0:T(8,128)(2,1)}, u32[]{:S(2)}, u32[]{:S(2)}) collective-permute-start(bf16[576,256]{1,0:T(8,128)(2,1)S(1)} %get-tuple-element.24), channel_id=1, source_target_pairs={{0,4},{1,5},{2,6},{3,7},{4,8},{5,9},{6,10},{7,11},{8,12},{9,13},{1... | collective-permute-start | bytes 884744 | tf_op jit(solution)/shard_map/ppermute | solution.py:24
  83.6 13.0 %all-to-all-done = bf16[64,48,128]{2,1,0:T(8,128)(2,1)} async-done(((bf16[64,48,128]{2,1,0:T(8,128)(2,1)}), bf16[64,48,128]{2,1,0:T(8,128)(2,1)}, u32[]{:S(2)}, u32[]{:S(2)}) %all-to-all-start) | async-done | bytes 786464 | tf_op jit(solution)/shard_map/all_to_all | solution.py:242
  97.9 5.2 %collective-permute-start.8 = (f32[48,128]{1,0:T(8,128)S(1)}, f32[48,128]{1,0:T(8,128)S(1)}, u32[]{:S(2)}, u32[]{:S(2)}) collective-permute-start(f32[48,128]{1,0:T(8,128)S(1)} %convert_reduce_fusion), channel_id=1, source_target_pairs={{0,32},{32,0},{1,33},{33,1},{2,34},{34,2},{3,35},{35,3},{4,36},{36... | collective-permute-start | bytes 73736 | tf_op jit(solution)/shard_map/ppermute | solution.py:28
  103.1 3.8 %collective-permute-done.9 = bf16[576,256]{1,0:T(8,128)(2,1)} collective-permute-done((bf16[576,256]{1,0:T(8,128)(2,1)S(1)}, bf16[576,256]{1,0:T(8,128)(2,1)}, u32[]{:S(2)}, u32[]{:S(2)}) %collective-permute-start.9) | collective-permute-done | bytes 294944 | tf_op jit(solution)/shard_map/ppermute | solution.py:24
  106.9 1.7 %add_convert_fusion.3 = bf16[576,256]{1,0:T(8,128)(2,1)} fusion(f32[576,256]{1,0:T(8,128)S(1)} %get-tuple-element.23, bf16[576,256]{1,0:T(8,128)(2,1)} %collective-permute-done.9), kind=kLoop, calls=%fused_computation.8 | loop fusion | flops 442368 | bytes 1179648 | tf_op jit(solution)/shard_map/convert_element_type | solution.py:244
  109.7 4.6 %all-to-all-start.1 = ((bf16[64,48,128]{2,1,0:T(8,128)(2,1)}), bf16[64,48,128]{2,1,0:T(8,128)(2,1)S(1)}, u32[]{:S(2)}, u32[]{:S(2)}) async-start(bf16[64,48,128]{2,1,0:T(8,128)(2,1)} %broadcast_in_dim.2), calls=%async_computation.1 | async-start | bytes 1572864 | tf_op jit(solution)/shard_map/all_to_all | solution.py:251
  114.3 9.4 %collective-permute-start.12 = (bf16[576,256]{1,0:T(8,128)(2,1)S(1)}, bf16[576,256]{1,0:T(8,128)(2,1)S(1)}, u32[]{:S(2)}, u32[]{:S(2)}) collective-permute-start(bf16[576,256]{1,0:T(8,128)(2,1)S(1)} %copy-done.11), channel_id=1, source_target_pairs={{0,509},{1,508},{2,511},{3,510},{4,0},{5,1},{6,2},{7,3},{8,4},{9,5... | collective-permute-start | bytes 884744 | tf_op jit(solution)/shard_map/ppermute | solution.py:24
  123.8 14.2 %collective-permute-done.12 = bf16[576,256]{1,0:T(8,128)(2,1)S(1)} collective-permute-done((bf16[576,256]{1,0:T(8,128)(2,1)S(1)}, bf16[576,256]{1,0:T(8,128)(2,1)S(1)}, u32[]{:S(2)}, u32[]{:S(2)}) %collective-permute-start.12) | collective-permute-done | bytes 294944 | tf_op jit(solution)/shard_map/ppermute | solution.py:24
  138.8 3.8 %collective-permute-start.13 = (bf16[3072,128]{1,0:T(8,128)(2,1)S(1)}, bf16[3072,128]{1,0:T(8,128)(2,1)S(1)}, u32[]{:S(2)}, u32[]{:S(2)}) collective-permute-start(bf16[3072,128]{1,0:T(8,128)(2,1)S(1)} %bitcast.11), channel_id=1, source_target_pairs={{0,2},{2,0},{1,3},{3,1},{4,6},{6,4},{5,7},{7,5},{8,10},{10,8},{9,1... | collective-permute-start | bytes 2359304 | tf_op jit(solution)/shard_map/ppermute | solution.py:28
  142.6 1.9 %collective-permute-done.13.other = bf16[3072,128]{1,0:T(8,128)(2,1)S(1)} collective-permute-done((bf16[3072,128]{1,0:T(8,128)(2,1)S(1)}, bf16[3072,128]{1,0:T(8,128)(2,1)S(1)}, u32[]{:S(2)}, u32[]{:S(2)}) %collective-permute-start.13) | collective-permute-done | bytes 786464 | tf_op jit(solution)/shard_map/ppermute | solution.py:28
  (49 shorter events, 14.0 us)
Async XLA Ops:
  0.6 22.2 %copy-start = (bf16[1152,576]{0,1:T(8,128)(2,1)S(1)}, bf16[1152,576]{0,1:T(8,128)(2,1)}, u32[]{:S(2)}) copy-start(bf16[1152,576]{0,1:T(8,128)(2,1)} %param.6) | copy-start | bytes 3981316
  0.6 19.2 %collective-permute-start = (bf16[576,256]{1,0:T(8,128)(2,1)}, bf16[576,256]{1,0:T(8,128)(2,1)S(1)}, u32[]{:S(2)}, u32[]{:S(2)}) collective-permute-start(bf16[576,256]{1,0:T(8,128)(2,1)} %bitcast.15), channel_id=1, source_target_pairs={{0,1},{1,0},{2,3},{3,2},{4,5},{5,4},{6,7},{7,6},{8,9},{9,8},{10,11... | collective-permute-start | bytes 884744 | tf_op jit(solution)/shard_map/ppermute | solution.py:28
  4.7 29.0 %collective-permute-start.5 = (bf16[256,1152]{1,0:T(8,128)(2,1)}, bf16[256,1152]{1,0:T(8,128)(2,1)S(1)}, u32[]{:S(2)}, u32[]{:S(2)}) collective-permute-start(bf16[256,1152]{1,0:T(8,128)(2,1)} %features.3), channel_id=1, source_target_pairs={{0,509},{1,508},{2,511},{3,510},{4,0},{5,1},{6,2},{7,3},{8,4},{9,5... | collective-permute-start | bytes 1769480 | tf_op jit(solution)/shard_map/ppermute | solution.py:24
  20.9 22.3 %collective-permute-start.1 = (bf16[1152,256]{1,0:T(8,128)(2,1)S(1)}, bf16[1152,256]{1,0:T(8,128)(2,1)}, u32[]{:S(2)}, u32[]{:S(2)}) collective-permute-start(bf16[1152,256]{1,0:T(8,128)(2,1)S(1)} %pad_maximum_fusion.t0), channel_id=1, source_target_pairs={{0,4},{1,5},{2,6},{3,7},{4,8},{5,9},{6,10},{7,11},{8,12},{9,13},{1... | collective-permute-start | bytes 1769480 | tf_op jit(solution)/shard_map/ppermute | solution.py:24
  24.4 9.3 %collective-permute-start.4 = (bf16[576,256]{1,0:T(8,128)(2,1)S(1)}, bf16[576,256]{1,0:T(8,128)(2,1)S(1)}, u32[]{:S(2)}, u32[]{:S(2)}) collective-permute-start(bf16[576,256]{1,0:T(8,128)(2,1)S(1)} %convolution_convert_fusion), channel_id=1, source_target_pairs={{0,1},{1,0},{2,3},{3,2},{4,5},{5,4},{6,7},{7,6},{8,9},{9,8},{10,11... | collective-permute-start | bytes 884744 | tf_op jit(solution)/shard_map/ppermute | solution.py:28
  26.7 22.3 %collective-permute-start.2 = (bf16[1152,256]{1,0:T(8,128)(2,1)S(1)}, bf16[1152,256]{1,0:T(8,128)(2,1)}, u32[]{:S(2)}, u32[]{:S(2)}) collective-permute-start(bf16[1152,256]{1,0:T(8,128)(2,1)S(1)} %pad_maximum_fusion.t0), channel_id=1, source_target_pairs={{0,2},{1,3},{4,6},{5,7},{8,10},{9,11},{12,14},{13,15},{16,18},{17,... | collective-permute-start | bytes 1769480 | tf_op jit(solution)/shard_map/ppermute | solution.py:228
  33.8 18.8 %collective-permute-start.6 = (bf16[1152,256]{1,0:T(8,128)(2,1)S(1)}, bf16[1152,256]{1,0:T(8,128)(2,1)}, u32[]{:S(2)}, u32[]{:S(2)}) collective-permute-start(bf16[1152,256]{1,0:T(8,128)(2,1)S(1)} %pad_maximum_fusion.1.i0), channel_id=1, source_target_pairs={{0,509},{1,508},{2,511},{3,510},{4,0},{5,1},{6,2},{7,3},{8,4},{9,5... | collective-permute-start | bytes 1769480 | tf_op jit(solution)/shard_map/ppermute | solution.py:24
  43.1 9.4 %collective-permute-start.3 = (bf16[1152,256]{1,0:T(8,128)(2,1)}, bf16[1152,256]{1,0:T(8,128)(2,1)}, u32[]{:S(2)}, u32[]{:S(2)}) collective-permute-start(bf16[1152,256]{1,0:T(8,128)(2,1)} %collective-permute-done.1.tm), channel_id=1, source_target_pairs={{0,2},{2,0},{1,3},{3,1},{4,6},{6,4},{5,7},{7,5},{8,10},{10,8},{9,1... | collective-permute-start | bytes 1769480 | tf_op jit(solution)/shard_map/ppermute | solution.py:28
  49.0 9.8 %copy-start.1 = (bf16[256,1152]{1,0:T(8,128)(2,1)S(1)}, bf16[256,1152]{1,0:T(8,128)(2,1)}, u32[]{:S(2)}) copy-start(bf16[256,1152]{1,0:T(8,128)(2,1)} %features.3) | copy-start | bytes 1769476
  58.8 6.9 %copy-start.4 = (f32[576,256]{1,0:T(8,128)}, f32[576,256]{1,0:T(8,128)S(1)}, u32[]{:S(2)}) copy-start(f32[576,256]{1,0:T(8,128)S(1)} %get-tuple-element.25) | copy-start | bytes 1769476
  58.8 6.9 %copy-start.6 = (f32[576,256]{1,0:T(8,128)}, f32[576,256]{1,0:T(8,128)S(1)}, u32[]{:S(2)}) copy-start(f32[576,256]{1,0:T(8,128)S(1)} %get-tuple-element.27) | copy-start | bytes 1769476
  58.8 6.9 %copy-start.8 = (bf16[576,256]{1,0:T(8,128)(2,1)}, bf16[576,256]{1,0:T(8,128)(2,1)S(1)}, u32[]{:S(2)}) copy-start(bf16[576,256]{1,0:T(8,128)(2,1)S(1)} %get-tuple-element.26) | copy-start | bytes 884740
  59.7 6.9 %collective-permute-start.7 = (bf16[2592,128]{1,0:T(8,128)(2,1)S(1)}, bf16[2592,128]{1,0:T(8,128)(2,1)S(1)}, u32[]{:S(2)}, u32[]{:S(2)}) collective-permute-start(bf16[2592,128]{1,0:T(8,128)(2,1)S(1)} %weight_part.3), channel_id=1, source_target_pairs={{0,2},{2,0},{1,3},{3,1},{4,6},{6,4},{5,7},{7,5},{8,10},{10,8},{9,1... | collective-permute-start | bytes 1990664 | tf_op jit(solution)/shard_map/ppermute | solution.py:28
  66.8 15.1 %copy-start.7 = (f32[576,256]{1,0:T(8,128)S(1)}, f32[576,256]{1,0:T(8,128)}, u32[]{:S(2)}) copy-start(f32[576,256]{1,0:T(8,128)} %copy-done.6) | copy-start | bytes 1769476
  67.7 15.1 %copy-start.5 = (f32[576,256]{1,0:T(8,128)S(1)}, f32[576,256]{1,0:T(8,128)}, u32[]{:S(2)}) copy-start(f32[576,256]{1,0:T(8,128)} %copy-done.4) | copy-start | bytes 1769476
  67.7 28.9 %all-to-all-start = ((bf16[64,48,128]{2,1,0:T(8,128)(2,1)}), bf16[64,48,128]{2,1,0:T(8,128)(2,1)}, u32[]{:S(2)}, u32[]{:S(2)}) async-start(bf16[64,48,128]{2,1,0:T(8,128)(2,1)} %bitcast.13), calls=%async_computation | async-start | bytes 1572864 | tf_op jit(solution)/shard_map/all_to_all | solution.py:242
  74.2 7.7 %collective-permute-start.11 = (bf16[576,256]{1,0:T(8,128)(2,1)}, bf16[576,256]{1,0:T(8,128)(2,1)S(1)}, u32[]{:S(2)}, u32[]{:S(2)}) collective-permute-start(bf16[576,256]{1,0:T(8,128)(2,1)} %copy-done.9), channel_id=1, source_target_pairs={{2,0},{3,1},{6,4},{7,5},{10,8},{11,9},{14,12},{15,13},{18,16},{19,... | collective-permute-start | bytes 884744 | tf_op jit(solution)/shard_map/ppermute | solution.py:246
  76.8 6.0 %collective-permute-start.10 = (bf16[576,256]{1,0:T(8,128)(2,1)}, bf16[576,256]{1,0:T(8,128)(2,1)S(1)}, u32[]{:S(2)}, u32[]{:S(2)}) collective-permute-start(bf16[576,256]{1,0:T(8,128)(2,1)} %copy-done.8), channel_id=1, source_target_pairs={{0,2},{2,0},{1,3},{3,1},{4,6},{6,4},{5,7},{7,5},{8,10},{10,8},{9,1... | collective-permute-start | bytes 884744 | tf_op jit(solution)/shard_map/ppermute | solution.py:28
  78.7 28.2 %collective-permute-start.9 = (bf16[576,256]{1,0:T(8,128)(2,1)S(1)}, bf16[576,256]{1,0:T(8,128)(2,1)}, u32[]{:S(2)}, u32[]{:S(2)}) collective-permute-start(bf16[576,256]{1,0:T(8,128)(2,1)S(1)} %get-tuple-element.24), channel_id=1, source_target_pairs={{0,4},{1,5},{2,6},{3,7},{4,8},{5,9},{6,10},{7,11},{8,12},{9,13},{1... | collective-permute-start | bytes 884744 | tf_op jit(solution)/shard_map/ppermute | solution.py:24
  97.9 10.8 %collective-permute-start.8 = (f32[48,128]{1,0:T(8,128)S(1)}, f32[48,128]{1,0:T(8,128)S(1)}, u32[]{:S(2)}, u32[]{:S(2)}) collective-permute-start(f32[48,128]{1,0:T(8,128)S(1)} %convert_reduce_fusion), channel_id=1, source_target_pairs={{0,32},{32,0},{1,33},{33,1},{2,34},{34,2},{3,35},{35,3},{4,36},{36... | collective-permute-start | bytes 73736 | tf_op jit(solution)/shard_map/ppermute | solution.py:28
  108.7 29.3 %copy-start.10 = (f32[576,256]{1,0:T(8,128)S(1)}, f32[576,256]{1,0:T(8,128)}, u32[]{:S(2)}) copy-start(f32[576,256]{1,0:T(8,128)} %convert_add_fusion) | copy-start | bytes 1769476
  109.7 29.1 %all-to-all-start.1 = ((bf16[64,48,128]{2,1,0:T(8,128)(2,1)}), bf16[64,48,128]{2,1,0:T(8,128)(2,1)S(1)}, u32[]{:S(2)}, u32[]{:S(2)}) async-start(bf16[64,48,128]{2,1,0:T(8,128)(2,1)} %broadcast_in_dim.2), calls=%async_computation.1 | async-start | bytes 1572864 | tf_op jit(solution)/shard_map/all_to_all | solution.py:251
  114.3 23.6 %collective-permute-start.12 = (bf16[576,256]{1,0:T(8,128)(2,1)S(1)}, bf16[576,256]{1,0:T(8,128)(2,1)S(1)}, u32[]{:S(2)}, u32[]{:S(2)}) collective-permute-start(bf16[576,256]{1,0:T(8,128)(2,1)S(1)} %copy-done.11), channel_id=1, source_target_pairs={{0,509},{1,508},{2,511},{3,510},{4,0},{5,1},{6,2},{7,3},{8,4},{9,5... | collective-permute-start | bytes 884744 | tf_op jit(solution)/shard_map/ppermute | solution.py:24
  138.8 5.7 %collective-permute-start.13 = (bf16[3072,128]{1,0:T(8,128)(2,1)S(1)}, bf16[3072,128]{1,0:T(8,128)(2,1)S(1)}, u32[]{:S(2)}, u32[]{:S(2)}) collective-permute-start(bf16[3072,128]{1,0:T(8,128)(2,1)S(1)} %bitcast.11), channel_id=1, source_target_pairs={{0,2},{2,0},{1,3},{3,1},{4,6},{6,4},{5,7},{7,5},{8,10},{10,8},{9,1... | collective-permute-start | bytes 2359304 | tf_op jit(solution)/shard_map/ppermute | solution.py:28
  (4 other events, 14.5 us)

commit v4 on v0

v4 whole, which is shorter than its diff:
```python
import functools

import jax
import jax.numpy as jnp
from jax import lax
from jax.experimental import pallas as pl
from jax.experimental.pallas import tpu as pltpu
from jax.sharding import Mesh, PartitionSpec as P

AXES = ("z", "xh", "y", "core", "rep")
DP = ("z", "xh", "y", "core")
PLANE = ("z", "y")
SIZES = (8, 2, 8, 2, 2)
N_DP, RUN = 256, 16

epsilon = 1e-06
f32, bf16 = jnp.float32, jnp.bfloat16


def shifted(array, by):
    pairs = []
    for block in range(N_DP):
        to = (block + by) % N_DP
        cross = block // RUN != to // RUN
        pairs += [(2 * block + rep, 2 * to + (1 - rep if cross else rep)) for rep in range(2)]
    return lax.ppermute(array, AXES, pairs)


def swapped(array, axis):
    return lax.ppermute(array, axis, [(0, 1), (1, 0)])


def dot(a, b, contract):
    return lax.dot_general(a, b, ((contract[:1], contract[1:]), ((), ())), preferred_element_type=f32)


def column(row):
    return jnp.broadcast_to(row, (128, row.shape[1])).T[:, :1]


def row(col):
    return jnp.broadcast_to(col, (col.shape[0], 128)).T[:1]


def inverse(*refs):
    squares = 0.0
    for ref in refs:
        values = ref[...].astype(f32)
        squares = squares + jnp.sum(values * values, axis=0, keepdims=True)
    return lax.rsqrt(squares + epsilon)


def part(which, size):
    return pl.ds(pl.multiple_of(which * size, size), size)


def pair(scale, offset, image, text, flip, image_col, text_inv, diagonal=False):
    half = text.shape[0] // 2
    raw = dot(image[:, :half], text[part(flip, half)], (1, 0)) + dot(image[:, half:], text[part(1 - flip, half)], (1, 0))
    s = raw * image_col * text_inv
    g = 1.0 / (1.0 + jnp.exp(-(scale * s + offset)))
    if diagonal:
        at = lax.broadcasted_iota(jnp.int32, g.shape, 0) == lax.broadcasted_iota(jnp.int32, g.shape, 1)
        g = g - jnp.where(at, 1.0, 0.0)
    gs = g * s
    return (
        (g * text_inv).astype(bf16),
        (g * image_col).astype(bf16),
        jnp.sum(gs, axis=1, keepdims=True),
        jnp.sum(gs, axis=0, keepdims=True),
    )


def removed(grad, hat, scale, inv, dots):
    return (grad - hat.astype(f32) * (inv * dots)) * (scale * inv)


def place():
    y = lax.axis_index("y")
    return lax.axis_index("core"), (y == 0).astype(jnp.int32), (y == lax.axis_size("y") - 1).astype(jnp.int32)


I0_INV, T0_INV, TM_INV, DOT01, C0, C1 = range(6)
IP_INV, P1_INV, P0_INV, C2, C3, C4 = range(6)


def first_kernel(log_scale, bias, t0, tm, i_own, i_far, own, i0_n, b, stats):
    half, (_, ft, _) = own.shape[0], place()
    scale, offset = jnp.exp(jnp.full((1, 1), log_scale[0], f32)), bias[0]
    i0_n[:, :half] = i_own[...].T
    i0_n[:, half:] = i_far[...].T
    i0_inv, t0_inv, tm_inv = inverse(i_own, i_far), inverse(t0), inverse(tm)
    i0_col = column(i0_inv)
    a0, b[0], r0, c0 = pair(scale, offset, i0_n, t0, 0, i0_col, t0_inv, True)
    a1, b[1], r1, c1 = pair(scale, offset, i0_n, tm, ft, i0_col, tm_inv)
    own[...] = dot(t0[:half], a0, (1, 1)) + dot(tm[part(ft, half)], a1, (1, 1))
    stats[...] = jnp.concatenate([i0_inv, t0_inv, tm_inv, row(r0 + r1), c0, c1, c0, c1], 0)


def second_kernel(
    log_scale, bias, tm, p0, p1, i_e, i_f, own, i_own, i0_n, stats,
    gi_own, gi_back, w_own, w_next, ip, b, stats2,
    ip_n,
):
    half = own.shape[0]
    core, ft, fi = place()
    scale, offset = jnp.exp(jnp.full((1, 1), log_scale[0], f32)), bias[0]
    ip[part(fi, half)] = i_e[...]
    ip[part(1 - fi, half)] = i_f[...]
    ip_n[...] = ip[...].T
    i0_inv, tm_inv, dots01 = stats[I0_INV : I0_INV + 1], stats[TM_INV : TM_INV + 1], stats[DOT01 : DOT01 + 1]
    ip_inv, p1_inv, p0_inv = inverse(ip), inverse(p1), inverse(p0)
    i0_col, ip_col = column(i0_inv), column(ip_inv)
    a2, b[0], r2, c2 = pair(scale, offset, ip_n, tm, ft, ip_col, tm_inv)
    a3, b[1], r3, c3 = pair(scale, offset, i0_n, p1, ft, i0_col, p1_inv)
    own_sum = own[...] + dot(p1[part(ft, half)], a3, (1, 1))

    def store_next(first, other, dots):
        near = removed(first(), ip[:half], scale, ip_inv, dots).astype(bf16)
        gi_back[...] = near
        w_next[...] = near

        @pl.when(fi == 1)
        def _():
            gi_back[...] = removed(other(), ip[half:], scale, ip_inv, dots).astype(bf16)

    def store_stats(c4):
        stats2[...] = jnp.concatenate([ip_inv, p1_inv, p0_inv, c2, c3, c4, c2, c3], 0)

    @pl.when(core == 0)
    def _():
        a4, b[2], r4, c4 = pair(scale, offset, ip_n, p1, ft, ip_col, p1_inv)
        whole = removed(own_sum, i_own[...], scale, i0_inv, dots01 + row(r3))
        gi_own[...] = whole
        w_own[...] = whole.astype(bf16)
        store_next(
            lambda: dot(tm[part(ft, half)], a2, (1, 1)) + dot(p1[part(ft, half)], a4, (1, 1)),
            lambda: dot(tm[part(1 - ft, half)], a2, (1, 1)) + dot(p1[part(1 - ft, half)], a4, (1, 1)),
            row(r2 + r4),
        )
        store_stats(c4)

    @pl.when(core == 1)
    def _():
        a4, b[2], r4, c4 = pair(scale, offset, i0_n, p0, 0, i0_col, p0_inv)
        whole = removed(own_sum + dot(p0[:half], a4, (1, 1)), i_own[...], scale, i0_inv, dots01 + row(r3 + r4))
        gi_own[...] = whole
        w_own[...] = whole.astype(bf16)
        store_next(
            lambda: dot(tm[part(ft, half)], a2, (1, 1)),
            lambda: dot(tm[part(1 - ft, half)], a2, (1, 1)),
            row(r2),
        )
        store_stats(c4)


def text_kernel(log_scale, t0, tm, p0, p1, i_own, i_far, ip, b01, b234, stats, stats2, gt_own, gt_back, d_p1, d_p0):
    half = gt_own.shape[0]
    core, ft, _ = place()
    scale = jnp.exp(jnp.full((1, 1), log_scale[0], f32))
    t0_inv, tm_inv, p1_inv = stats[T0_INV : T0_INV + 1], stats[TM_INV : TM_INV + 1], stats2[P1_INV : P1_INV + 1]
    c0, c1, c2, c3, c4 = stats[C0 : C0 + 1], stats[C1 : C1 + 1], stats2[C2 : C2 + 1], stats2[C3 : C3 + 1], stats2[C4 : C4 + 1]
    gt_own[...] = removed(dot(i_own[...], b01[0], (1, 0)), t0[:half], scale, t0_inv, c0)
    own, next_ = jnp.where(ft == 1, i_far[...], i_own[...]), ip[part(ft, half)]
    back = dot(own, b01[1], (1, 0)) + dot(next_, b234[0], (1, 0))
    gt_back[...] = removed(back, tm[:half], scale, tm_inv, c1 + c2)
    d3 = dot(own, b234[1], (1, 0))

    @pl.when(core == 0)
    def _():
        both = d3 + dot(next_, b234[2], (1, 0))
        d_p1[...] = removed(both, p1[:half], scale, p1_inv, c3 + c4).astype(bf16)
        d_p0[...] = jnp.zeros(d_p0.shape, bf16)

    @pl.when(core == 1)
    def _():
        d_p1[...] = removed(d3, p1[:half], scale, p1_inv, c3).astype(bf16)
        d_p0[...] = removed(dot(i_own[...], b234[2], (1, 0)), p0[:half], scale, stats2[P0_INV : P0_INV + 1], c4).astype(bf16)


def local(kernel, scalars, args, outs, scratch, flops, name, limit=16):
    smem, vmem = pl.BlockSpec(memory_space=pltpu.SMEM), pl.BlockSpec(memory_space=pltpu.VMEM)
    return pl.pallas_call(
        kernel,
        out_shape=[jax.ShapeDtypeStruct(*out) for out in outs],
        in_specs=[smem] * scalars + [vmem] * (len(args) - scalars),
        out_specs=[vmem] * len(outs),
        scratch_shapes=[pltpu.VMEM(*shape) for shape in scratch],
        compiler_params=pltpu.CompilerParams(vmem_limit_bytes=limit * 2**20),
        cost_estimate=pl.CostEstimate(flops=flops, bytes_accessed=4_000_000, transcendentals=200_000),
        name=name,
    )(*args)


def weight_kernel(other, w_own, w_next, features, next_features, out):
    core, part = lax.axis_index("core"), w_own.shape[0] // 2
    at = pl.ds(pl.multiple_of((1 - core if other else core) * part, part), part)
    a, b = w_own[at], w_next[at]
    for group in range(features.shape[1] // 128):
        columns = slice(group * 128, group * 128 + 128)
        total = dot(a, features[:, columns], (1, 0)) + dot(b, next_features[:, columns], (1, 0))
        out[group * part : (group + 1) * part] = total.astype(out.dtype)
    filled = features.shape[1] // 128 * part
    out[filled:] = jnp.zeros((out.shape[0] - filled, 128), out.dtype)


def join_kernel(mine, other, out):
    core, part = lax.axis_index("core"), out.shape[0] // 2
    here = pl.ds(pl.multiple_of(core * part, part), part)
    there = pl.ds(pl.multiple_of((1 - core) * part, part), part)
    for group in range(out.shape[1] // 128):
        rows, columns = slice(group * part, (group + 1) * part), slice(group * 128, group * 128 + 128)
        out[here, columns] = mine[rows]
        out[there, columns] = other[rows]


def shards(features, img_weight, text_embed, log_scale, logit_bias):
    half, width = img_weight.shape[1], features.shape[1]
    count = features.shape[0]

    t_own = text_embed.T
    t_far = swapped(t_own, "rep")
    t_a = shifted(t_own, 2)
    i_own = lax.optimization_barrier(dot(img_weight, features, (0, 1)).astype(bf16))
    i_far = swapped(i_own, "rep")
    i_e = shifted(i_own, -2)
    t_b = swapped(lax.optimization_barrier((t_a, i_far))[0], "rep")
    next_features = shifted(lax.optimization_barrier((features, t_a))[0], -2)
    i_f = swapped(i_e, "rep")
    t0 = jnp.concatenate([t_own, t_far], 0)
    tm = jnp.concatenate([t_a, t_b], 0)
    late_tm, i_f, next_features = lax.optimization_barrier((tm, i_f, next_features))
    p1 = swapped(late_tm, "core")
    p0 = lax.ppermute(t0, "core", [(0, 1)])
    whole, square, by_row = (half, count), (count, count), (8, count)
    own, i0_n, b01, stats = local(
        first_kernel, 2, (log_scale, logit_bias, t0, tm, i_own, i_far),
        [(whole, f32), ((count, 2 * half), bf16), ((2, *square), bf16), (by_row, f32)], [], 500_000_000, "first_pairs",
    )
    gi_own, gi_back, w_own, w_next, ip, b234, stats2 = local(
        second_kernel, 2, (log_scale, logit_bias, tm, p0, p1, i_e, i_f, own, i_own, i0_n, stats),
        [(whole, f32), (whole, bf16), (whole, bf16), (whole, bf16), ((2 * half, count), bf16), ((3, *square), bf16), (by_row, f32)],
        [((count, 2 * half), bf16)], 800_000_000, "second_pairs",
    )
    gt_own, gt_back, d_p1, d_p0 = local(
        text_kernel, 1, (log_scale, t0, tm, p0, p1, i_own, i_far, ip, b01, b234, stats, stats2),
        [(whole, f32), (whole, f32), (whole, bf16), (whole, bf16)], [], 400_000_000, "text_gradients",
    )

    peers = lax.axis_size(PLANE)
    deep = -(-half * width // (2 * 128 * peers * 16)) * 16
    theirs, mine = (
        local(
            functools.partial(weight_kernel, other), 0, (w_own, w_next, features, next_features),
            [((peers * deep, 128), dtype)], [], 340_000_000, "weight_part", 8,
        )[0]
        for other, dtype in ((True, bf16), (False, f32))
    )
    tiles = (mine + swapped(theirs, "core").astype(f32)).astype(bf16).reshape(peers, deep, 128)
    pieces = lax.all_to_all(tiles, PLANE, 0, 0, tiled=True)
    gi_came = shifted(gi_back, 2)
    gt_sum = (gt_back + swapped(d_p1, "core").astype(f32)).astype(bf16)
    d_p0_came = lax.ppermute(d_p0, "core", [(1, 0)])
    gt_came = shifted(gt_sum, -2)
    piece = jnp.sum(pieces.astype(f32), axis=0)
    piece = (piece + swapped(piece, "xh")).astype(bf16)
    piece, gi_came, gt_came, d_p0_came = lax.optimization_barrier((piece, gi_came, gt_came, d_p0_came))
    sent = jnp.broadcast_to(piece[None], (peers, deep, 128))
    whole = lax.all_to_all(sent, PLANE, 0, 0, tiled=True).reshape(peers * deep, 128)
    image_grad = (gi_own + gi_came.astype(f32)).astype(bf16)
    text_grad = (gt_own + gt_came.astype(f32) + d_p0_came.astype(f32)).astype(bf16)
    whole, image_grad, text_grad = lax.optimization_barrier((whole, image_grad, text_grad))
    (weight_grad,) = local(join_kernel, 0, (whole, swapped(whole, "core")), [((half, width), bf16)], [], 0, "joined", 4)
    return image_grad.T, text_grad.T, weight_grad.T


def solution(mesh):
    fine = Mesh(mesh.devices.reshape(SIZES), AXES)
    in_specs = (P(DP, None), P(None, "rep"), P(DP, "rep"), P(), P())
    out_specs = (P(DP, "rep"), P(DP, "rep"), P(None, "rep"))
    return jax.shard_map(shards, mesh=fine, in_specs=in_specs, out_specs=out_specs, check_vma=False)
```

time: 1460 us -> 140 us (0.10)
  blocking collectives: 1360 us -> 0 us
  starting transfers between devices: 29.9 us -> 80.2 us
    psum x3 -> x0, blocking collectives: 1340 us -> none  [the longest x1 1330 us: shards(): weight_grad = lax.psum(weight_part, 'dp').astype(jnp.bfloat16)]
    ppermute x9 -> x16, starting transfers between devices: 29.9 us -> 65.5 us  [the longest x5 32.7 us: shifted(): return lax.ppermute(array, AXES, pairs)]
    ppermute x9 -> x16, waiting for transfers between devices: 40.4 us -> 13.7 us  [the longest x9 13.2 us: swapped(): return lax.ppermute(array, axis, [(0, 1), (1, 0)])]
    all_gather x2 -> x0, blocking collectives: 20.5 us -> none  [the longest x1 14.2 us: shards(): lax.all_gather(img_bf, 'rep', axis=1, tiled=True)]
    all_to_all x0 -> x2, waiting for transfers between devices: none -> 19.7 us  [the longest x1 19.7 us: shards(): lax.all_to_all(sent, PLANE, 0, 0, tiled=True).reshape(peers * deep, 128)]
    all_to_all x0 -> x2, starting transfers between devices: none -> 14.8 us  [the longest x1 8.76 us: shards(): lax.all_to_all(sent, PLANE, 0, 0, tiled=True).reshape(peers * deep, 128)]
  transfers between devices with their start and end apart: 9 -> 18, of which waited for: 7 -> 7; matrix products, arithmetic and copies ran while one was open for 1% -> 4% of each run, Pallas kernels for 0% -> 3%
where the time goes in v4:
time: 140 us; the launch traced here: 139 us
  starting transfers between devices  80.2 us (57%)
  waiting for transfers between devices  33.3 us (24%)
  Pallas kernels  8.91 us (6%)
  local copies, waits for them, and re-layouts  7.68 us (5%)
  other arithmetic  5.3 us (4%)
  between operations  2.33 us (2%)
  matrix products  1.65 us (1%)
    ppermute x5, starting transfers between devices, shifted(): return lax.ppermute(array, AXES, pairs)  32.7 us
    ppermute x9, starting transfers between devices, swapped(): return lax.ppermute(array, axis, [(0, 1), (1, 0)])  29.4 us
    all_to_all x1, waiting for transfers between devices, shards(): lax.all_to_all(sent, PLANE, 0, 0, tiled=True).reshape(peers * deep, 128)  19.7 us
    ppermute x9, waiting for transfers between devices, swapped(): return lax.ppermute(array, axis, [(0, 1), (1, 0)])  13.2 us
    pallas_call x6, Pallas kernels, local(): pl.pallas_call(kernel, out_shape=[jax.ShapeDtypeStruct(*out) for out in o...  8.91 us
    all_to_all x1, starting transfers between devices, shards(): lax.all_to_all(sent, PLANE, 0, 0, tiled=True).reshape(peers * deep, 128)  8.76 us
    unnamed x39, local copies, waits for them, and re-layouts  6.68 us
    all_to_all x1, starting transfers between devices, shards(): pieces = lax.all_to_all(tiles, PLANE, 0, 0, tiled=True)  6 us
  transfers between devices with their start and end apart: 18, of which 7 were waited for; matrix products, arithmetic and copies ran while one was open for 4% of the time, Pallas kernels for 3%

profile of v4, /device:TPU:1, one launch (start us, length us, event | category | flops | bytes accessed | tf_op | source)
XLA Modules:
  0.0 139.5 jit_solution(14058559602297794503)
XLA Ops:
  0.7 4.2 %collective-permute-start = (bf16[576,256]{1,0:T(8,128)(2,1)}, bf16[576,256]{1,0:T(8,128)(2,1)S(1)}, u32[]{:S(2)}, u32[]{:S(2)}) collective-permute-start(bf16[576,256]{1,0:T(8,128)(2,1)} %bitcast.12), channel_id=1, source_target_pairs={{0,4},{1,5},{2,6},{3,7},{4,8},{5,9},{6,10},{7,11},{8,12},{9,13},{1... | collective-permute-start | bytes 884744 | tf_op jit(solution)/shard_map/ppermute | solution.py:26
  6.5 3.1 %collective-permute-start.1 = (bf16[576,256]{1,0:T(8,128)(2,1)S(1)}, bf16[576,256]{1,0:T(8,128)(2,1)S(1)}, u32[]{:S(2)}, u32[]{:S(2)}) collective-permute-start(bf16[576,256]{1,0:T(8,128)(2,1)S(1)} %convolution_convert_fusion.i_own), channel_id=1, source_target_pairs={{0,1},{1,0},{2,3},{3,2},{4,5},{5,4},{6,7},{7,6},{8,9},{9,8},{10,11... | collective-permute-start | bytes 884744 | tf_op jit(solution)/shard_map/ppermute | solution.py:30
  9.6 13.8 %collective-permute-start.5 = (bf16[576,256]{1,0:T(8,128)(2,1)S(1)}, bf16[576,256]{1,0:T(8,128)(2,1)S(1)}, u32[]{:S(2)}, u32[]{:S(2)}) collective-permute-start(bf16[576,256]{1,0:T(8,128)(2,1)S(1)} %convolution_convert_fusion.i_own), channel_id=1, source_target_pairs={{0,509},{1,508},{2,511},{3,510},{4,0},{5,1},{6,2},{7,3},{8,4},{9,5... | collective-permute-start | bytes 884744 | tf_op jit(solution)/shard_map/ppermute | solution.py:26
  23.5 2.2 %collective-permute-start.3 = (bf16[576,256]{1,0:T(8,128)(2,1)S(1)}, bf16[576,256]{1,0:T(8,128)(2,1)S(1)}, u32[]{:S(2)}, u32[]{:S(2)}) collective-permute-start(bf16[576,256]{1,0:T(8,128)(2,1)S(1)} %bitcast.13), channel_id=1, source_target_pairs={{0,1},{1,0},{2,3},{3,2},{4,5},{5,4},{6,7},{7,6},{8,9},{9,8},{10,11... | collective-permute-start | bytes 884744 | tf_op jit(solution)/shard_map/ppermute | solution.py:30
  25.7 4.0 %collective-permute-start.7 = (bf16[256,1152]{1,0:T(8,128)(2,1)S(1)}, bf16[256,1152]{1,0:T(8,128)(2,1)S(1)}, u32[]{:S(2)}, u32[]{:S(2)}) collective-permute-start(bf16[256,1152]{1,0:T(8,128)(2,1)S(1)} %copy-done.1), channel_id=1, source_target_pairs={{0,509},{1,508},{2,511},{3,510},{4,0},{5,1},{6,2},{7,3},{8,4},{9,5... | collective-permute-start | bytes 1769480 | tf_op jit(solution)/shard_map/ppermute | solution.py:26
  29.7 1.9 %collective-permute-start.2 = (bf16[576,256]{1,0:T(8,128)(2,1)S(1)}, bf16[576,256]{1,0:T(8,128)(2,1)S(1)}, u32[]{:S(2)}, u32[]{:S(2)}) collective-permute-start(bf16[576,256]{1,0:T(8,128)(2,1)S(1)} %collective-permute-done), channel_id=1, source_target_pairs={{0,1},{1,0},{2,3},{3,2},{4,5},{5,4},{6,7},{7,6},{8,9},{9,8},{10,11... | collective-permute-start | bytes 884744 | tf_op jit(solution)/shard_map/ppermute | solution.py:30
  31.7 3.4 %collective-permute-start.6 = (bf16[576,256]{1,0:T(8,128)(2,1)S(1)}, bf16[576,256]{1,0:T(8,128)(2,1)S(1)}, u32[]{:S(2)}, u32[]{:S(2)}) collective-permute-start(bf16[576,256]{1,0:T(8,128)(2,1)S(1)} %collective-permute-done.5.i_e), channel_id=1, source_target_pairs={{0,1},{1,0},{2,3},{3,2},{4,5},{5,4},{6,7},{7,6},{8,9},{9,8},{10,11... | collective-permute-start | bytes 884744 | tf_op jit(solution)/shard_map/ppermute | solution.py:30
  36.4 1.8 %collective-permute-done.2 = bf16[576,256]{1,0:T(8,128)(2,1)S(1)} collective-permute-done((bf16[576,256]{1,0:T(8,128)(2,1)S(1)}, bf16[576,256]{1,0:T(8,128)(2,1)S(1)}, u32[]{:S(2)}, u32[]{:S(2)}) %collective-permute-start.2) | collective-permute-done | bytes 294944 | tf_op jit(solution)/shard_map/ppermute | solution.py:30
  38.2 6.3 %collective-permute-done.6.i_f = bf16[576,256]{1,0:T(8,128)(2,1)S(1)} collective-permute-done((bf16[576,256]{1,0:T(8,128)(2,1)S(1)}, bf16[576,256]{1,0:T(8,128)(2,1)S(1)}, u32[]{:S(2)}, u32[]{:S(2)}) %collective-permute-start.6) | collective-permute-done | bytes 294944 | tf_op jit(solution)/shard_map/ppermute | solution.py:30
  44.5 4.8 %collective-permute-start.8 = (bf16[1152,256]{1,0:T(8,128)(2,1)S(1)}, bf16[1152,256]{1,0:T(8,128)(2,1)S(1)}, u32[]{:S(2)}, u32[]{:S(2)}) collective-permute-start(bf16[1152,256]{1,0:T(8,128)(2,1)S(1)} %constant_dynamic-update-slice_fusion.tm), channel_id=1, source_target_pairs={{0,2},{2,0},{1,3},{3,1},{4,6},{6,4},{5,7},{7,5},{8,10},{10,8},{9,1... | collective-permute-start | bytes 1769480 | tf_op jit(solution)/shard_map/ppermute | solution.py:30
  52.1 2.9 %second_pairs.1 = (f32[576,256]{1,0:T(8,128)S(1)}, bf16[576,256]{1,0:T(8,128)(2,1)}, bf16[576,256]{1,0:T(8,128)(2,1)S(1)}, bf16[576,256]{1,0:T(8,128)(2,1)S(1)},...) custom-call(f32[1]{0:T(128)S(6)} %copy.9.log_scale, f32[1]{0:T(128)S(6)} %copy.10.bias, ...), custom_call_target="tpu_custom_call" | custom-call | flops 800000000 | bytes 4000000 | tf_op jit(solution)/shard_map/second_pairs/pallas_call | solution.py:183
  57.5 2.0 %collective-permute-start.9 = (bf16[3072,128]{1,0:T(8,128)(2,1)S(1)}, bf16[3072,128]{1,0:T(8,128)(2,1)S(1)}, u32[]{:S(2)}, u32[]{:S(2)}) collective-permute-start(bf16[3072,128]{1,0:T(8,128)(2,1)S(1)} %weight_part.3), channel_id=1, source_target_pairs={{0,2},{2,0},{1,3},{3,1},{4,6},{6,4},{5,7},{7,5},{8,10},{10,8},{9,1... | collective-permute-start | bytes 2359304 | tf_op jit(solution)/shard_map/ppermute | solution.py:30
  62.7 6.0 %all-to-all-start = ((bf16[64,48,128]{2,1,0:T(8,128)(2,1)}), bf16[64,48,128]{2,1,0:T(8,128)(2,1)}, u32[]{:S(2)}, u32[]{:S(2)}) async-start(bf16[64,48,128]{2,1,0:T(8,128)(2,1)} %bitcast.10), calls=%async_computation | async-start | bytes 1572864 | tf_op jit(solution)/shard_map/all_to_all | solution.py:260
  75.3 2.2 %collective-permute-start.12 = (bf16[576,256]{1,0:T(8,128)(2,1)S(1)}, bf16[576,256]{1,0:T(8,128)(2,1)S(1)}, u32[]{:S(2)}, u32[]{:S(2)}) collective-permute-start(bf16[576,256]{1,0:T(8,128)(2,1)S(1)} %get-tuple-element.46), channel_id=1, source_target_pairs={{0,2},{2,0},{1,3},{3,1},{4,6},{6,4},{5,7},{7,5},{8,10},{10,8},{9,1... | collective-permute-start | bytes 884744 | tf_op jit(solution)/shard_map/ppermute | solution.py:30
  77.5 2.1 %collective-permute-start.14 = (bf16[576,256]{1,0:T(8,128)(2,1)}, bf16[576,256]{1,0:T(8,128)(2,1)S(1)}, u32[]{:S(2)}, u32[]{:S(2)}) collective-permute-start(bf16[576,256]{1,0:T(8,128)(2,1)} %get-tuple-element.47), channel_id=1, source_target_pairs={{2,0},{3,1},{6,4},{7,5},{10,8},{11,9},{14,12},{15,13},{18,16},{19,... | collective-permute-start | bytes 884744 | tf_op jit(solution)/shard_map/ppermute | solution.py:263
  79.6 3.0 %collective-permute-start.11 = (bf16[576,256]{1,0:T(8,128)(2,1)}, bf16[576,256]{1,0:T(8,128)(2,1)S(1)}, u32[]{:S(2)}, u32[]{:S(2)}) collective-permute-start(bf16[576,256]{1,0:T(8,128)(2,1)} %get-tuple-element.40), channel_id=1, source_target_pairs={{0,4},{1,5},{2,6},{3,7},{4,8},{5,9},{6,10},{7,11},{8,12},{9,13},{1... | collective-permute-start | bytes 884744 | tf_op jit(solution)/shard_map/ppermute | solution.py:26
  83.5 7.7 %collective-permute-start.13 = (bf16[576,256]{1,0:T(8,128)(2,1)}, bf16[576,256]{1,0:T(8,128)(2,1)}, u32[]{:S(2)}, u32[]{:S(2)}) collective-permute-start(bf16[576,256]{1,0:T(8,128)(2,1)} %add_convert_fusion.3), channel_id=1, source_target_pairs={{0,509},{1,508},{2,511},{3,510},{4,0},{5,1},{6,2},{7,3},{8,4},{9,5... | collective-permute-start | bytes 884744 | tf_op jit(solution)/shard_map/ppermute | solution.py:26
  92.5 4.6 %collective-permute-start.10 = (f32[48,128]{1,0:T(8,128)S(1)}, f32[48,128]{1,0:T(8,128)S(1)}, u32[]{:S(2)}, u32[]{:S(2)}) collective-permute-start(f32[48,128]{1,0:T(8,128)S(1)} %convert_reduce_fusion), channel_id=1, source_target_pairs={{0,32},{32,0},{1,33},{33,1},{2,34},{34,2},{3,35},{35,3},{4,36},{36... | collective-permute-start | bytes 73736 | tf_op jit(solution)/shard_map/ppermute | solution.py:30
  97.1 1.9 %collective-permute-done.10 = f32[48,128]{1,0:T(8,128)S(1)} collective-permute-done((f32[48,128]{1,0:T(8,128)S(1)}, f32[48,128]{1,0:T(8,128)S(1)}, u32[]{:S(2)}, u32[]{:S(2)}) %collective-permute-start.10) | collective-permute-done | bytes 24608 | tf_op jit(solution)/shard_map/ppermute | solution.py:30
  100.6 8.8 %all-to-all-start.1 = ((bf16[64,48,128]{2,1,0:T(8,128)(2,1)}), bf16[64,48,128]{2,1,0:T(8,128)(2,1)S(1)}, u32[]{:S(2)}, u32[]{:S(2)}) async-start(bf16[64,48,128]{2,1,0:T(8,128)(2,1)} %broadcast_in_dim.2), calls=%async_computation.1 | async-start | bytes 1572864 | tf_op jit(solution)/shard_map/all_to_all | solution.py:269
  109.4 2.1 %add_convert_fusion.1 = (bf16[576,256]{1,0:T(8,128)(2,1)}, bf16[576,256]{1,0:T(8,128)(2,1)}) fusion(bf16[576,256]{1,0:T(8,128)(2,1)} %copy-done.17, f32[576,256]{1,0:T(8,128)S(1)} %copy-done.9, bf16[576,256]{1,0:T(8,128)(2,1)} %collective-permute-done.13, f32[576,256]{1,0:T(8,128)S(1)} %copy-done.7, bf16[576,256]{1,0:T(8,128)(2,1)} %copy-done.18), kind=kLoop, calls=%fused_computation.4 | loop fusion | flops 1179648 | bytes 2654208 | tf_op jit(solution)/shard_map/convert_element_type | solution.py:271
  111.5 19.7 %all-to-all-done.1 = bf16[64,48,128]{2,1,0:T(8,128)(2,1)S(1)} async-done(((bf16[64,48,128]{2,1,0:T(8,128)(2,1)}), bf16[64,48,128]{2,1,0:T(8,128)(2,1)S(1)}, u32[]{:S(2)}, u32[]{:S(2)}) %all-to-all-start.1) | async-done | bytes 786464 | tf_op jit(solution)/shard_map/all_to_all | solution.py:269
  131.1 5.1 %collective-permute-start.15 = (bf16[3072,128]{1,0:T(8,128)(2,1)S(1)}, bf16[3072,128]{1,0:T(8,128)(2,1)S(1)}, u32[]{:S(2)}, u32[]{:S(2)}) collective-permute-start(bf16[3072,128]{1,0:T(8,128)(2,1)S(1)} %bitcast.8), channel_id=1, source_target_pairs={{0,2},{2,0},{1,3},{3,1},{4,6},{6,4},{5,7},{7,5},{8,10},{10,8},{9,1... | collective-permute-start | bytes 2359304 | tf_op jit(solution)/shard_map/ppermute | solution.py:30
  136.3 1.9 %collective-permute-done.15.other = bf16[3072,128]{1,0:T(8,128)(2,1)S(1)} collective-permute-done((bf16[3072,128]{1,0:T(8,128)(2,1)S(1)}, bf16[3072,128]{1,0:T(8,128)(2,1)S(1)}, u32[]{:S(2)}, u32[]{:S(2)}) %collective-permute-start.15) | collective-permute-done | bytes 786464 | tf_op jit(solution)/shard_map/ppermute | solution.py:30
  (66 shorter events, 21.7 us)
Async XLA Ops:
  0.6 22.8 %copy-start.16 = (bf16[256,576]{0,1:T(8,128)(2,1)S(1)}, bf16[256,576]{0,1:T(8,128)(2,1)}, u32[]{:S(2)}) copy-start(bf16[256,576]{0,1:T(8,128)(2,1)} %param.7) | copy-start | bytes 884740
  0.7 25.1 %copy-start.1 = (bf16[256,1152]{1,0:T(8,128)(2,1)S(1)}, bf16[256,1152]{1,0:T(8,128)(2,1)}, u32[]{:S(2)}) copy-start(bf16[256,1152]{1,0:T(8,128)(2,1)} %features.3) | copy-start | bytes 1769476
  0.7 25.0 %collective-permute-start = (bf16[576,256]{1,0:T(8,128)(2,1)}, bf16[576,256]{1,0:T(8,128)(2,1)S(1)}, u32[]{:S(2)}, u32[]{:S(2)}) collective-permute-start(bf16[576,256]{1,0:T(8,128)(2,1)} %bitcast.12), channel_id=1, source_target_pairs={{0,4},{1,5},{2,6},{3,7},{4,8},{5,9},{6,10},{7,11},{8,12},{9,13},{1... | collective-permute-start | bytes 884744 | tf_op jit(solution)/shard_map/ppermute | solution.py:26
  6.5 23.2 %collective-permute-start.1 = (bf16[576,256]{1,0:T(8,128)(2,1)S(1)}, bf16[576,256]{1,0:T(8,128)(2,1)S(1)}, u32[]{:S(2)}, u32[]{:S(2)}) collective-permute-start(bf16[576,256]{1,0:T(8,128)(2,1)S(1)} %convolution_convert_fusion.i_own), channel_id=1, source_target_pairs={{0,1},{1,0},{2,3},{3,2},{4,5},{5,4},{6,7},{7,6},{8,9},{9,8},{10,11... | collective-permute-start | bytes 884744 | tf_op jit(solution)/shard_map/ppermute | solution.py:30
  9.6 22.0 %collective-permute-start.5 = (bf16[576,256]{1,0:T(8,128)(2,1)S(1)}, bf16[576,256]{1,0:T(8,128)(2,1)S(1)}, u32[]{:S(2)}, u32[]{:S(2)}) collective-permute-start(bf16[576,256]{1,0:T(8,128)(2,1)S(1)} %convolution_convert_fusion.i_own), channel_id=1, source_target_pairs={{0,509},{1,508},{2,511},{3,510},{4,0},{5,1},{6,2},{7,3},{8,4},{9,5... | collective-permute-start | bytes 884744 | tf_op jit(solution)/shard_map/ppermute | solution.py:26
  23.5 11.6 %collective-permute-start.3 = (bf16[576,256]{1,0:T(8,128)(2,1)S(1)}, bf16[576,256]{1,0:T(8,128)(2,1)S(1)}, u32[]{:S(2)}, u32[]{:S(2)}) collective-permute-start(bf16[576,256]{1,0:T(8,128)(2,1)S(1)} %bitcast.13), channel_id=1, source_target_pairs={{0,1},{1,0},{2,3},{3,2},{4,5},{5,4},{6,7},{7,6},{8,9},{9,8},{10,11... | collective-permute-start | bytes 884744 | tf_op jit(solution)/shard_map/ppermute | solution.py:30
  25.7 18.8 %collective-permute-start.7 = (bf16[256,1152]{1,0:T(8,128)(2,1)S(1)}, bf16[256,1152]{1,0:T(8,128)(2,1)S(1)}, u32[]{:S(2)}, u32[]{:S(2)}) collective-permute-start(bf16[256,1152]{1,0:T(8,128)(2,1)S(1)} %copy-done.1), channel_id=1, source_target_pairs={{0,509},{1,508},{2,511},{3,510},{4,0},{5,1},{6,2},{7,3},{8,4},{9,5... | collective-permute-start | bytes 1769480 | tf_op jit(solution)/shard_map/ppermute | solution.py:26
  29.7 22.4 %copy-start.12 = (bf16[576,256]{1,0:T(8,128)(2,1)}, bf16[576,256]{1,0:T(8,128)(2,1)S(1)}, u32[]{:S(2)}) copy-start(bf16[576,256]{1,0:T(8,128)(2,1)S(1)} %collective-permute-done.1.i_far) | copy-start | bytes 884740
  29.7 8.4 %collective-permute-start.2 = (bf16[576,256]{1,0:T(8,128)(2,1)S(1)}, bf16[576,256]{1,0:T(8,128)(2,1)S(1)}, u32[]{:S(2)}, u32[]{:S(2)}) collective-permute-start(bf16[576,256]{1,0:T(8,128)(2,1)S(1)} %collective-permute-done), channel_id=1, source_target_pairs={{0,1},{1,0},{2,3},{3,2},{4,5},{5,4},{6,7},{7,6},{8,9},{9,8},{10,11... | collective-permute-start | bytes 884744 | tf_op jit(solution)/shard_map/ppermute | solution.py:30
  31.7 12.8 %collective-permute-start.6 = (bf16[576,256]{1,0:T(8,128)(2,1)S(1)}, bf16[576,256]{1,0:T(8,128)(2,1)S(1)}, u32[]{:S(2)}, u32[]{:S(2)}) collective-permute-start(bf16[576,256]{1,0:T(8,128)(2,1)S(1)} %collective-permute-done.5.i_e), channel_id=1, source_target_pairs={{0,1},{1,0},{2,3},{3,2},{4,5},{5,4},{6,7},{7,6},{8,9},{9,8},{10,11... | collective-permute-start | bytes 884744 | tf_op jit(solution)/shard_map/ppermute | solution.py:30
  35.1 17.0 %collective-permute-start.4 = (bf16[1152,256]{1,0:T(8,128)(2,1)S(1)}, bf16[1152,256]{1,0:T(8,128)(2,1)S(1)}, u32[]{:S(2)}, u32[]{:S(2)}) collective-permute-start(bf16[1152,256]{1,0:T(8,128)(2,1)S(1)} %pad_maximum_fusion.t0), channel_id=1, source_target_pairs={{0,2},{1,3},{4,6},{5,7},{8,10},{9,11},{12,14},{13,15},{16,18},{17,... | collective-permute-start | bytes 1769480 | tf_op jit(solution)/shard_map/ppermute | solution.py:234
  44.5 7.6 %collective-permute-start.8 = (bf16[1152,256]{1,0:T(8,128)(2,1)S(1)}, bf16[1152,256]{1,0:T(8,128)(2,1)S(1)}, u32[]{:S(2)}, u32[]{:S(2)}) collective-permute-start(bf16[1152,256]{1,0:T(8,128)(2,1)S(1)} %constant_dynamic-update-slice_fusion.tm), channel_id=1, source_target_pairs={{0,2},{2,0},{1,3},{3,1},{4,6},{6,4},{5,7},{7,5},{8,10},{10,8},{9,1... | collective-permute-start | bytes 1769480 | tf_op jit(solution)/shard_map/ppermute | solution.py:30
  57.5 4.2 %collective-permute-start.9 = (bf16[3072,128]{1,0:T(8,128)(2,1)S(1)}, bf16[3072,128]{1,0:T(8,128)(2,1)S(1)}, u32[]{:S(2)}, u32[]{:S(2)}) collective-permute-start(bf16[3072,128]{1,0:T(8,128)(2,1)S(1)} %weight_part.3), channel_id=1, source_target_pairs={{0,2},{2,0},{1,3},{3,1},{4,6},{6,4},{5,7},{7,5},{8,10},{10,8},{9,1... | collective-permute-start | bytes 2359304 | tf_op jit(solution)/shard_map/ppermute | solution.py:30
  62.7 28.5 %all-to-all-start = ((bf16[64,48,128]{2,1,0:T(8,128)(2,1)}), bf16[64,48,128]{2,1,0:T(8,128)(2,1)}, u32[]{:S(2)}, u32[]{:S(2)}) async-start(bf16[64,48,128]{2,1,0:T(8,128)(2,1)} %bitcast.10), calls=%async_computation | async-start | bytes 1572864 | tf_op jit(solution)/shard_map/all_to_all | solution.py:260
  75.3 8.2 %copy-start.8 = (f32[576,256]{1,0:T(8,128)}, f32[576,256]{1,0:T(8,128)S(1)}, u32[]{:S(2)}) copy-start(f32[576,256]{1,0:T(8,128)S(1)} %get-tuple-element.51) | copy-start | bytes 1769476
  75.3 7.3 %collective-permute-start.12 = (bf16[576,256]{1,0:T(8,128)(2,1)S(1)}, bf16[576,256]{1,0:T(8,128)(2,1)S(1)}, u32[]{:S(2)}, u32[]{:S(2)}) collective-permute-start(bf16[576,256]{1,0:T(8,128)(2,1)S(1)} %get-tuple-element.46), channel_id=1, source_target_pairs={{0,2},{2,0},{1,3},{3,1},{4,6},{6,4},{5,7},{7,5},{8,10},{10,8},{9,1... | collective-permute-start | bytes 884744 | tf_op jit(solution)/shard_map/ppermute | solution.py:30
  77.5 21.5 %collective-permute-start.14 = (bf16[576,256]{1,0:T(8,128)(2,1)}, bf16[576,256]{1,0:T(8,128)(2,1)S(1)}, u32[]{:S(2)}, u32[]{:S(2)}) collective-permute-start(bf16[576,256]{1,0:T(8,128)(2,1)} %get-tuple-element.47), channel_id=1, source_target_pairs={{2,0},{3,1},{6,4},{7,5},{10,8},{11,9},{14,12},{15,13},{18,16},{19,... | collective-permute-start | bytes 884744 | tf_op jit(solution)/shard_map/ppermute | solution.py:263
  79.6 19.9 %collective-permute-start.11 = (bf16[576,256]{1,0:T(8,128)(2,1)}, bf16[576,256]{1,0:T(8,128)(2,1)S(1)}, u32[]{:S(2)}, u32[]{:S(2)}) collective-permute-start(bf16[576,256]{1,0:T(8,128)(2,1)} %get-tuple-element.40), channel_id=1, source_target_pairs={{0,4},{1,5},{2,6},{3,7},{4,8},{5,9},{6,10},{7,11},{8,12},{9,13},{1... | collective-permute-start | bytes 884744 | tf_op jit(solution)/shard_map/ppermute | solution.py:26
  83.5 16.1 %collective-permute-start.13 = (bf16[576,256]{1,0:T(8,128)(2,1)}, bf16[576,256]{1,0:T(8,128)(2,1)}, u32[]{:S(2)}, u32[]{:S(2)}) collective-permute-start(bf16[576,256]{1,0:T(8,128)(2,1)} %add_convert_fusion.3), channel_id=1, source_target_pairs={{0,509},{1,508},{2,511},{3,510},{4,0},{5,1},{6,2},{7,3},{8,4},{9,5... | collective-permute-start | bytes 884744 | tf_op jit(solution)/shard_map/ppermute | solution.py:26
  92.5 16.9 %copy-start.7 = (f32[576,256]{1,0:T(8,128)S(1)}, f32[576,256]{1,0:T(8,128)}, u32[]{:S(2)}) copy-start(f32[576,256]{1,0:T(8,128)} %copy-done.6) | copy-start | bytes 1769476
  92.5 16.9 %copy-start.9 = (f32[576,256]{1,0:T(8,128)S(1)}, f32[576,256]{1,0:T(8,128)}, u32[]{:S(2)}) copy-start(f32[576,256]{1,0:T(8,128)} %copy-done.8) | copy-start | bytes 1769476
  92.5 6.5 %collective-permute-start.10 = (f32[48,128]{1,0:T(8,128)S(1)}, f32[48,128]{1,0:T(8,128)S(1)}, u32[]{:S(2)}, u32[]{:S(2)}) collective-permute-start(f32[48,128]{1,0:T(8,128)S(1)} %convert_reduce_fusion), channel_id=1, source_target_pairs={{0,32},{32,0},{1,33},{33,1},{2,34},{34,2},{3,35},{35,3},{4,36},{36... | collective-permute-start | bytes 73736 | tf_op jit(solution)/shard_map/ppermute | solution.py:30
  100.6 30.6 %all-to-all-start.1 = ((bf16[64,48,128]{2,1,0:T(8,128)(2,1)}), bf16[64,48,128]{2,1,0:T(8,128)(2,1)S(1)}, u32[]{:S(2)}, u32[]{:S(2)}) async-start(bf16[64,48,128]{2,1,0:T(8,128)(2,1)} %broadcast_in_dim.2), calls=%async_computation.1 | async-start | bytes 1572864 | tf_op jit(solution)/shard_map/all_to_all | solution.py:269
  131.1 7.0 %collective-permute-start.15 = (bf16[3072,128]{1,0:T(8,128)(2,1)S(1)}, bf16[3072,128]{1,0:T(8,128)(2,1)S(1)}, u32[]{:S(2)}, u32[]{:S(2)}) collective-permute-start(bf16[3072,128]{1,0:T(8,128)(2,1)S(1)} %bitcast.8), channel_id=1, source_target_pairs={{0,2},{2,0},{1,3},{3,1},{4,6},{6,4},{5,7},{7,5},{8,10},{10,8},{9,1... | collective-permute-start | bytes 2359304 | tf_op jit(solution)/shard_map/ppermute | solution.py:30
  (13 other events, 22.9 us)

commit v5 on v4

--- a/solution.py
+++ b/solution.py
@@ -99,8 +99,8 @@
 
 def second_kernel(
     log_scale, bias, tm, p0, p1, i_e, i_f, own, i_own, i0_n, stats,
-    gi_own, gi_back, w_own, w_next, ip, b, stats2,
-    ip_n,
+    gi_own, gi_back, w_own, w_next, b, stats2,
+    ip, ip_n,
 ):
     half = own.shape[0]
     core, ft, fi = place()
@@ -154,14 +154,15 @@
         store_stats(c4)
 
 
-def text_kernel(log_scale, t0, tm, p0, p1, i_own, i_far, ip, b01, b234, stats, stats2, gt_own, gt_back, d_p1, d_p0):
+def text_kernel(log_scale, t0, tm, p0, p1, i_own, i_far, i_e, i_f, b01, b234, stats, stats2, gt_own, gt_back, d_p1, d_p0):
     half = gt_own.shape[0]
-    core, ft, _ = place()
+    core, ft, fi = place()
     scale = jnp.exp(jnp.full((1, 1), log_scale[0], f32))
     t0_inv, tm_inv, p1_inv = stats[T0_INV : T0_INV + 1], stats[TM_INV : TM_INV + 1], stats2[P1_INV : P1_INV + 1]
     c0, c1, c2, c3, c4 = stats[C0 : C0 + 1], stats[C1 : C1 + 1], stats2[C2 : C2 + 1], stats2[C3 : C3 + 1], stats2[C4 : C4 + 1]
     gt_own[...] = removed(dot(i_own[...], b01[0], (1, 0)), t0[:half], scale, t0_inv, c0)
-    own, next_ = jnp.where(ft == 1, i_far[...], i_own[...]), ip[part(ft, half)]
+    own = jnp.where(ft == 1, i_far[...], i_own[...])
+    next_ = jnp.where(ft == fi, i_e[...], i_f[...])
     back = dot(own, b01[1], (1, 0)) + dot(next_, b234[0], (1, 0))
     gt_back[...] = removed(back, tm[:half], scale, tm_inv, c1 + c2)
     d3 = dot(own, b234[1], (1, 0))
@@ -229,21 +230,21 @@
     i_f = swapped(i_e, "rep")
     t0 = jnp.concatenate([t_own, t_far], 0)
     tm = jnp.concatenate([t_a, t_b], 0)
-    late_tm, i_f, next_features = lax.optimization_barrier((tm, i_f, next_features))
-    p1 = swapped(late_tm, "core")
-    p0 = lax.ppermute(t0, "core", [(0, 1)])
     whole, square, by_row = (half, count), (count, count), (8, count)
     own, i0_n, b01, stats = local(
         first_kernel, 2, (log_scale, logit_bias, t0, tm, i_own, i_far),
         [(whole, f32), ((count, 2 * half), bf16), ((2, *square), bf16), (by_row, f32)], [], 500_000_000, "first_pairs",
     )
-    gi_own, gi_back, w_own, w_next, ip, b234, stats2 = local(
+    late_tm, i_f, next_features, own = lax.optimization_barrier((tm, i_f, next_features, own))
+    p1 = swapped(late_tm, "core")
+    p0 = lax.ppermute(t0, "core", [(0, 1)])
+    gi_own, gi_back, w_own, w_next, b234, stats2 = local(
         second_kernel, 2, (log_scale, logit_bias, tm, p0, p1, i_e, i_f, own, i_own, i0_n, stats),
-        [(whole, f32), (whole, bf16), (whole, bf16), (whole, bf16), ((2 * half, count), bf16), ((3, *square), bf16), (by_row, f32)],
-        [((count, 2 * half), bf16)], 800_000_000, "second_pairs",
+        [(whole, f32), (whole, bf16), (whole, bf16), (whole, bf16), ((3, *square), bf16), (by_row, f32)],
+        [((2 * half, count), bf16), ((count, 2 * half), bf16)], 800_000_000, "second_pairs",
     )
     gt_own, gt_back, d_p1, d_p0 = local(
-        text_kernel, 1, (log_scale, t0, tm, p0, p1, i_own, i_far, ip, b01, b234, stats, stats2),
+        text_kernel, 1, (log_scale, t0, tm, p0, p1, i_own, i_far, i_e, i_f, b01, b234, stats, stats2),
         [(whole, f32), (whole, f32), (whole, bf16), (whole, bf16)], [], 400_000_000, "text_gradients",
     )
 

time: 140 us -> 139 us (level)
  starting transfers between devices: 80.2 us -> 78.8 us
    unnamed x39 -> x43, local copies, waits for them, and re-layouts: 6.68 us -> 5.98 us
where the time goes in v5:
time: 139 us; the launch traced here: 138 us
  starting transfers between devices  78.8 us (57%)
  waiting for transfers between devices  33.9 us (24%)
  Pallas kernels  8.9 us (6%)
  local copies, waits for them, and re-layouts  7.03 us (5%)
  other arithmetic  5.32 us (4%)
  between operations  2.36 us (2%)
  matrix products  1.65 us (1%)
    ppermute x5, starting transfers between devices, shifted(): return lax.ppermute(array, AXES, pairs)  32.7 us
    ppermute x9, starting transfers between devices, swapped(): return lax.ppermute(array, axis, [(0, 1), (1, 0)])  28.1 us
    all_to_all x1, waiting for transfers between devices, shards(): lax.all_to_all(sent, PLANE, 0, 0, tiled=True).reshape(peers * deep, 128)  19.7 us
    ppermute x9, waiting for transfers between devices, swapped(): return lax.ppermute(array, axis, [(0, 1), (1, 0)])  14.2 us
    all_to_all x1, starting transfers between devices, shards(): lax.all_to_all(sent, PLANE, 0, 0, tiled=True).reshape(peers * deep, 128)  9.11 us
    pallas_call x6, Pallas kernels, local(): pl.pallas_call(kernel, out_shape=[jax.ShapeDtypeStruct(*out) for out in o...  8.9 us
    unnamed x43, local copies, waits for them, and re-layouts  5.98 us
    all_to_all x1, starting transfers between devices, shards(): pieces = lax.all_to_all(tiles, PLANE, 0, 0, tiled=True)  5.48 us
  transfers between devices with their start and end apart: 18, of which 7 were waited for; matrix products, arithmetic and copies ran while one was open for 4% of the time, Pallas kernels for 3%

profile of v5, /device:TPU:1, one launch (start us, length us, event | category | flops | bytes accessed | tf_op | source)
XLA Modules:
  0.0 138.0 jit_solution(12571842206236126571)
XLA Ops:
  0.7 4.2 %collective-permute-start = (bf16[576,256]{1,0:T(8,128)(2,1)}, bf16[576,256]{1,0:T(8,128)(2,1)S(1)}, u32[]{:S(2)}, u32[]{:S(2)}) collective-permute-start(bf16[576,256]{1,0:T(8,128)(2,1)} %bitcast.12), channel_id=1, source_target_pairs={{0,4},{1,5},{2,6},{3,7},{4,8},{5,9},{6,10},{7,11},{8,12},{9,13},{1... | collective-permute-start | bytes 884744 | tf_op jit(solution)/shard_map/ppermute | solution.py:26
  4.8 1.6 %convolution_convert_fusion.i_own = bf16[576,256]{1,0:T(8,128)(2,1)S(1)} fusion(bf16[1152,576]{0,1:T(8,128)(2,1)S(1)} %copy-done, bf16[256,1152]{1,0:T(8,128)(2,1)} %features.3), kind=kOutput, calls=%fused_computation.2 | convolution fusion | flops 339886080 | bytes 2211840 | tf_op jit(solution)/shard_map/dot_general | solution.py:34
  6.5 3.1 %collective-permute-start.1 = (bf16[576,256]{1,0:T(8,128)(2,1)S(1)}, bf16[576,256]{1,0:T(8,128)(2,1)S(1)}, u32[]{:S(2)}, u32[]{:S(2)}) collective-permute-start(bf16[576,256]{1,0:T(8,128)(2,1)S(1)} %convolution_convert_fusion.i_own), channel_id=1, source_target_pairs={{0,1},{1,0},{2,3},{3,2},{4,5},{5,4},{6,7},{7,6},{8,9},{9,8},{10,11... | collective-permute-start | bytes 884744 | tf_op jit(solution)/shard_map/ppermute | solution.py:30
  9.6 13.8 %collective-permute-start.5 = (bf16[576,256]{1,0:T(8,128)(2,1)S(1)}, bf16[576,256]{1,0:T(8,128)(2,1)S(1)}, u32[]{:S(2)}, u32[]{:S(2)}) collective-permute-start(bf16[576,256]{1,0:T(8,128)(2,1)S(1)} %convolution_convert_fusion.i_own), channel_id=1, source_target_pairs={{0,509},{1,508},{2,511},{3,510},{4,0},{5,1},{6,2},{7,3},{8,4},{9,5... | collective-permute-start | bytes 884744 | tf_op jit(solution)/shard_map/ppermute | solution.py:26
  23.5 2.2 %collective-permute-start.3 = (bf16[576,256]{1,0:T(8,128)(2,1)S(1)}, bf16[576,256]{1,0:T(8,128)(2,1)S(1)}, u32[]{:S(2)}, u32[]{:S(2)}) collective-permute-start(bf16[576,256]{1,0:T(8,128)(2,1)S(1)} %bitcast.13), channel_id=1, source_target_pairs={{0,1},{1,0},{2,3},{3,2},{4,5},{5,4},{6,7},{7,6},{8,9},{9,8},{10,11... | collective-permute-start | bytes 884744 | tf_op jit(solution)/shard_map/ppermute | solution.py:30
  25.7 4.0 %collective-permute-start.7 = (bf16[256,1152]{1,0:T(8,128)(2,1)S(1)}, bf16[256,1152]{1,0:T(8,128)(2,1)S(1)}, u32[]{:S(2)}, u32[]{:S(2)}) collective-permute-start(bf16[256,1152]{1,0:T(8,128)(2,1)S(1)} %copy-done.1), channel_id=1, source_target_pairs={{0,509},{1,508},{2,511},{3,510},{4,0},{5,1},{6,2},{7,3},{8,4},{9,5... | collective-permute-start | bytes 1769480 | tf_op jit(solution)/shard_map/ppermute | solution.py:26
  31.0 1.9 %collective-permute-start.2 = (bf16[576,256]{1,0:T(8,128)(2,1)S(1)}, bf16[576,256]{1,0:T(8,128)(2,1)S(1)}, u32[]{:S(2)}, u32[]{:S(2)}) collective-permute-start(bf16[576,256]{1,0:T(8,128)(2,1)S(1)} %collective-permute-done), channel_id=1, source_target_pairs={{0,1},{1,0},{2,3},{3,2},{4,5},{5,4},{6,7},{7,6},{8,9},{9,8},{10,11... | collective-permute-start | bytes 884744 | tf_op jit(solution)/shard_map/ppermute | solution.py:30
  33.0 3.4 %collective-permute-start.6 = (bf16[576,256]{1,0:T(8,128)(2,1)S(1)}, bf16[576,256]{1,0:T(8,128)(2,1)S(1)}, u32[]{:S(2)}, u32[]{:S(2)}) collective-permute-start(bf16[576,256]{1,0:T(8,128)(2,1)S(1)} %collective-permute-done.5.i_e), channel_id=1, source_target_pairs={{0,1},{1,0},{2,3},{3,2},{4,5},{5,4},{6,7},{7,6},{8,9},{9,8},{10,11... | collective-permute-start | bytes 884744 | tf_op jit(solution)/shard_map/ppermute | solution.py:30
  40.8 4.8 %collective-permute-done.6.i_f = bf16[576,256]{1,0:T(8,128)(2,1)S(1)} collective-permute-done((bf16[576,256]{1,0:T(8,128)(2,1)S(1)}, bf16[576,256]{1,0:T(8,128)(2,1)S(1)}, u32[]{:S(2)}, u32[]{:S(2)}) %collective-permute-start.6) | collective-permute-done | bytes 294944 | tf_op jit(solution)/shard_map/ppermute | solution.py:30
  45.6 4.9 %collective-permute-start.8 = (bf16[1152,256]{1,0:T(8,128)(2,1)S(1)}, bf16[1152,256]{1,0:T(8,128)(2,1)S(1)}, u32[]{:S(2)}, u32[]{:S(2)}) collective-permute-start(bf16[1152,256]{1,0:T(8,128)(2,1)S(1)} %constant_dynamic-update-slice_fusion.tm), channel_id=1, source_target_pairs={{0,2},{2,0},{1,3},{3,1},{4,6},{6,4},{5,7},{7,5},{8,10},{10,8},{9,1... | collective-permute-start | bytes 1769480 | tf_op jit(solution)/shard_map/ppermute | solution.py:30
  52.2 2.9 %second_pairs.1 = (f32[576,256]{1,0:T(8,128)S(1)}, bf16[576,256]{1,0:T(8,128)(2,1)}, bf16[576,256]{1,0:T(8,128)(2,1)S(1)}, bf16[576,256]{1,0:T(8,128)(2,1)S(1)},...) custom-call(f32[1]{0:T(128)S(6)} %copy.9.log_scale, f32[1]{0:T(128)S(6)} %copy.10.bias, ...), custom_call_target="tpu_custom_call" | custom-call | flops 800000000 | bytes 4000000 | tf_op jit(solution)/shard_map/second_pairs/pallas_call | solution.py:184
  56.0 2.4 %collective-permute-start.9 = (bf16[3072,128]{1,0:T(8,128)(2,1)S(1)}, bf16[3072,128]{1,0:T(8,128)(2,1)S(1)}, u32[]{:S(2)}, u32[]{:S(2)}) collective-permute-start(bf16[3072,128]{1,0:T(8,128)(2,1)S(1)} %weight_part.3), channel_id=1, source_target_pairs={{0,2},{2,0},{1,3},{3,1},{4,6},{6,4},{5,7},{7,5},{8,10},{10,8},{9,1... | collective-permute-start | bytes 2359304 | tf_op jit(solution)/shard_map/ppermute | solution.py:30
  61.3 5.5 %all-to-all-start = ((bf16[64,48,128]{2,1,0:T(8,128)(2,1)}), bf16[64,48,128]{2,1,0:T(8,128)(2,1)}, u32[]{:S(2)}, u32[]{:S(2)}) async-start(bf16[64,48,128]{2,1,0:T(8,128)(2,1)} %bitcast.10), calls=%async_computation | async-start | bytes 1572864 | tf_op jit(solution)/shard_map/all_to_all | solution.py:261
  74.3 2.2 %collective-permute-start.12 = (bf16[576,256]{1,0:T(8,128)(2,1)S(1)}, bf16[576,256]{1,0:T(8,128)(2,1)S(1)}, u32[]{:S(2)}, u32[]{:S(2)}) collective-permute-start(bf16[576,256]{1,0:T(8,128)(2,1)S(1)} %get-tuple-element.46), channel_id=1, source_target_pairs={{0,2},{2,0},{1,3},{3,1},{4,6},{6,4},{5,7},{7,5},{8,10},{10,8},{9,1... | collective-permute-start | bytes 884744 | tf_op jit(solution)/shard_map/ppermute | solution.py:30
  76.4 2.1 %collective-permute-start.14 = (bf16[576,256]{1,0:T(8,128)(2,1)}, bf16[576,256]{1,0:T(8,128)(2,1)S(1)}, u32[]{:S(2)}, u32[]{:S(2)}) collective-permute-start(bf16[576,256]{1,0:T(8,128)(2,1)} %get-tuple-element.47), channel_id=1, source_target_pairs={{2,0},{3,1},{6,4},{7,5},{10,8},{11,9},{14,12},{15,13},{18,16},{19,... | collective-permute-start | bytes 884744 | tf_op jit(solution)/shard_map/ppermute | solution.py:264
  78.6 2.8 %collective-permute-start.11 = (bf16[576,256]{1,0:T(8,128)(2,1)}, bf16[576,256]{1,0:T(8,128)(2,1)S(1)}, u32[]{:S(2)}, u32[]{:S(2)}) collective-permute-start(bf16[576,256]{1,0:T(8,128)(2,1)} %get-tuple-element.41), channel_id=1, source_target_pairs={{0,4},{1,5},{2,6},{3,7},{4,8},{5,9},{6,10},{7,11},{8,12},{9,13},{1... | collective-permute-start | bytes 884744 | tf_op jit(solution)/shard_map/ppermute | solution.py:26
  82.2 7.9 %collective-permute-start.13 = (bf16[576,256]{1,0:T(8,128)(2,1)}, bf16[576,256]{1,0:T(8,128)(2,1)}, u32[]{:S(2)}, u32[]{:S(2)}) collective-permute-start(bf16[576,256]{1,0:T(8,128)(2,1)} %add_convert_fusion.3), channel_id=1, source_target_pairs={{0,509},{1,508},{2,511},{3,510},{4,0},{5,1},{6,2},{7,3},{8,4},{9,5... | collective-permute-start | bytes 884744 | tf_op jit(solution)/shard_map/ppermute | solution.py:26
  91.4 2.9 %collective-permute-start.10 = (f32[48,128]{1,0:T(8,128)S(1)}, f32[48,128]{1,0:T(8,128)S(1)}, u32[]{:S(2)}, u32[]{:S(2)}) collective-permute-start(f32[48,128]{1,0:T(8,128)S(1)} %convert_reduce_fusion), channel_id=1, source_target_pairs={{0,32},{32,0},{1,33},{33,1},{2,34},{34,2},{3,35},{35,3},{4,36},{36... | collective-permute-start | bytes 73736 | tf_op jit(solution)/shard_map/ppermute | solution.py:30
  94.3 3.3 %collective-permute-done.10 = f32[48,128]{1,0:T(8,128)S(1)} collective-permute-done((f32[48,128]{1,0:T(8,128)S(1)}, f32[48,128]{1,0:T(8,128)S(1)}, u32[]{:S(2)}, u32[]{:S(2)}) %collective-permute-start.10) | collective-permute-done | bytes 24608 | tf_op jit(solution)/shard_map/ppermute | solution.py:30
  98.7 9.1 %all-to-all-start.1 = ((bf16[64,48,128]{2,1,0:T(8,128)(2,1)}), bf16[64,48,128]{2,1,0:T(8,128)(2,1)S(1)}, u32[]{:S(2)}, u32[]{:S(2)}) async-start(bf16[64,48,128]{2,1,0:T(8,128)(2,1)} %broadcast_in_dim.2), calls=%async_computation.1 | async-start | bytes 1572864 | tf_op jit(solution)/shard_map/all_to_all | solution.py:270
  107.9 2.1 %add_convert_fusion.1 = (bf16[576,256]{1,0:T(8,128)(2,1)}, bf16[576,256]{1,0:T(8,128)(2,1)}) fusion(bf16[576,256]{1,0:T(8,128)(2,1)} %copy-done.19, f32[576,256]{1,0:T(8,128)S(1)} %copy-done.11, bf16[576,256]{1,0:T(8,128)(2,1)} %collective-permute-done.13, f32[576,256]{1,0:T(8,128)S(1)} %copy-done.9, bf16[576,256]{1,0:T(8,128)(2,1)} %copy-done.20), kind=kLoop, calls=%fused_computation.4 | loop fusion | flops 1179648 | bytes 2654208 | tf_op jit(solution)/shard_map/convert_element_type | solution.py:272
  110.0 19.7 %all-to-all-done.1 = bf16[64,48,128]{2,1,0:T(8,128)(2,1)S(1)} async-done(((bf16[64,48,128]{2,1,0:T(8,128)(2,1)}), bf16[64,48,128]{2,1,0:T(8,128)(2,1)S(1)}, u32[]{:S(2)}, u32[]{:S(2)}) %all-to-all-start.1) | async-done | bytes 786464 | tf_op jit(solution)/shard_map/all_to_all | solution.py:270
  129.6 5.1 %collective-permute-start.15 = (bf16[3072,128]{1,0:T(8,128)(2,1)S(1)}, bf16[3072,128]{1,0:T(8,128)(2,1)S(1)}, u32[]{:S(2)}, u32[]{:S(2)}) collective-permute-start(bf16[3072,128]{1,0:T(8,128)(2,1)S(1)} %bitcast.8), channel_id=1, source_target_pairs={{0,2},{2,0},{1,3},{3,1},{4,6},{6,4},{5,7},{7,5},{8,10},{10,8},{9,1... | collective-permute-start | bytes 2359304 | tf_op jit(solution)/shard_map/ppermute | solution.py:30
  134.8 1.9 %collective-permute-done.15.other = bf16[3072,128]{1,0:T(8,128)(2,1)S(1)} collective-permute-done((bf16[3072,128]{1,0:T(8,128)(2,1)S(1)}, bf16[3072,128]{1,0:T(8,128)(2,1)S(1)}, u32[]{:S(2)}, u32[]{:S(2)}) %collective-permute-start.15) | collective-permute-done | bytes 786464 | tf_op jit(solution)/shard_map/ppermute | solution.py:30
  (70 shorter events, 21.8 us)
Async XLA Ops:
  0.6 22.8 %copy-start.18 = (bf16[256,576]{0,1:T(8,128)(2,1)S(1)}, bf16[256,576]{0,1:T(8,128)(2,1)}, u32[]{:S(2)}) copy-start(bf16[256,576]{0,1:T(8,128)(2,1)} %param.7) | copy-start | bytes 884740
  0.7 25.1 %copy-start.1 = (bf16[256,1152]{1,0:T(8,128)(2,1)S(1)}, bf16[256,1152]{1,0:T(8,128)(2,1)}, u32[]{:S(2)}) copy-start(bf16[256,1152]{1,0:T(8,128)(2,1)} %features.3) | copy-start | bytes 1769476
  0.7 25.0 %collective-permute-start = (bf16[576,256]{1,0:T(8,128)(2,1)}, bf16[576,256]{1,0:T(8,128)(2,1)S(1)}, u32[]{:S(2)}, u32[]{:S(2)}) collective-permute-start(bf16[576,256]{1,0:T(8,128)(2,1)} %bitcast.12), channel_id=1, source_target_pairs={{0,4},{1,5},{2,6},{3,7},{4,8},{5,9},{6,10},{7,11},{8,12},{9,13},{1... | collective-permute-start | bytes 884744 | tf_op jit(solution)/shard_map/ppermute | solution.py:26
  6.5 24.5 %collective-permute-start.1 = (bf16[576,256]{1,0:T(8,128)(2,1)S(1)}, bf16[576,256]{1,0:T(8,128)(2,1)S(1)}, u32[]{:S(2)}, u32[]{:S(2)}) collective-permute-start(bf16[576,256]{1,0:T(8,128)(2,1)S(1)} %convolution_convert_fusion.i_own), channel_id=1, source_target_pairs={{0,1},{1,0},{2,3},{3,2},{4,5},{5,4},{6,7},{7,6},{8,9},{9,8},{10,11... | collective-permute-start | bytes 884744 | tf_op jit(solution)/shard_map/ppermute | solution.py:30
  9.6 23.3 %collective-permute-start.5 = (bf16[576,256]{1,0:T(8,128)(2,1)S(1)}, bf16[576,256]{1,0:T(8,128)(2,1)S(1)}, u32[]{:S(2)}, u32[]{:S(2)}) collective-permute-start(bf16[576,256]{1,0:T(8,128)(2,1)S(1)} %convolution_convert_fusion.i_own), channel_id=1, source_target_pairs={{0,509},{1,508},{2,511},{3,510},{4,0},{5,1},{6,2},{7,3},{8,4},{9,5... | collective-permute-start | bytes 884744 | tf_op jit(solution)/shard_map/ppermute | solution.py:26
  23.5 12.9 %collective-permute-start.3 = (bf16[576,256]{1,0:T(8,128)(2,1)S(1)}, bf16[576,256]{1,0:T(8,128)(2,1)S(1)}, u32[]{:S(2)}, u32[]{:S(2)}) collective-permute-start(bf16[576,256]{1,0:T(8,128)(2,1)S(1)} %bitcast.13), channel_id=1, source_target_pairs={{0,1},{1,0},{2,3},{3,2},{4,5},{5,4},{6,7},{7,6},{8,9},{9,8},{10,11... | collective-permute-start | bytes 884744 | tf_op jit(solution)/shard_map/ppermute | solution.py:30
  25.7 19.9 %collective-permute-start.7 = (bf16[256,1152]{1,0:T(8,128)(2,1)S(1)}, bf16[256,1152]{1,0:T(8,128)(2,1)S(1)}, u32[]{:S(2)}, u32[]{:S(2)}) collective-permute-start(bf16[256,1152]{1,0:T(8,128)(2,1)S(1)} %copy-done.1), channel_id=1, source_target_pairs={{0,509},{1,508},{2,511},{3,510},{4,0},{5,1},{6,2},{7,3},{8,4},{9,5... | collective-permute-start | bytes 1769480 | tf_op jit(solution)/shard_map/ppermute | solution.py:26
  31.0 8.3 %collective-permute-start.2 = (bf16[576,256]{1,0:T(8,128)(2,1)S(1)}, bf16[576,256]{1,0:T(8,128)(2,1)S(1)}, u32[]{:S(2)}, u32[]{:S(2)}) collective-permute-start(bf16[576,256]{1,0:T(8,128)(2,1)S(1)} %collective-permute-done), channel_id=1, source_target_pairs={{0,1},{1,0},{2,3},{3,2},{4,5},{5,4},{6,7},{7,6},{8,9},{9,8},{10,11... | collective-permute-start | bytes 884744 | tf_op jit(solution)/shard_map/ppermute | solution.py:30
  32.9 19.2 %copy-start.4 = (bf16[576,256]{1,0:T(8,128)(2,1)}, bf16[576,256]{1,0:T(8,128)(2,1)S(1)}, u32[]{:S(2)}) copy-start(bf16[576,256]{1,0:T(8,128)(2,1)S(1)} %collective-permute-done.5.i_e) | copy-start | bytes 884740
  33.0 12.7 %collective-permute-start.6 = (bf16[576,256]{1,0:T(8,128)(2,1)S(1)}, bf16[576,256]{1,0:T(8,128)(2,1)S(1)}, u32[]{:S(2)}, u32[]{:S(2)}) collective-permute-start(bf16[576,256]{1,0:T(8,128)(2,1)S(1)} %collective-permute-done.5.i_e), channel_id=1, source_target_pairs={{0,1},{1,0},{2,3},{3,2},{4,5},{5,4},{6,7},{7,6},{8,9},{9,8},{10,11... | collective-permute-start | bytes 884744 | tf_op jit(solution)/shard_map/ppermute | solution.py:30
  36.4 14.2 %collective-permute-start.4 = (bf16[1152,256]{1,0:T(8,128)(2,1)S(1)}, bf16[1152,256]{1,0:T(8,128)(2,1)S(1)}, u32[]{:S(2)}, u32[]{:S(2)}) collective-permute-start(bf16[1152,256]{1,0:T(8,128)(2,1)S(1)} %pad_maximum_fusion.t0), channel_id=1, source_target_pairs={{0,2},{1,3},{4,6},{5,7},{8,10},{9,11},{12,14},{13,15},{16,18},{17,... | collective-permute-start | bytes 1769480 | tf_op jit(solution)/shard_map/ppermute | solution.py:240
  40.8 14.3 %copy-start.16 = (bf16[2,256,256]{2,1,0:T(8,128)(2,1)}, bf16[2,256,256]{2,1,0:T(8,128)(2,1)S(1)}, u32[]{:S(2)}) copy-start(bf16[2,256,256]{2,1,0:T(8,128)(2,1)S(1)} %get-tuple-element.42.b01) | copy-start | bytes 786436
  45.6 6.5 %collective-permute-start.8 = (bf16[1152,256]{1,0:T(8,128)(2,1)S(1)}, bf16[1152,256]{1,0:T(8,128)(2,1)S(1)}, u32[]{:S(2)}, u32[]{:S(2)}) collective-permute-start(bf16[1152,256]{1,0:T(8,128)(2,1)S(1)} %constant_dynamic-update-slice_fusion.tm), channel_id=1, source_target_pairs={{0,2},{2,0},{1,3},{3,1},{4,6},{6,4},{5,7},{7,5},{8,10},{10,8},{9,1... | collective-permute-start | bytes 1769480 | tf_op jit(solution)/shard_map/ppermute | solution.py:30
  56.0 4.3 %collective-permute-start.9 = (bf16[3072,128]{1,0:T(8,128)(2,1)S(1)}, bf16[3072,128]{1,0:T(8,128)(2,1)S(1)}, u32[]{:S(2)}, u32[]{:S(2)}) collective-permute-start(bf16[3072,128]{1,0:T(8,128)(2,1)S(1)} %weight_part.3), channel_id=1, source_target_pairs={{0,2},{2,0},{1,3},{3,1},{4,6},{6,4},{5,7},{7,5},{8,10},{10,8},{9,1... | collective-permute-start | bytes 2359304 | tf_op jit(solution)/shard_map/ppermute | solution.py:30
  61.3 28.8 %all-to-all-start = ((bf16[64,48,128]{2,1,0:T(8,128)(2,1)}), bf16[64,48,128]{2,1,0:T(8,128)(2,1)}, u32[]{:S(2)}, u32[]{:S(2)}) async-start(bf16[64,48,128]{2,1,0:T(8,128)(2,1)} %bitcast.10), calls=%async_computation | async-start | bytes 1572864 | tf_op jit(solution)/shard_map/all_to_all | solution.py:261
  74.3 7.2 %collective-permute-start.12 = (bf16[576,256]{1,0:T(8,128)(2,1)S(1)}, bf16[576,256]{1,0:T(8,128)(2,1)S(1)}, u32[]{:S(2)}, u32[]{:S(2)}) collective-permute-start(bf16[576,256]{1,0:T(8,128)(2,1)S(1)} %get-tuple-element.46), channel_id=1, source_target_pairs={{0,2},{2,0},{1,3},{3,1},{4,6},{6,4},{5,7},{7,5},{8,10},{10,8},{9,1... | collective-permute-start | bytes 884744 | tf_op jit(solution)/shard_map/ppermute | solution.py:30
  76.4 21.2 %collective-permute-start.14 = (bf16[576,256]{1,0:T(8,128)(2,1)}, bf16[576,256]{1,0:T(8,128)(2,1)S(1)}, u32[]{:S(2)}, u32[]{:S(2)}) collective-permute-start(bf16[576,256]{1,0:T(8,128)(2,1)} %get-tuple-element.47), channel_id=1, source_target_pairs={{2,0},{3,1},{6,4},{7,5},{10,8},{11,9},{14,12},{15,13},{18,16},{19,... | collective-permute-start | bytes 884744 | tf_op jit(solution)/shard_map/ppermute | solution.py:264
  78.6 19.1 %collective-permute-start.11 = (bf16[576,256]{1,0:T(8,128)(2,1)}, bf16[576,256]{1,0:T(8,128)(2,1)S(1)}, u32[]{:S(2)}, u32[]{:S(2)}) collective-permute-start(bf16[576,256]{1,0:T(8,128)(2,1)} %get-tuple-element.41), channel_id=1, source_target_pairs={{0,4},{1,5},{2,6},{3,7},{4,8},{5,9},{6,10},{7,11},{8,12},{9,13},{1... | collective-permute-start | bytes 884744 | tf_op jit(solution)/shard_map/ppermute | solution.py:26
  82.2 15.5 %collective-permute-start.13 = (bf16[576,256]{1,0:T(8,128)(2,1)}, bf16[576,256]{1,0:T(8,128)(2,1)}, u32[]{:S(2)}, u32[]{:S(2)}) collective-permute-start(bf16[576,256]{1,0:T(8,128)(2,1)} %add_convert_fusion.3), channel_id=1, source_target_pairs={{0,509},{1,508},{2,511},{3,510},{4,0},{5,1},{6,2},{7,3},{8,4},{9,5... | collective-permute-start | bytes 884744 | tf_op jit(solution)/shard_map/ppermute | solution.py:26
  91.4 16.4 %copy-start.9 = (f32[576,256]{1,0:T(8,128)S(1)}, f32[576,256]{1,0:T(8,128)}, u32[]{:S(2)}) copy-start(f32[576,256]{1,0:T(8,128)} %copy-done.8) | copy-start | bytes 1769476
  91.4 16.4 %copy-start.11 = (f32[576,256]{1,0:T(8,128)S(1)}, f32[576,256]{1,0:T(8,128)}, u32[]{:S(2)}) copy-start(f32[576,256]{1,0:T(8,128)} %copy-done.10) | copy-start | bytes 1769476
  91.4 6.2 %collective-permute-start.10 = (f32[48,128]{1,0:T(8,128)S(1)}, f32[48,128]{1,0:T(8,128)S(1)}, u32[]{:S(2)}, u32[]{:S(2)}) collective-permute-start(f32[48,128]{1,0:T(8,128)S(1)} %convert_reduce_fusion), channel_id=1, source_target_pairs={{0,32},{32,0},{1,33},{33,1},{2,34},{34,2},{3,35},{35,3},{4,36},{36... | collective-permute-start | bytes 73736 | tf_op jit(solution)/shard_map/ppermute | solution.py:30
  98.7 30.9 %all-to-all-start.1 = ((bf16[64,48,128]{2,1,0:T(8,128)(2,1)}), bf16[64,48,128]{2,1,0:T(8,128)(2,1)S(1)}, u32[]{:S(2)}, u32[]{:S(2)}) async-start(bf16[64,48,128]{2,1,0:T(8,128)(2,1)} %broadcast_in_dim.2), calls=%async_computation.1 | async-start | bytes 1572864 | tf_op jit(solution)/shard_map/all_to_all | solution.py:270
  129.6 7.0 %collective-permute-start.15 = (bf16[3072,128]{1,0:T(8,128)(2,1)S(1)}, bf16[3072,128]{1,0:T(8,128)(2,1)S(1)}, u32[]{:S(2)}, u32[]{:S(2)}) collective-permute-start(bf16[3072,128]{1,0:T(8,128)(2,1)S(1)} %bitcast.8), channel_id=1, source_target_pairs={{0,2},{2,0},{1,3},{3,1},{4,6},{6,4},{5,7},{7,5},{8,10},{10,8},{9,1... | collective-permute-start | bytes 2359304 | tf_op jit(solution)/shard_map/ppermute | solution.py:30
  (15 other events, 50.7 us)

commit v6 on v5

--- a/solution.py
+++ b/solution.py
@@ -235,7 +235,7 @@
         first_kernel, 2, (log_scale, logit_bias, t0, tm, i_own, i_far),
         [(whole, f32), ((count, 2 * half), bf16), ((2, *square), bf16), (by_row, f32)], [], 500_000_000, "first_pairs",
     )
-    late_tm, i_f, next_features, own = lax.optimization_barrier((tm, i_f, next_features, own))
+    late_tm, next_features, own = lax.optimization_barrier((tm, next_features, own))
     p1 = swapped(late_tm, "core")
     p0 = lax.ppermute(t0, "core", [(0, 1)])
     gi_own, gi_back, w_own, w_next, b234, stats2 = local(

time: 139 us -> 148 us (1.065)
  waiting for transfers between devices: 33.9 us -> 50.6 us
  starting transfers between devices: 78.8 us -> 69.8 us
    ppermute x5, waiting for transfers between devices: 0.01 us -> 12.5 us  [shifted(): return lax.ppermute(array, AXES, pairs)]
    ppermute x5, starting transfers between devices: 32.7 us -> 22.4 us  [shifted(): return lax.ppermute(array, AXES, pairs)]
    ppermute x9, waiting for transfers between devices: 14.2 us -> 17.9 us  [swapped(): return lax.ppermute(array, axis, [(0, 1), (1, 0)])]
where the time goes in v6:
time: 148 us; the launch traced here: 147 us
  starting transfers between devices  69.8 us (47%)
  waiting for transfers between devices  50.6 us (34%)
  Pallas kernels  8.95 us (6%)
  local copies, waits for them, and re-layouts  7.88 us (5%)
  other arithmetic  5.27 us (4%)
  between operations  2.35 us (2%)
  matrix products  1.65 us (1%)
    ppermute x9, starting transfers between devices, swapped(): return lax.ppermute(array, axis, [(0, 1), (1, 0)])  28.4 us
    ppermute x5, starting transfers between devices, shifted(): return lax.ppermute(array, AXES, pairs)  22.4 us
    all_to_all x1, waiting for transfers between devices, shards(): lax.all_to_all(sent, PLANE, 0, 0, tiled=True).reshape(peers * deep, 128)  20.2 us
    ppermute x9, waiting for transfers between devices, swapped(): return lax.ppermute(array, axis, [(0, 1), (1, 0)])  17.9 us
    ppermute x5, waiting for transfers between devices, shifted(): return lax.ppermute(array, AXES, pairs)  12.5 us
    all_to_all x1, starting transfers between devices, shards(): lax.all_to_all(sent, PLANE, 0, 0, tiled=True).reshape(peers * deep, 128)  10.1 us
    pallas_call x6, Pallas kernels, local(): pl.pallas_call(kernel, out_shape=[jax.ShapeDtypeStruct(*out) for out in o...  8.95 us
    unnamed x43, local copies, waits for them, and re-layouts  6.82 us
  transfers between devices with their start and end apart: 18, of which 7 were waited for; matrix products, arithmetic and copies ran while one was open for 4% of the time, Pallas kernels for 3%

profile of v6, /device:TPU:1, one launch (start us, length us, event | category | flops | bytes accessed | tf_op | source)
XLA Modules:
  0.0 146.5 jit_solution(9059016828255776377)
XLA Ops:
  0.7 4.2 %collective-permute-start = (bf16[576,256]{1,0:T(8,128)(2,1)}, bf16[576,256]{1,0:T(8,128)(2,1)S(1)}, u32[]{:S(2)}, u32[]{:S(2)}) collective-permute-start(bf16[576,256]{1,0:T(8,128)(2,1)} %bitcast.12), channel_id=1, source_target_pairs={{0,4},{1,5},{2,6},{3,7},{4,8},{5,9},{6,10},{7,11},{8,12},{9,13},{1... | collective-permute-start | bytes 884744 | tf_op jit(solution)/shard_map/ppermute | solution.py:26
  6.5 3.1 %collective-permute-start.1 = (bf16[576,256]{1,0:T(8,128)(2,1)S(1)}, bf16[576,256]{1,0:T(8,128)(2,1)S(1)}, u32[]{:S(2)}, u32[]{:S(2)}) collective-permute-start(bf16[576,256]{1,0:T(8,128)(2,1)S(1)} %convolution_convert_fusion.i_own), channel_id=1, source_target_pairs={{0,1},{1,0},{2,3},{3,2},{4,5},{5,4},{6,7},{7,6},{8,9},{9,8},{10,11... | collective-permute-start | bytes 884744 | tf_op jit(solution)/shard_map/ppermute | solution.py:30
  9.6 2.2 %collective-permute-start.3 = (bf16[576,256]{1,0:T(8,128)(2,1)S(1)}, bf16[576,256]{1,0:T(8,128)(2,1)S(1)}, u32[]{:S(2)}, u32[]{:S(2)}) collective-permute-start(bf16[576,256]{1,0:T(8,128)(2,1)S(1)} %bitcast.13), channel_id=1, source_target_pairs={{0,1},{1,0},{2,3},{3,2},{4,5},{5,4},{6,7},{7,6},{8,9},{9,8},{10,11... | collective-permute-start | bytes 884744 | tf_op jit(solution)/shard_map/ppermute | solution.py:30
  11.8 12.5 %collective-permute-done = bf16[576,256]{1,0:T(8,128)(2,1)S(1)} collective-permute-done((bf16[576,256]{1,0:T(8,128)(2,1)}, bf16[576,256]{1,0:T(8,128)(2,1)S(1)}, u32[]{:S(2)}, u32[]{:S(2)}) %collective-permute-start) | collective-permute-done | bytes 294944 | tf_op jit(solution)/shard_map/ppermute | solution.py:26
  24.3 3.0 %collective-permute-start.5 = (bf16[256,1152]{1,0:T(8,128)(2,1)S(1)}, bf16[256,1152]{1,0:T(8,128)(2,1)S(1)}, u32[]{:S(2)}, u32[]{:S(2)}) collective-permute-start(bf16[256,1152]{1,0:T(8,128)(2,1)S(1)} %copy-done.1), channel_id=1, source_target_pairs={{0,509},{1,508},{2,511},{3,510},{4,0},{5,1},{6,2},{7,3},{8,4},{9,5... | collective-permute-start | bytes 1769480 | tf_op jit(solution)/shard_map/ppermute | solution.py:26
  27.4 3.0 %collective-permute-start.7 = (bf16[576,256]{1,0:T(8,128)(2,1)S(1)}, bf16[576,256]{1,0:T(8,128)(2,1)S(1)}, u32[]{:S(2)}, u32[]{:S(2)}) collective-permute-start(bf16[576,256]{1,0:T(8,128)(2,1)S(1)} %convolution_convert_fusion.i_own), channel_id=1, source_target_pairs={{0,509},{1,508},{2,511},{3,510},{4,0},{5,1},{6,2},{7,3},{8,4},{9,5... | collective-permute-start | bytes 884744 | tf_op jit(solution)/shard_map/ppermute | solution.py:26
  31.7 1.9 %collective-permute-start.2 = (bf16[576,256]{1,0:T(8,128)(2,1)S(1)}, bf16[576,256]{1,0:T(8,128)(2,1)S(1)}, u32[]{:S(2)}, u32[]{:S(2)}) collective-permute-start(bf16[576,256]{1,0:T(8,128)(2,1)S(1)} %collective-permute-done), channel_id=1, source_target_pairs={{0,1},{1,0},{2,3},{3,2},{4,5},{5,4},{6,7},{7,6},{8,9},{9,8},{10,11... | collective-permute-start | bytes 884744 | tf_op jit(solution)/shard_map/ppermute | solution.py:30
  35.0 5.0 %collective-permute-done.2 = bf16[576,256]{1,0:T(8,128)(2,1)S(1)} collective-permute-done((bf16[576,256]{1,0:T(8,128)(2,1)S(1)}, bf16[576,256]{1,0:T(8,128)(2,1)S(1)}, u32[]{:S(2)}, u32[]{:S(2)}) %collective-permute-start.2) | collective-permute-done | bytes 294944 | tf_op jit(solution)/shard_map/ppermute | solution.py:30
  41.5 4.9 %collective-permute-start.6 = (bf16[1152,256]{1,0:T(8,128)(2,1)S(1)}, bf16[1152,256]{1,0:T(8,128)(2,1)S(1)}, u32[]{:S(2)}, u32[]{:S(2)}) collective-permute-start(bf16[1152,256]{1,0:T(8,128)(2,1)S(1)} %constant_dynamic-update-slice_fusion.tm), channel_id=1, source_target_pairs={{0,2},{2,0},{1,3},{3,1},{4,6},{6,4},{5,7},{7,5},{8,10},{10,8},{9,1... | collective-permute-start | bytes 1769480 | tf_op jit(solution)/shard_map/ppermute | solution.py:30
  46.5 1.9 %collective-permute-start.8 = (bf16[576,256]{1,0:T(8,128)(2,1)S(1)}, bf16[576,256]{1,0:T(8,128)(2,1)S(1)}, u32[]{:S(2)}, u32[]{:S(2)}) collective-permute-start(bf16[576,256]{1,0:T(8,128)(2,1)S(1)} %collective-permute-done.7.i_e), channel_id=1, source_target_pairs={{0,1},{1,0},{2,3},{3,2},{4,5},{5,4},{6,7},{7,6},{8,9},{9,8},{10,11... | collective-permute-start | bytes 884744 | tf_op jit(solution)/shard_map/ppermute | solution.py:30
  48.4 6.7 %collective-permute-done.8.i_f = bf16[576,256]{1,0:T(8,128)(2,1)S(1)} collective-permute-done((bf16[576,256]{1,0:T(8,128)(2,1)S(1)}, bf16[576,256]{1,0:T(8,128)(2,1)S(1)}, u32[]{:S(2)}, u32[]{:S(2)}) %collective-permute-start.8) | collective-permute-done | bytes 294944 | tf_op jit(solution)/shard_map/ppermute | solution.py:30
  55.1 2.9 %second_pairs.1 = (f32[576,256]{1,0:T(8,128)S(1)}, bf16[576,256]{1,0:T(8,128)(2,1)}, bf16[576,256]{1,0:T(8,128)(2,1)S(1)}, bf16[576,256]{1,0:T(8,128)(2,1)S(1)},...) custom-call(f32[1]{0:T(128)S(6)} %copy.9.log_scale, f32[1]{0:T(128)S(6)} %copy.10.bias, ...), custom_call_target="tpu_custom_call" | custom-call | flops 800000000 | bytes 4000000 | tf_op jit(solution)/shard_map/second_pairs/pallas_call | solution.py:184
  59.7 4.7 %collective-permute-start.9 = (bf16[3072,128]{1,0:T(8,128)(2,1)S(1)}, bf16[3072,128]{1,0:T(8,128)(2,1)S(1)}, u32[]{:S(2)}, u32[]{:S(2)}) collective-permute-start(bf16[3072,128]{1,0:T(8,128)(2,1)S(1)} %weight_part.3), channel_id=1, source_target_pairs={{0,2},{2,0},{1,3},{3,1},{4,6},{6,4},{5,7},{7,5},{8,10},{10,8},{9,1... | collective-permute-start | bytes 2359304 | tf_op jit(solution)/shard_map/ppermute | solution.py:30
  67.4 5.5 %all-to-all-start = ((bf16[64,48,128]{2,1,0:T(8,128)(2,1)}), bf16[64,48,128]{2,1,0:T(8,128)(2,1)}, u32[]{:S(2)}, u32[]{:S(2)}) async-start(bf16[64,48,128]{2,1,0:T(8,128)(2,1)} %bitcast.10), calls=%async_computation | async-start | bytes 1572864 | tf_op jit(solution)/shard_map/all_to_all | solution.py:261
  80.3 2.2 %collective-permute-start.12 = (bf16[576,256]{1,0:T(8,128)(2,1)S(1)}, bf16[576,256]{1,0:T(8,128)(2,1)S(1)}, u32[]{:S(2)}, u32[]{:S(2)}) collective-permute-start(bf16[576,256]{1,0:T(8,128)(2,1)S(1)} %get-tuple-element.44), channel_id=1, source_target_pairs={{0,2},{2,0},{1,3},{3,1},{4,6},{6,4},{5,7},{7,5},{8,10},{10,8},{9,1... | collective-permute-start | bytes 884744 | tf_op jit(solution)/shard_map/ppermute | solution.py:30
  82.5 2.1 %collective-permute-start.14 = (bf16[576,256]{1,0:T(8,128)(2,1)}, bf16[576,256]{1,0:T(8,128)(2,1)S(1)}, u32[]{:S(2)}, u32[]{:S(2)}) collective-permute-start(bf16[576,256]{1,0:T(8,128)(2,1)} %get-tuple-element.45), channel_id=1, source_target_pairs={{2,0},{3,1},{6,4},{7,5},{10,8},{11,9},{14,12},{15,13},{18,16},{19,... | collective-permute-start | bytes 884744 | tf_op jit(solution)/shard_map/ppermute | solution.py:264
  84.7 2.9 %collective-permute-start.11 = (bf16[576,256]{1,0:T(8,128)(2,1)}, bf16[576,256]{1,0:T(8,128)(2,1)S(1)}, u32[]{:S(2)}, u32[]{:S(2)}) collective-permute-start(bf16[576,256]{1,0:T(8,128)(2,1)} %get-tuple-element.39), channel_id=1, source_target_pairs={{0,4},{1,5},{2,6},{3,7},{4,8},{5,9},{6,10},{7,11},{8,12},{9,13},{1... | collective-permute-start | bytes 884744 | tf_op jit(solution)/shard_map/ppermute | solution.py:26
  88.4 9.3 %collective-permute-start.13 = (bf16[576,256]{1,0:T(8,128)(2,1)}, bf16[576,256]{1,0:T(8,128)(2,1)}, u32[]{:S(2)}, u32[]{:S(2)}) collective-permute-start(bf16[576,256]{1,0:T(8,128)(2,1)} %add_convert_fusion.3), channel_id=1, source_target_pairs={{0,509},{1,508},{2,511},{3,510},{4,0},{5,1},{6,2},{7,3},{8,4},{9,5... | collective-permute-start | bytes 884744 | tf_op jit(solution)/shard_map/ppermute | solution.py:26
  99.0 3.1 %collective-permute-start.10 = (f32[48,128]{1,0:T(8,128)S(1)}, f32[48,128]{1,0:T(8,128)S(1)}, u32[]{:S(2)}, u32[]{:S(2)}) collective-permute-start(f32[48,128]{1,0:T(8,128)S(1)} %convert_reduce_fusion), channel_id=1, source_target_pairs={{0,32},{32,0},{1,33},{33,1},{2,34},{34,2},{3,35},{35,3},{4,36},{36... | collective-permute-start | bytes 73736 | tf_op jit(solution)/shard_map/ppermute | solution.py:30
  102.1 3.4 %collective-permute-done.10 = f32[48,128]{1,0:T(8,128)S(1)} collective-permute-done((f32[48,128]{1,0:T(8,128)S(1)}, f32[48,128]{1,0:T(8,128)S(1)}, u32[]{:S(2)}, u32[]{:S(2)}) %collective-permute-start.10) | collective-permute-done | bytes 24608 | tf_op jit(solution)/shard_map/ppermute | solution.py:30
  106.6 10.1 %all-to-all-start.1 = ((bf16[64,48,128]{2,1,0:T(8,128)(2,1)}), bf16[64,48,128]{2,1,0:T(8,128)(2,1)S(1)}, u32[]{:S(2)}, u32[]{:S(2)}) async-start(bf16[64,48,128]{2,1,0:T(8,128)(2,1)} %broadcast_in_dim.2), calls=%async_computation.1 | async-start | bytes 1572864 | tf_op jit(solution)/shard_map/all_to_all | solution.py:270
  116.7 2.1 %add_convert_fusion.1 = (bf16[576,256]{1,0:T(8,128)(2,1)}, bf16[576,256]{1,0:T(8,128)(2,1)}) fusion(bf16[576,256]{1,0:T(8,128)(2,1)} %copy-done.19, f32[576,256]{1,0:T(8,128)S(1)} %copy-done.11, bf16[576,256]{1,0:T(8,128)(2,1)} %collective-permute-done.13, f32[576,256]{1,0:T(8,128)S(1)} %copy-done.9, bf16[576,256]{1,0:T(8,128)(2,1)} %copy-done.20), kind=kLoop, calls=%fused_computation.4 | loop fusion | flops 1179648 | bytes 2654208 | tf_op jit(solution)/shard_map/convert_element_type | solution.py:272
  118.9 20.2 %all-to-all-done.1 = bf16[64,48,128]{2,1,0:T(8,128)(2,1)S(1)} async-done(((bf16[64,48,128]{2,1,0:T(8,128)(2,1)}), bf16[64,48,128]{2,1,0:T(8,128)(2,1)S(1)}, u32[]{:S(2)}, u32[]{:S(2)}) %all-to-all-start.1) | async-done | bytes 786464 | tf_op jit(solution)/shard_map/all_to_all | solution.py:270
  139.0 4.3 %collective-permute-start.15 = (bf16[3072,128]{1,0:T(8,128)(2,1)S(1)}, bf16[3072,128]{1,0:T(8,128)(2,1)S(1)}, u32[]{:S(2)}, u32[]{:S(2)}) collective-permute-start(bf16[3072,128]{1,0:T(8,128)(2,1)S(1)} %bitcast.8), channel_id=1, source_target_pairs={{0,2},{2,0},{1,3},{3,1},{4,6},{6,4},{5,7},{7,5},{8,10},{10,8},{9,1... | collective-permute-start | bytes 2359304 | tf_op jit(solution)/shard_map/ppermute | solution.py:30
  (70 shorter events, 22.9 us)
Async XLA Ops:
  0.7 23.7 %copy-start.1 = (bf16[256,1152]{1,0:T(8,128)(2,1)S(1)}, bf16[256,1152]{1,0:T(8,128)(2,1)}, u32[]{:S(2)}) copy-start(bf16[256,1152]{1,0:T(8,128)(2,1)} %features.3) | copy-start | bytes 1769476
  0.7 23.7 %collective-permute-start = (bf16[576,256]{1,0:T(8,128)(2,1)}, bf16[576,256]{1,0:T(8,128)(2,1)S(1)}, u32[]{:S(2)}, u32[]{:S(2)}) collective-permute-start(bf16[576,256]{1,0:T(8,128)(2,1)} %bitcast.12), channel_id=1, source_target_pairs={{0,4},{1,5},{2,6},{3,7},{4,8},{5,9},{6,10},{7,11},{8,12},{9,13},{1... | collective-permute-start | bytes 884744 | tf_op jit(solution)/shard_map/ppermute | solution.py:26
  6.5 25.2 %collective-permute-start.1 = (bf16[576,256]{1,0:T(8,128)(2,1)S(1)}, bf16[576,256]{1,0:T(8,128)(2,1)S(1)}, u32[]{:S(2)}, u32[]{:S(2)}) collective-permute-start(bf16[576,256]{1,0:T(8,128)(2,1)S(1)} %convolution_convert_fusion.i_own), channel_id=1, source_target_pairs={{0,1},{1,0},{2,3},{3,2},{4,5},{5,4},{6,7},{7,6},{8,9},{9,8},{10,11... | collective-permute-start | bytes 884744 | tf_op jit(solution)/shard_map/ppermute | solution.py:30
  9.6 24.0 %collective-permute-start.3 = (bf16[576,256]{1,0:T(8,128)(2,1)S(1)}, bf16[576,256]{1,0:T(8,128)(2,1)S(1)}, u32[]{:S(2)}, u32[]{:S(2)}) collective-permute-start(bf16[576,256]{1,0:T(8,128)(2,1)S(1)} %bitcast.13), channel_id=1, source_target_pairs={{0,1},{1,0},{2,3},{3,2},{4,5},{5,4},{6,7},{7,6},{8,9},{9,8},{10,11... | collective-permute-start | bytes 884744 | tf_op jit(solution)/shard_map/ppermute | solution.py:30
  24.3 17.1 %collective-permute-start.5 = (bf16[256,1152]{1,0:T(8,128)(2,1)S(1)}, bf16[256,1152]{1,0:T(8,128)(2,1)S(1)}, u32[]{:S(2)}, u32[]{:S(2)}) collective-permute-start(bf16[256,1152]{1,0:T(8,128)(2,1)S(1)} %copy-done.1), channel_id=1, source_target_pairs={{0,509},{1,508},{2,511},{3,510},{4,0},{5,1},{6,2},{7,3},{8,4},{9,5... | collective-permute-start | bytes 1769480 | tf_op jit(solution)/shard_map/ppermute | solution.py:26
  27.4 19.1 %collective-permute-start.7 = (bf16[576,256]{1,0:T(8,128)(2,1)S(1)}, bf16[576,256]{1,0:T(8,128)(2,1)S(1)}, u32[]{:S(2)}, u32[]{:S(2)}) collective-permute-start(bf16[576,256]{1,0:T(8,128)(2,1)S(1)} %convolution_convert_fusion.i_own), channel_id=1, source_target_pairs={{0,509},{1,508},{2,511},{3,510},{4,0},{5,1},{6,2},{7,3},{8,4},{9,5... | collective-permute-start | bytes 884744 | tf_op jit(solution)/shard_map/ppermute | solution.py:26
  31.7 9.8 %copy-start.14 = (bf16[576,256]{1,0:T(8,128)(2,1)}, bf16[576,256]{1,0:T(8,128)(2,1)S(1)}, u32[]{:S(2)}) copy-start(bf16[576,256]{1,0:T(8,128)(2,1)S(1)} %collective-permute-done.1.i_far) | copy-start | bytes 884740
  31.7 8.3 %collective-permute-start.2 = (bf16[576,256]{1,0:T(8,128)(2,1)S(1)}, bf16[576,256]{1,0:T(8,128)(2,1)S(1)}, u32[]{:S(2)}, u32[]{:S(2)}) collective-permute-start(bf16[576,256]{1,0:T(8,128)(2,1)S(1)} %collective-permute-done), channel_id=1, source_target_pairs={{0,1},{1,0},{2,3},{3,2},{4,5},{5,4},{6,7},{7,6},{8,9},{9,8},{10,11... | collective-permute-start | bytes 884744 | tf_op jit(solution)/shard_map/ppermute | solution.py:30
  33.7 21.4 %collective-permute-start.4 = (bf16[1152,256]{1,0:T(8,128)(2,1)S(1)}, bf16[1152,256]{1,0:T(8,128)(2,1)S(1)}, u32[]{:S(2)}, u32[]{:S(2)}) collective-permute-start(bf16[1152,256]{1,0:T(8,128)(2,1)S(1)} %pad_maximum_fusion.t0), channel_id=1, source_target_pairs={{0,2},{1,3},{4,6},{5,7},{8,10},{9,11},{12,14},{13,15},{16,18},{17,... | collective-permute-start | bytes 1769480 | tf_op jit(solution)/shard_map/ppermute | solution.py:240
  41.5 16.5 %copy-start.16 = (bf16[2,256,256]{2,1,0:T(8,128)(2,1)}, bf16[2,256,256]{2,1,0:T(8,128)(2,1)S(1)}, u32[]{:S(2)}) copy-start(bf16[2,256,256]{2,1,0:T(8,128)(2,1)S(1)} %get-tuple-element.40.b01) | copy-start | bytes 786436
  41.5 13.6 %collective-permute-start.6 = (bf16[1152,256]{1,0:T(8,128)(2,1)S(1)}, bf16[1152,256]{1,0:T(8,128)(2,1)S(1)}, u32[]{:S(2)}, u32[]{:S(2)}) collective-permute-start(bf16[1152,256]{1,0:T(8,128)(2,1)S(1)} %constant_dynamic-update-slice_fusion.tm), channel_id=1, source_target_pairs={{0,2},{2,0},{1,3},{3,1},{4,6},{6,4},{5,7},{7,5},{8,10},{10,8},{9,1... | collective-permute-start | bytes 1769480 | tf_op jit(solution)/shard_map/ppermute | solution.py:30
  46.4 11.5 %copy-start.4 = (bf16[576,256]{1,0:T(8,128)(2,1)}, bf16[576,256]{1,0:T(8,128)(2,1)S(1)}, u32[]{:S(2)}) copy-start(bf16[576,256]{1,0:T(8,128)(2,1)S(1)} %collective-permute-done.7.i_e) | copy-start | bytes 884740
  46.5 8.6 %collective-permute-start.8 = (bf16[576,256]{1,0:T(8,128)(2,1)S(1)}, bf16[576,256]{1,0:T(8,128)(2,1)S(1)}, u32[]{:S(2)}, u32[]{:S(2)}) collective-permute-start(bf16[576,256]{1,0:T(8,128)(2,1)S(1)} %collective-permute-done.7.i_e), channel_id=1, source_target_pairs={{0,1},{1,0},{2,3},{3,2},{4,5},{5,4},{6,7},{7,6},{8,9},{9,8},{10,11... | collective-permute-start | bytes 884744 | tf_op jit(solution)/shard_map/ppermute | solution.py:30
  59.7 6.6 %collective-permute-start.9 = (bf16[3072,128]{1,0:T(8,128)(2,1)S(1)}, bf16[3072,128]{1,0:T(8,128)(2,1)S(1)}, u32[]{:S(2)}, u32[]{:S(2)}) collective-permute-start(bf16[3072,128]{1,0:T(8,128)(2,1)S(1)} %weight_part.3), channel_id=1, source_target_pairs={{0,2},{2,0},{1,3},{3,1},{4,6},{6,4},{5,7},{7,5},{8,10},{10,8},{9,1... | collective-permute-start | bytes 2359304 | tf_op jit(solution)/shard_map/ppermute | solution.py:30
  67.4 30.3 %all-to-all-start = ((bf16[64,48,128]{2,1,0:T(8,128)(2,1)}), bf16[64,48,128]{2,1,0:T(8,128)(2,1)}, u32[]{:S(2)}, u32[]{:S(2)}) async-start(bf16[64,48,128]{2,1,0:T(8,128)(2,1)} %bitcast.10), calls=%async_computation | async-start | bytes 1572864 | tf_op jit(solution)/shard_map/all_to_all | solution.py:261
  80.3 7.3 %collective-permute-start.12 = (bf16[576,256]{1,0:T(8,128)(2,1)S(1)}, bf16[576,256]{1,0:T(8,128)(2,1)S(1)}, u32[]{:S(2)}, u32[]{:S(2)}) collective-permute-start(bf16[576,256]{1,0:T(8,128)(2,1)S(1)} %get-tuple-element.44), channel_id=1, source_target_pairs={{0,2},{2,0},{1,3},{3,1},{4,6},{6,4},{5,7},{7,5},{8,10},{10,8},{9,1... | collective-permute-start | bytes 884744 | tf_op jit(solution)/shard_map/ppermute | solution.py:30
  82.5 23.0 %collective-permute-start.14 = (bf16[576,256]{1,0:T(8,128)(2,1)}, bf16[576,256]{1,0:T(8,128)(2,1)S(1)}, u32[]{:S(2)}, u32[]{:S(2)}) collective-permute-start(bf16[576,256]{1,0:T(8,128)(2,1)} %get-tuple-element.45), channel_id=1, source_target_pairs={{2,0},{3,1},{6,4},{7,5},{10,8},{11,9},{14,12},{15,13},{18,16},{19,... | collective-permute-start | bytes 884744 | tf_op jit(solution)/shard_map/ppermute | solution.py:264
  84.7 20.8 %collective-permute-start.11 = (bf16[576,256]{1,0:T(8,128)(2,1)}, bf16[576,256]{1,0:T(8,128)(2,1)S(1)}, u32[]{:S(2)}, u32[]{:S(2)}) collective-permute-start(bf16[576,256]{1,0:T(8,128)(2,1)} %get-tuple-element.39), channel_id=1, source_target_pairs={{0,4},{1,5},{2,6},{3,7},{4,8},{5,9},{6,10},{7,11},{8,12},{9,13},{1... | collective-permute-start | bytes 884744 | tf_op jit(solution)/shard_map/ppermute | solution.py:26
  88.4 17.1 %collective-permute-start.13 = (bf16[576,256]{1,0:T(8,128)(2,1)}, bf16[576,256]{1,0:T(8,128)(2,1)}, u32[]{:S(2)}, u32[]{:S(2)}) collective-permute-start(bf16[576,256]{1,0:T(8,128)(2,1)} %add_convert_fusion.3), channel_id=1, source_target_pairs={{0,509},{1,508},{2,511},{3,510},{4,0},{5,1},{6,2},{7,3},{8,4},{9,5... | collective-permute-start | bytes 884744 | tf_op jit(solution)/shard_map/ppermute | solution.py:26
  99.0 17.7 %copy-start.9 = (f32[576,256]{1,0:T(8,128)S(1)}, f32[576,256]{1,0:T(8,128)}, u32[]{:S(2)}) copy-start(f32[576,256]{1,0:T(8,128)} %copy-done.8) | copy-start | bytes 1769476
  99.0 17.8 %copy-start.11 = (f32[576,256]{1,0:T(8,128)S(1)}, f32[576,256]{1,0:T(8,128)}, u32[]{:S(2)}) copy-start(f32[576,256]{1,0:T(8,128)} %copy-done.10) | copy-start | bytes 1769476
  99.0 6.5 %collective-permute-start.10 = (f32[48,128]{1,0:T(8,128)S(1)}, f32[48,128]{1,0:T(8,128)S(1)}, u32[]{:S(2)}, u32[]{:S(2)}) collective-permute-start(f32[48,128]{1,0:T(8,128)S(1)} %convert_reduce_fusion), channel_id=1, source_target_pairs={{0,32},{32,0},{1,33},{33,1},{2,34},{34,2},{3,35},{35,3},{4,36},{36... | collective-permute-start | bytes 73736 | tf_op jit(solution)/shard_map/ppermute | solution.py:30
  106.6 32.5 %all-to-all-start.1 = ((bf16[64,48,128]{2,1,0:T(8,128)(2,1)}), bf16[64,48,128]{2,1,0:T(8,128)(2,1)S(1)}, u32[]{:S(2)}, u32[]{:S(2)}) async-start(bf16[64,48,128]{2,1,0:T(8,128)(2,1)} %broadcast_in_dim.2), calls=%async_computation.1 | async-start | bytes 1572864 | tf_op jit(solution)/shard_map/all_to_all | solution.py:270
  139.0 6.2 %collective-permute-start.15 = (bf16[3072,128]{1,0:T(8,128)(2,1)S(1)}, bf16[3072,128]{1,0:T(8,128)(2,1)S(1)}, u32[]{:S(2)}, u32[]{:S(2)}) collective-permute-start(bf16[3072,128]{1,0:T(8,128)(2,1)S(1)} %bitcast.8), channel_id=1, source_target_pairs={{0,2},{2,0},{1,3},{3,1},{4,6},{6,4},{5,7},{7,5},{8,10},{10,8},{9,1... | collective-permute-start | bytes 2359304 | tf_op jit(solution)/shard_map/ppermute | solution.py:30
  (15 other events, 42.5 us)
